TPU v7x, 256 devices: a whole 4x4x8 slice. The times are simulated.
256 devices in a mesh: row: 32 (over z, y), col: 8 (over x, core).
Axes of the slice: x: 4, y: 4, z: 8, core: 2. Of those that a mesh axis runs over, the one named last changes fastest.
Arguments:
- factor: bfloat16 [28672, 28672], P('row', 'col'), as said below
- basis: bfloat16 [28672, 512], P('row'), may hold values from -6 to 6
Outputs:
- eigen_basis: float32 [28672, 512], P(('row', 'col'))
- middle_basis: bfloat16 [28672, 512], P('col')
Inputs may be any that keep to these rules, and one draw needn't show every extreme that they name: factor is exactly symmetric.
All inputs are finite; a program needn't handle non-finite values.
Results may differ from a plain program's by a relative error of at most 0.0029.
Values may be sent and summed in bfloat16 or wider, within the bound.
No kernel may reach another device: no remote copies, remote signals or barrier semaphores. Data moves between devices by JAX's collectives and lax.ppermute only.
A program may use at most 128 MiB of HBM per device.

v0:
```python
import math

import jax
import jax.numpy as jnp
from jax import lax
from jax.experimental import pallas as pl
from jax.experimental.pallas import tpu as pltpu
from jax.sharding import PartitionSpec as P

M = 28672
K = 512
B = 128
R = 8
AXES = ("z", "y", "x", "core")
SIZES = (8, 4, 4, 2)
HALF = K // 2
FEW = 128
ROWS = M // 256


def dot(a, b, ca, cb):
    return lax.dot_general(a, b, (((ca,), (cb,)), ((), ())), precision=lax.Precision.HIGHEST,
                           preferred_element_type=jnp.float32)


def reciprocal_rows(top, at, lane, sub):
    wide = [jnp.broadcast_to(top[:, at + j:at + j + 1], (R, B)) for j in range(R)]
    e = {(i, j): jnp.broadcast_to(wide[j][i:i + 1, :], (R, B)) for i in range(R) for j in range(i + 1)}
    inside = (lane >= at) & (lane < at + R)
    rhs = jnp.where(inside, jnp.where(lane - at == sub, 1.0, 0.0), top)
    row = [jnp.broadcast_to(rhs[i:i + 1, :], (R, B)) for i in range(R)]
    ratio, solved, final = {}, [None] * R, [None] * R
    for k in range(0, R, 2):
        a, b, c = e[k, k], e[k + 1, k], e[k + 1, k + 1]
        det = a * c - b * b
        over = 1.0 / det
        for i in range(k + 2, R):
            ratio[i, k] = (e[i, k] * c - e[i, k + 1] * b) * over
            ratio[i, k + 1] = (e[i, k + 1] * a - e[i, k] * b) * over
        for i in range(k + 2, R):
            for j in range(k + 2, i + 1):
                e[i, j] = e[i, j] - (ratio[i, k] * e[j, k] + ratio[i, k + 1] * e[j, k + 1])
            row[i] = row[i] - (ratio[i, k] * row[k] + ratio[i, k + 1] * row[k + 1])
        solved[k] = (c * row[k] - b * row[k + 1]) * over
        solved[k + 1] = (a * row[k + 1] - b * row[k]) * over
        root = lax.rsqrt(a)
        final[k] = row[k] * root
        final[k + 1] = (row[k + 1] - (b * root) * final[k]) * (lax.rsqrt(det) * (a * root))
    back = [None] * R
    for k in reversed(range(R)):
        z = solved[k]
        for i in reversed(range(k + 2 - k % 2, R)):
            z = z - ratio[i, k] * back[i]
        back[k] = z
    out = final[0]
    for k in range(1, R):
        out = jnp.where(sub == k, final[k], out)
    return jnp.where(lane < at + R, out, 0.0), back, inside


def leaf(block):
    n = B // R
    w = [block[R * i:R * i + R, :] for i in range(n)]
    lane = lax.broadcasted_iota(jnp.int32, (R, B), 1)
    sub = lax.broadcasted_iota(jnp.int32, (R, B), 0)
    done = []
    for p in range(n):
        at = R * p
        rows, back, inside = reciprocal_rows(w[p], at, lane, sub)
        done.append(rows)
        for i in range(p + 1, n):
            new = jnp.where(inside, 0.0, w[i])
            for j in reversed(range(R)):
                new = new - jnp.broadcast_to(w[i][:, at + j:at + j + 1], (R, B)) * back[j]
            w[i] = new
    return jnp.concatenate(done, axis=0)


def unit(n):
    return lax.broadcasted_iota(jnp.int32, (n, n), 0) == lax.broadcasted_iota(jnp.int32, (n, n), 1)


def chol_inverse(gram_ref, out_ref, work):
    gram = gram_ref[...]
    diagonal = jnp.where(unit(K), gram, 0.0)
    along = lax.rsqrt(jnp.sum(diagonal, axis=0, keepdims=True))
    work[...] = gram * along * lax.rsqrt(jnp.sum(diagonal, axis=1, keepdims=True))

    def block(b, _):
        at = pl.multiple_of(b * B, B)
        low = leaf(work[pl.ds(at, B), pl.ds(at, B)])
        work[pl.ds(at, B), pl.ds(at, B)] = jnp.where(unit(B), 1.0, 0.0)
        top = dot(low, work[pl.ds(at, B), :], 1, 0)
        lane = lax.broadcasted_iota(jnp.int32, (B, K), 1)
        out_ref[pl.ds(at, B), :] = jnp.where(lane < at + B, top, 0.0) * along
        for i in range(1, K // B):
            @pl.when(i > b)
            def _():
                to = B * i
                work[to:to + B, pl.ds(at, B)] = jnp.zeros((B, B), jnp.float32)
                work[to:to + B, :] = work[to:to + B, :] - dot(top[:, to:to + B], top, 0, 0)
        return 0

    lax.fori_loop(0, K // B, block, 0)


def inverse_factor(gram):
    return pl.pallas_call(
        chol_inverse,
        out_shape=jax.ShapeDtypeStruct((K, K), jnp.float32),
        in_specs=[pl.BlockSpec(memory_space=pltpu.VMEM)],
        out_specs=pl.BlockSpec(memory_space=pltpu.VMEM),
        scratch_shapes=[pltpu.VMEM((K, K), jnp.float32)],
        compiler_params=pltpu.CompilerParams(vmem_limit_bytes=32 * 1024 * 1024),
        cost_estimate=pl.CostEstimate(flops=2 * K ** 3, bytes_accessed=8 * K * K, transcendentals=0),
    )(gram)


def permute(values, where):
    places = [(z, y, x, c) for z in range(8) for y in range(4) for x in range(4) for c in range(2)]
    index = {place: i for i, place in enumerate(places)}
    return lax.ppermute(values, AXES, [(index[p], index[where(*p)]) for p in places])


def other_core(z, y, x, c):
    return z, y, x, 1 - c


def exchange(pieces, axes):
    return lax.all_to_all(pieces, axes, 0, 0, tiled=True)


def copies(values, axes):
    return jnp.broadcast_to(values[None], (lax.axis_size(axes),) + values.shape)


def up(z, y, x, c):
    return z, (y + 1) % 4, x, c


def down(z, y, x, c):
    return z, (y - 1) % 4, x, c


def gather_y(own):
    half = own.shape[0] // 2
    before, after = permute(own, up), permute(own, down)
    far = jnp.concatenate([permute(before[:half], up), permute(after[half:], down)], axis=0)
    return [own, after, far, before]


def gather_y_small(own):
    far = permute(own, lambda z, y, x, c: (z, (y + 2) % 4, x, c))
    rows = own.shape[0]
    out = jnp.zeros((4 * rows, own.shape[1]), own.dtype)
    for step, piece in enumerate([own, permute(own, down), far, permute(own, up)]):
        out = lax.dynamic_update_slice_in_dim(out, piece, lax.rem(lax.axis_index("y") + step, 4) * rows, 0)
    return out


def column_block(z, y, x, c):
    return 2 * x + c, y, z // 2, z % 2


def spread(many, few):
    many, few = lax.optimization_barrier((many, few))
    return lax.all_gather(many, "z", axis=0, tiled=True), few


def basis_rows(basis):
    sent = lax.dynamic_slice(basis, (lax.axis_index("core") * 4 * ROWS, FEW), (4 * ROWS, K - FEW))
    many = permute(sent, lambda z, y, x, c: (2 * y + c, x, z // 2, z % 2))
    few = permute(basis[:, :FEW], column_block)
    many, few = spread(many, few)
    return many, gather_y(few)


def middle_rows(rows):
    def chunk_place(z, y, x, c):
        chunk = 8 * y + 2 * x + c
        return chunk // 4, chunk % 4, z // 2, z % 2
    many = permute(rows[:, FEW:], chunk_place)
    few = permute(rows[:, :FEW], column_block)
    many, few = spread(gather_y_small(many), few)
    return many, gather_y(exchange(copies(few, "z"), "z").reshape(8 * ROWS, FEW))


def few_step(place, a_ref, *refs):
    pieces, out_ref = refs[:4], refs[4]
    a = a_ref[...].reshape(4 * ROWS, 8 * ROWS)
    for j in range(4):
        @pl.when(pl.program_id(1) == j)
        def _():
            term = jnp.dot(a, pieces[j][...], preferred_element_type=jnp.float32).reshape(4, ROWS, FEW)
            if j == 0:
                out_ref[...] = term
            else:
                out_ref[...] += term


def product_few(factor, pieces):
    core = lax.axis_index("core")
    place = jnp.stack([lax.axis_index("y"), core]).astype(jnp.int32)
    return pl.pallas_call(
        few_step,
        out_shape=jax.ShapeDtypeStruct((2, 4, ROWS, FEW), jnp.float32),
        grid_spec=pltpu.PrefetchScalarGridSpec(
            num_scalar_prefetch=1,
            grid=(2, 4),
            in_specs=[
                pl.BlockSpec((4, None, ROWS, 8 * ROWS),
                             lambda h, q, place: (0, lax.rem(place[1] + 1 + h, 2), 0, lax.rem(place[0] + q, 4))),
            ] + [pl.BlockSpec((8 * ROWS, FEW), lambda h, q, place: (0, 0))] * 4,
            out_specs=pl.BlockSpec((None, 4, ROWS, FEW), lambda h, q, place: (h, 0, 0, 0)),
        ),
        compiler_params=pltpu.CompilerParams(vmem_limit_bytes=40 * 1024 * 1024),
        cost_estimate=pl.CostEstimate(flops=2 * 8 * ROWS * M // 8 * FEW, bytes_accessed=8 * 1024 * 1024, transcendentals=0),
    )(place, factor.reshape(4, 2, ROWS, 32 * ROWS), *pieces)


def many_step(place, a_ref, b_ref, *refs):
    step = pl.program_id(0)
    a = a_ref[...].reshape(4 * ROWS, 8 * ROWS)
    out_ref = refs[-1]
    if len(refs) > 1:
        pieces, out_ref, rows_ref = refs[:4], refs[4], refs[5]
        rows_ref[:, FEW:] = b_ref[...]
        for j in range(4):
            @pl.when(lax.rem(place[1] + j, 4) == step)
            def _():
                rows_ref[:, :FEW] = pieces[j][...]
    term = jnp.dot(a, b_ref[...], preferred_element_type=jnp.float32).reshape(out_ref.shape)

    @pl.when(step == 0)
    def _():
        out_ref[...] = term

    @pl.when(step > 0)
    def _():
        out_ref[...] += term


def product_many(factor, many, core, pieces=()):
    place = jnp.stack([core, lax.axis_index("y")]).astype(jnp.int32)
    out_shape = [jax.ShapeDtypeStruct((4, ROWS, K - FEW), jnp.float32)]
    out_specs = [pl.BlockSpec((4, ROWS, K - FEW), lambda q, place: (0, 0, 0))]
    if pieces:
        out_shape.append(jax.ShapeDtypeStruct((32 * ROWS, K), jnp.bfloat16))
        out_specs.append(pl.BlockSpec((8 * ROWS, K), lambda q, place: (q, 0)))
    return pl.pallas_call(
        many_step,
        out_shape=out_shape,
        grid_spec=pltpu.PrefetchScalarGridSpec(
            num_scalar_prefetch=1,
            grid=(4,),
            in_specs=[
                pl.BlockSpec((4, None, ROWS, 8 * ROWS), lambda q, place: (0, place[0], 0, q)),
                pl.BlockSpec((8 * ROWS, K - FEW), lambda q, place: (q, 0)),
            ] + [pl.BlockSpec((8 * ROWS, FEW), lambda q, place: (0, 0))] * len(pieces),
            out_specs=out_specs,
        ),
        compiler_params=pltpu.CompilerParams(vmem_limit_bytes=40 * 1024 * 1024),
        cost_estimate=pl.CostEstimate(flops=2 * 4 * ROWS * M // 8 * (K - FEW), bytes_accessed=8 * 1024 * 1024, transcendentals=0),
    )(place, factor.reshape(4, 2, ROWS, 32 * ROWS), many, *pieces)


def summed_product(factor, many, pieces, keep):
    core = lax.axis_index("core")
    both = product_few(factor, pieces)
    few = jnp.sum(exchange(both[1] + permute(both[0], other_core), "x"), axis=0)
    many, few = lax.optimization_barrier((many, few))
    came = permute(product_many(factor, many, 1 - core)[0], other_core)
    mine = product_many(factor, many, core, pieces if keep else [])
    total = jnp.sum(exchange(mine[0] + came, "x"), axis=0)
    return jnp.concatenate([few, total], axis=1), mine[-1]


def gram_inverse(values):
    gram = dot(values, values, 0, 0)
    core = lax.axis_index("core")
    half = lambda which: lax.dynamic_slice_in_dim(gram, which * HALF, HALF, 0)
    share = half(core) + permute(half(1 - core), other_core)
    share = jnp.sum(exchange(share.reshape(16, HALF // 16, K), ("y", "x")), axis=0)
    share = jnp.sum(exchange(copies(share, "z"), "z"), axis=0)
    share = exchange(copies(share, ("y", "x")), ("y", "x")).reshape(HALF, K)
    came = permute(share, other_core)
    first = jnp.where(core == 0, share, came)
    second = jnp.where(core == 0, came, share)
    return inverse_factor(jnp.concatenate([first, second], axis=0))


def shards(factor, basis):
    scale = math.sqrt(M)
    first, _ = summed_product(factor, *basis_rows(basis), False)
    middle = (dot(first, gram_inverse(first), 1, 1) * scale).astype(jnp.bfloat16)
    second, column_basis = summed_product(factor, *middle_rows(middle), True)
    return dot(second, gram_inverse(second), 1, 1) * scale, column_basis


def solution(mesh):
    fine = jax.sharding.Mesh(mesh.devices.reshape(SIZES), AXES)
    return jax.shard_map(
        shards,
        mesh=fine,
        in_specs=(P(("z", "y"), ("x", "core")), P(("z", "y"), None)),
        out_specs=(P(AXES, None), P(("x", "core"), None)),
        check_vma=False,
    )
```

profile of v0, /device:TPU:1, one launch (start us, length us, event | category | flops | bytes accessed | tf_op | source)
XLA Modules:
  0.0 389.0 jit_solution(18233723381170097030)
XLA Ops:
  8.2 4.9 %collective-permute-start = (bf16[448,384]{1,0:T(8,128)(2,1)S(1)}, bf16[448,384]{1,0:T(8,128)(2,1)S(1)}, u32[]{:S(2)}, u32[]{:S(2)}) collective-permute-start(bf16[448,384]{1,0:T(8,128)(2,1)S(1)} %constant_dynamic-slice_fusion.2), channel_id=1, source_target_pairs={{0,0},{1,32},{2,8},{3,40},{4,16},{5,48},{6,24},{7,56},{8,64},{9,96... | collective-permute-start | bytes 1032200 | tf_op jit(solution)/shard_map/ppermute | solution.py:122
  14.1 1.9 collective-permute-start.1
  16.1 6.5 %collective-permute-done.1.refs_0_ = bf16[896,128]{1,0:T(8,128)(2,1)S(1)} collective-permute-done((bf16[896,128]{1,0:T(8,128)(2,1)S(1)}, bf16[896,128]{1,0:T(8,128)(2,1)S(1)}, u32[]{:S(2)}, u32[]{:S(2)}) %collective-permute-start.1) | collective-permute-done | bytes 229408 | tf_op jit(solution)/shard_map/ppermute | solution.py:122
  23.4 16.6 %collective-permute-start.3 = (bf16[896,128]{1,0:T(8,128)(2,1)S(1)}, bf16[896,128]{1,0:T(8,128)(2,1)S(1)}, u32[]{:S(2)}, u32[]{:S(2)}) collective-permute-start(bf16[896,128]{1,0:T(8,128)(2,1)S(1)} %collective-permute-done.1.refs_0_), channel_id=1, source_target_pairs={{0,8},{1,9},{2,10},{3,11},{4,12},{5,13},{6,14},{7,15},{8,16},{9,17... | collective-permute-start | bytes 688136 | tf_op jit(solution)/shard_map/ppermute | solution.py:122
  39.9 4.5 %collective-permute-start.2 = (bf16[896,128]{1,0:T(8,128)(2,1)S(1)}, bf16[896,128]{1,0:T(8,128)(2,1)S(1)}, u32[]{:S(2)}, u32[]{:S(2)}) collective-permute-start(bf16[896,128]{1,0:T(8,128)(2,1)S(1)} %collective-permute-done.1.refs_0_), channel_id=1, source_target_pairs={{0,24},{1,25},{2,26},{3,27},{4,28},{5,29},{6,30},{7,31},{8,0},{9,1... | collective-permute-start | bytes 688136 | tf_op jit(solution)/shard_map/ppermute | solution.py:122
  44.4 3.9 collective-permute-done.3.refs_3_
  48.4 3.0 collective-permute-start.5
  51.5 2.1 collective-permute-done.4
  53.9 2.8 copy-done
  56.7 5.0 %shard_map.41 = f32[2,4,112,128]{3,2,1,0:T(8,128)S(1)} custom-call(s32[2]{0:T(128)S(1)} %pad_add_fusion.place, bf16[4,2,112,3584]{3,2,1,0:T(8,128)(2,1)S(1)} %bitcast.27, bf16[896,128]{1,0:T(8,128)(2,1)S(1)} %collective-permute-done.1.refs_0_, bf16[896,128]{1,0:T(8,128)(2,1)S(1)} %collective-permute-done.2.refs_1_, ...), custom_call_target="tpu_custom_call" | custom-call | flops 822083584 | bytes 8388608 | tf_op jit(solution)/shard_map/pallas_call | solution.py:204
  64.0 21.0 %all-to-all-start = ((f32[4,112,128]{2,1,0:T(8,128)}), f32[4,112,128]{2,1,0:T(8,128)S(1)}, u32[]{:S(2)}, u32[]{:S(2)}) async-start(f32[4,112,128]{2,1,0:T(8,128)} %fusion.2), calls=%async_computation | async-start | bytes 458752 | tf_op jit(solution)/shard_map/all_to_all | solution.py:130
  85.1 5.4 %all-to-all-done = f32[4,112,128]{2,1,0:T(8,128)S(1)} async-done(((f32[4,112,128]{2,1,0:T(8,128)}), f32[4,112,128]{2,1,0:T(8,128)S(1)}, u32[]{:S(2)}, u32[]{:S(2)}) %all-to-all-start) | async-done | bytes 229408 | tf_op jit(solution)/shard_map/all_to_all | solution.py:130
  90.5 10.9 %all-gather.3.cloned.1.call-done.b_ref = bf16[3584,384]{1,0:T(8,128)(2,1)} async-done(((bf16[448,384]{1,0:T(8,128)(2,1)}), bf16[3584,384]{1,0:T(8,128)(2,1)}) %all-gather.3.cloned.1.call-update) | async-done | bytes 2752528 | tf_op jit(solution)/shard_map/all_gather | solution.py:167
  101.4 2.8 copy-done.1
  106.0 3.6 shard_map.43
  109.6 3.2 collective-permute-start.7
  112.9 3.5 shard_map.42
  117.4 4.0 %all-to-all-start.1 = ((f32[4,112,384]{2,1,0:T(8,128)}), f32[4,112,384]{2,1,0:T(8,128)S(1)}, u32[]{:S(2)}, u32[]{:S(2)}) async-start(f32[4,112,384]{2,1,0:T(8,128)} %add.52), calls=%async_computation.1 | async-start | bytes 1376256 | tf_op jit(solution)/shard_map/all_to_all | solution.py:130
  121.3 11.1 %all-to-all-done.1 = f32[4,112,384]{2,1,0:T(8,128)S(1)} async-done(((f32[4,112,384]{2,1,0:T(8,128)}), f32[4,112,384]{2,1,0:T(8,128)S(1)}, u32[]{:S(2)}, u32[]{:S(2)}) %all-to-all-start.1) | async-done | bytes 688160 | tf_op jit(solution)/shard_map/all_to_all | solution.py:130
  136.4 15.2 %all_to_all.55 = f32[16,16,512]{2,1,0:T(8,128)S(1)} all-to-all(f32[16,16,512]{2,1,0:T(8,128)S(1)} %bitcast.40), channel_id=1, replica_groups=mesh['z'=8,'y'=4,'x'=4,'core'=2] {'y','x'}, dimensions={0} | all-to-all | bytes 1048576 | tf_op jit(solution)/shard_map/all_to_all | solution.py:130
  151.7 12.9 %all_to_all.56 = f32[8,16,512]{2,1,0:T(8,128)S(1)} all-to-all(f32[8,16,512]{2,1,0:T(8,128)S(1)} %broadcast_in_dim.13), channel_id=1, replica_groups=mesh['z'=8,'y'=4,'x'=4,'core'=2] {'z'}, dimensions={0} | all-to-all | bytes 524288 | tf_op jit(solution)/shard_map/all_to_all | solution.py:130
  164.6 13.2 %all_to_all.57 = f32[16,16,512]{2,1,0:T(8,128)S(1)} all-to-all(f32[16,16,512]{2,1,0:T(8,128)S(1)} %broadcast_in_dim.14), channel_id=1, replica_groups=mesh['z'=8,'y'=4,'x'=4,'core'=2] {'y','x'}, dimensions={0} | all-to-all | bytes 1048576 | tf_op jit(solution)/shard_map/all_to_all | solution.py:130
  177.9 4.1 %collective-permute-start.9 = (f32[256,512]{1,0:T(8,128)S(1)}, f32[256,512]{1,0:T(8,128)S(1)}, u32[]{:S(2)}, u32[]{:S(2)}) collective-permute-start(f32[256,512]{1,0:T(8,128)S(1)} %bitcast.37), channel_id=1, source_target_pairs={{0,1},{1,0},{2,3},{3,2},{4,5},{5,4},{6,7},{7,6},{8,9},{9,8},{10,11... | collective-permute-start | bytes 1572872 | tf_op jit(solution)/shard_map/ppermute | solution.py:122
  183.7 20.3 %shard_map.44 = f32[512,512]{1,0:T(8,128)S(1)} custom-call(f32[512,512]{1,0:T(8,128)S(1)} %pad_maximum_fusion.gram_ref), custom_call_target="tpu_custom_call" | custom-call | flops 268435456 | bytes 2097152 | tf_op jit(solution)/shard_map/pallas_call | solution.py:108
  205.2 1.9 collective-permute-start.10
  207.2 3.6 collective-permute-start.14
  210.8 3.8 collective-permute-done.10
  214.6 3.7 collective-permute-start.11
  221.3 2.0 collective-permute-done.12
  225.3 15.1 %all_to_all.58 = bf16[8,112,128]{2,1,0:T(8,128)(2,1)S(1)} all-to-all(bf16[8,112,128]{2,1,0:T(8,128)(2,1)S(1)} %broadcast_in_dim.15), channel_id=1, replica_groups=mesh['z'=8,'y'=4,'x'=4,'core'=2] {'z'}, dimensions={0} | all-to-all | bytes 458752 | tf_op jit(solution)/shard_map/all_to_all | solution.py:130
  240.5 2.7 collective-permute-start.15
  243.1 3.7 collective-permute-done.16.refs_3_
  247.0 3.0 collective-permute-start.18
  249.9 2.9 collective-permute-done.17
  252.9 2.9 copy-done.3
  255.8 5.0 %shard_map.45 = f32[2,4,112,128]{3,2,1,0:T(8,128)S(1)} custom-call(s32[2]{0:T(128)S(1)} %pad_add_fusion.place, bf16[4,2,112,3584]{3,2,1,0:T(8,128)(2,1)S(1)} %bitcast.30, bf16[896,128]{1,0:T(8,128)(2,1)S(1)} %bitcast.35, bf16[896,128]{1,0:T(8,128)(2,1)S(1)} %collective-permute-done.15.refs_1_, ...), custom_call_target="tpu_custom_call" | custom-call | flops 822083584 | bytes 8388608 | tf_op jit(solution)/shard_map/pallas_call | solution.py:204
  260.8 5.8 %collective-permute-start.19 = (f32[4,112,128]{2,1,0:T(8,128)S(1)}, f32[4,112,128]{2,1,0:T(8,128)S(1)}, u32[]{:S(2)}, u32[]{:S(2)}) collective-permute-start(f32[4,112,128]{2,1,0:T(8,128)S(1)} %slice_bitcast_fusion), channel_id=1, source_target_pairs={{0,1},{1,0},{2,3},{3,2},{4,5},{5,4},{6,7},{7,6},{8,9},{9,8},{10,11... | collective-permute-start | bytes 688136 | tf_op jit(solution)/shard_map/ppermute | solution.py:122
  267.7 10.0 %all_to_all.59 = f32[4,112,128]{2,1,0:T(8,128)S(1)} all-to-all(f32[4,112,128]{2,1,0:T(8,128)S(1)} %fusion.1), channel_id=1, replica_groups=mesh['z'=8,'y'=4,'x'=4,'core'=2] {'x'}, dimensions={0} | all-to-all | bytes 458752 | tf_op jit(solution)/shard_map/all_to_all | solution.py:130
  277.8 2.8 copy-done.4
  282.4 3.6 shard_map.47
  287.9 2.8 copy-done.5
  290.7 5.2 %shard_map.46 = (f32[4,112,384]{2,1,0:T(8,128)S(1)}, bf16[3584,512]{1,0:T(8,128)(2,1)}) custom-call(s32[2]{0:T(128)S(1)} %pad_add_fusion.1.place, bf16[4,2,112,3584]{3,2,1,0:T(8,128)(2,1)S(1)} %bitcast.32, bf16[3584,384]{1,0:T(8,128)(2,1)S(1)} %copy-done.6, bf16[896,128]{1,0:T(8,128)(2,1)S(1)} %bitcast.36, ...), custom_call_target="tpu_custom_call" | custom-call | flops 1233125376 | bytes 8388608 | tf_op jit(solution)/shard_map/pallas_call | solution.py:250
  296.0 13.8 %all_to_all.60 = f32[4,112,384]{2,1,0:T(8,128)S(1)} all-to-all(f32[4,112,384]{2,1,0:T(8,128)S(1)} %add.64), channel_id=1, replica_groups=mesh['z'=8,'y'=4,'x'=4,'core'=2] {'x'}, dimensions={0} | all-to-all | bytes 1376256 | tf_op jit(solution)/shard_map/all_to_all | solution.py:130
  313.4 15.7 %all_to_all.61 = f32[16,16,512]{2,1,0:T(8,128)S(1)} all-to-all(f32[16,16,512]{2,1,0:T(8,128)S(1)} %bitcast.39), channel_id=1, replica_groups=mesh['z'=8,'y'=4,'x'=4,'core'=2] {'y','x'}, dimensions={0} | all-to-all | bytes 1048576 | tf_op jit(solution)/shard_map/all_to_all | solution.py:130
  329.2 11.6 %all_to_all.62 = f32[8,16,512]{2,1,0:T(8,128)S(1)} all-to-all(f32[8,16,512]{2,1,0:T(8,128)S(1)} %broadcast_in_dim.16), channel_id=1, replica_groups=mesh['z'=8,'y'=4,'x'=4,'core'=2] {'z'}, dimensions={0} | all-to-all | bytes 524288 | tf_op jit(solution)/shard_map/all_to_all | solution.py:130
  340.9 13.2 %all_to_all.63 = f32[16,16,512]{2,1,0:T(8,128)S(1)} all-to-all(f32[16,16,512]{2,1,0:T(8,128)S(1)} %broadcast_in_dim.17), channel_id=1, replica_groups=mesh['z'=8,'y'=4,'x'=4,'core'=2] {'y','x'}, dimensions={0} | all-to-all | bytes 1048576 | tf_op jit(solution)/shard_map/all_to_all | solution.py:130
  354.1 4.2 %collective-permute-start.22 = (f32[256,512]{1,0:T(8,128)S(1)}, f32[256,512]{1,0:T(8,128)S(1)}, u32[]{:S(2)}, u32[]{:S(2)}) collective-permute-start(f32[256,512]{1,0:T(8,128)S(1)} %bitcast.38), channel_id=1, source_target_pairs={{0,1},{1,0},{2,3},{3,2},{4,5},{5,4},{6,7},{7,6},{8,9},{9,8},{10,11... | collective-permute-start | bytes 1572872 | tf_op jit(solution)/shard_map/ppermute | solution.py:122
  360.0 20.3 %shard_map.48 = f32[512,512]{1,0:T(8,128)S(1)} custom-call(f32[512,512]{1,0:T(8,128)S(1)} %pad_maximum_fusion.1.gram_ref), custom_call_target="tpu_custom_call" | custom-call | flops 268435456 | bytes 2097152 | tf_op jit(solution)/shard_map/pallas_call | solution.py:108
  (95 shorter events, 32.6 us)
Async XLA Ops:
  7.2 94.3 %all-gather.3.cloned.1.call-start = ((), (), s32[]{:S(2)}) async-start(), calls=%async_computation.11 | async-start | bytes 3096576 | tf_op jit(solution)/shard_map/all_gather | solution.py:167
  8.2 14.4 %collective-permute-start = (bf16[448,384]{1,0:T(8,128)(2,1)S(1)}, bf16[448,384]{1,0:T(8,128)(2,1)S(1)}, u32[]{:S(2)}, u32[]{:S(2)}) collective-permute-start(bf16[448,384]{1,0:T(8,128)(2,1)S(1)} %constant_dynamic-slice_fusion.2), channel_id=1, source_target_pairs={{0,0},{1,32},{2,8},{3,40},{4,16},{5,48},{6,24},{7,56},{8,64},{9,96... | collective-permute-start | bytes 1032200 | tf_op jit(solution)/shard_map/ppermute | solution.py:122
  14.1 8.5 %collective-permute-start.1 = (bf16[896,128]{1,0:T(8,128)(2,1)S(1)}, bf16[896,128]{1,0:T(8,128)(2,1)S(1)}, u32[]{:S(2)}, u32[]{:S(2)}) collective-permute-start(bf16[896,128]{1,0:T(8,128)(2,1)S(1)} %slice.33), channel_id=1, source_target_pairs={{0,0},{1,32},{2,64},{3,96},{4,128},{5,160},{6,192},{7,224},{8,8},{... | collective-permute-start | bytes 688136 | tf_op jit(solution)/shard_map/ppermute | solution.py:122
  22.6 0.7 copy-start.9
  23.4 24.9 %collective-permute-start.3 = (bf16[896,128]{1,0:T(8,128)(2,1)S(1)}, bf16[896,128]{1,0:T(8,128)(2,1)S(1)}, u32[]{:S(2)}, u32[]{:S(2)}) collective-permute-start(bf16[896,128]{1,0:T(8,128)(2,1)S(1)} %collective-permute-done.1.refs_0_), channel_id=1, source_target_pairs={{0,8},{1,9},{2,10},{3,11},{4,12},{5,13},{6,14},{7,15},{8,16},{9,17... | collective-permute-start | bytes 688136 | tf_op jit(solution)/shard_map/ppermute | solution.py:122
  39.9 8.5 %collective-permute-start.2 = (bf16[896,128]{1,0:T(8,128)(2,1)S(1)}, bf16[896,128]{1,0:T(8,128)(2,1)S(1)}, u32[]{:S(2)}, u32[]{:S(2)}) collective-permute-start(bf16[896,128]{1,0:T(8,128)(2,1)S(1)} %collective-permute-done.1.refs_0_), channel_id=1, source_target_pairs={{0,24},{1,25},{2,26},{3,27},{4,28},{5,29},{6,30},{7,31},{8,0},{9,1... | collective-permute-start | bytes 688136 | tf_op jit(solution)/shard_map/ppermute | solution.py:122
  48.3 5.3 %collective-permute-start.4 = (bf16[448,128]{1,0:T(8,128)(2,1)S(1)}, bf16[448,128]{1,0:T(8,128)(2,1)S(1)}, u32[]{:S(2)}, u32[]{:S(2)}) collective-permute-start(bf16[448,128]{1,0:T(8,128)(2,1)S(1)} %slice.44), channel_id=1, source_target_pairs={{0,8},{1,9},{2,10},{3,11},{4,12},{5,13},{6,14},{7,15},{8,16},{9,17... | collective-permute-start | bytes 344072 | tf_op jit(solution)/shard_map/ppermute | solution.py:122
  48.4 5.4 %collective-permute-start.5 = (bf16[448,128]{1,0:T(8,128)(2,1)S(1)}, bf16[448,128]{1,0:T(8,128)(2,1)S(1)}, u32[]{:S(2)}, u32[]{:S(2)}) collective-permute-start(bf16[448,128]{1,0:T(8,128)(2,1)S(1)} %slice.45), channel_id=1, source_target_pairs={{0,24},{1,25},{2,26},{3,27},{4,28},{5,29},{6,30},{7,31},{8,0},{9,1... | collective-permute-start | bytes 344072 | tf_op jit(solution)/shard_map/ppermute | solution.py:122
  53.9 2.8 copy-start
  61.7 1.6 collective-permute-start.6
  64.0 26.5 %all-to-all-start = ((f32[4,112,128]{2,1,0:T(8,128)}), f32[4,112,128]{2,1,0:T(8,128)S(1)}, u32[]{:S(2)}, u32[]{:S(2)}) async-start(f32[4,112,128]{2,1,0:T(8,128)} %fusion.2), calls=%async_computation | async-start | bytes 458752 | tf_op jit(solution)/shard_map/all_to_all | solution.py:130
  101.4 2.8 copy-start.1
  104.3 1.8 copy-start.7
  106.0 6.8 %copy-start.2 = (bf16[896,3584]{1,0:T(8,128)(2,1)S(1)}, bf16[896,3584]{1,0:T(8,128)(2,1)}, u32[]{:S(2)}) copy-start(bf16[896,3584]{1,0:T(8,128)(2,1)} %param.2) | copy-start | bytes 19267588
  109.6 6.8 %collective-permute-start.7 = (f32[4,112,384]{2,1,0:T(8,128)S(1)}, f32[4,112,384]{2,1,0:T(8,128)S(1)}, u32[]{:S(2)}, u32[]{:S(2)}) collective-permute-start(f32[4,112,384]{2,1,0:T(8,128)S(1)} %shard_map.43), channel_id=1, source_target_pairs={{0,1},{1,0},{2,3},{3,2},{4,5},{5,4},{6,7},{7,6},{8,9},{9,8},{10,11... | collective-permute-start | bytes 2064392 | tf_op jit(solution)/shard_map/ppermute | solution.py:122
  117.4 15.0 %all-to-all-start.1 = ((f32[4,112,384]{2,1,0:T(8,128)}), f32[4,112,384]{2,1,0:T(8,128)S(1)}, u32[]{:S(2)}, u32[]{:S(2)}) async-start(f32[4,112,384]{2,1,0:T(8,128)} %add.52), calls=%async_computation.1 | async-start | bytes 1376256 | tf_op jit(solution)/shard_map/all_to_all | solution.py:130
  121.3 156.5 %all-gather.5.cloned.1.call-start = ((), (), s32[]{:S(2)}) async-start(), calls=%async_computation.12 | async-start | bytes 3096576 | tf_op jit(solution)/shard_map/all_gather | solution.py:167
  133.5 2.7 collective-permute-start.8
  177.9 5.6 %collective-permute-start.9 = (f32[256,512]{1,0:T(8,128)S(1)}, f32[256,512]{1,0:T(8,128)S(1)}, u32[]{:S(2)}, u32[]{:S(2)}) collective-permute-start(f32[256,512]{1,0:T(8,128)S(1)} %bitcast.37), channel_id=1, source_target_pairs={{0,1},{1,0},{2,3},{3,2},{4,5},{5,4},{6,7},{7,6},{8,9},{9,8},{10,11... | collective-permute-start | bytes 1572872 | tf_op jit(solution)/shard_map/ppermute | solution.py:122
  205.2 9.4 %collective-permute-start.10 = (bf16[112,384]{1,0:T(8,128)(2,1)S(1)}, bf16[112,384]{1,0:T(8,128)(2,1)S(1)}, u32[]{:S(2)}, u32[]{:S(2)}) collective-permute-start(bf16[112,384]{1,0:T(8,128)(2,1)S(1)} %slice.48), channel_id=1, source_target_pairs={{0,0},{1,8},{2,16},{3,24},{4,32},{5,40},{6,48},{7,56},{8,64},{9,72... | collective-permute-start | bytes 258056 | tf_op jit(solution)/shard_map/ppermute | solution.py:122
  207.2 17.4 %collective-permute-start.14 = (bf16[112,128]{1,0:T(8,128)(2,1)S(1)}, bf16[112,128]{1,0:T(8,128)(2,1)S(1)}, u32[]{:S(2)}, u32[]{:S(2)}) collective-permute-start(bf16[112,128]{1,0:T(8,128)(2,1)S(1)} %slice.49), channel_id=1, source_target_pairs={{0,0},{1,32},{2,64},{3,96},{4,128},{5,160},{6,192},{7,224},{8,8},{... | collective-permute-start | bytes 86024 | tf_op jit(solution)/shard_map/ppermute | solution.py:122
  214.6 6.6 %collective-permute-start.11 = (bf16[112,384]{1,0:T(8,128)(2,1)S(1)}, bf16[112,384]{1,0:T(8,128)(2,1)S(1)}, u32[]{:S(2)}, u32[]{:S(2)}) collective-permute-start(bf16[112,384]{1,0:T(8,128)(2,1)S(1)} %collective-permute-done.10), channel_id=1, source_target_pairs={{0,24},{1,25},{2,26},{3,27},{4,28},{5,29},{6,30},{7,31},{8,0},{9,1... | collective-permute-start | bytes 258056 | tf_op jit(solution)/shard_map/ppermute | solution.py:122
  218.3 5.0 %collective-permute-start.12 = (bf16[112,384]{1,0:T(8,128)(2,1)S(1)}, bf16[112,384]{1,0:T(8,128)(2,1)S(1)}, u32[]{:S(2)}, u32[]{:S(2)}) collective-permute-start(bf16[112,384]{1,0:T(8,128)(2,1)S(1)} %collective-permute-done.10), channel_id=1, source_target_pairs={{0,16},{1,17},{2,18},{3,19},{4,20},{5,21},{6,22},{7,23},{8,24},{9,... | collective-permute-start | bytes 258056 | tf_op jit(solution)/shard_map/ppermute | solution.py:122
  219.0 5.5 %collective-permute-start.13 = (bf16[112,384]{1,0:T(8,128)(2,1)S(1)}, bf16[112,384]{1,0:T(8,128)(2,1)S(1)}, u32[]{:S(2)}, u32[]{:S(2)}) collective-permute-start(bf16[112,384]{1,0:T(8,128)(2,1)S(1)} %collective-permute-done.10), channel_id=1, source_target_pairs={{0,8},{1,9},{2,10},{3,11},{4,12},{5,13},{6,14},{7,15},{8,16},{9,17... | collective-permute-start | bytes 258056 | tf_op jit(solution)/shard_map/ppermute | solution.py:122
  224.5 0.7 copy-start.8
  240.5 6.4 %collective-permute-start.16 = (bf16[896,128]{1,0:T(8,128)(2,1)S(1)}, bf16[896,128]{1,0:T(8,128)(2,1)S(1)}, u32[]{:S(2)}, u32[]{:S(2)}) collective-permute-start(bf16[896,128]{1,0:T(8,128)(2,1)S(1)} %bitcast.33), channel_id=1, source_target_pairs={{0,8},{1,9},{2,10},{3,11},{4,12},{5,13},{6,14},{7,15},{8,16},{9,17... | collective-permute-start | bytes 688136 | tf_op jit(solution)/shard_map/ppermute | solution.py:122
  240.5 6.5 %collective-permute-start.15 = (bf16[896,128]{1,0:T(8,128)(2,1)S(1)}, bf16[896,128]{1,0:T(8,128)(2,1)S(1)}, u32[]{:S(2)}, u32[]{:S(2)}) collective-permute-start(bf16[896,128]{1,0:T(8,128)(2,1)S(1)} %bitcast.34), channel_id=1, source_target_pairs={{0,24},{1,25},{2,26},{3,27},{4,28},{5,29},{6,30},{7,31},{8,0},{9,1... | collective-permute-start | bytes 688136 | tf_op jit(solution)/shard_map/ppermute | solution.py:122
  246.8 6.0 %collective-permute-start.17 = (bf16[448,128]{1,0:T(8,128)(2,1)S(1)}, bf16[448,128]{1,0:T(8,128)(2,1)S(1)}, u32[]{:S(2)}, u32[]{:S(2)}) collective-permute-start(bf16[448,128]{1,0:T(8,128)(2,1)S(1)} %slice.50), channel_id=1, source_target_pairs={{0,8},{1,9},{2,10},{3,11},{4,12},{5,13},{6,14},{7,15},{8,16},{9,17... | collective-permute-start | bytes 344072 | tf_op jit(solution)/shard_map/ppermute | solution.py:122
  247.0 5.9 %collective-permute-start.18 = (bf16[448,128]{1,0:T(8,128)(2,1)S(1)}, bf16[448,128]{1,0:T(8,128)(2,1)S(1)}, u32[]{:S(2)}, u32[]{:S(2)}) collective-permute-start(bf16[448,128]{1,0:T(8,128)(2,1)S(1)} %slice.51), channel_id=1, source_target_pairs={{0,24},{1,25},{2,26},{3,27},{4,28},{5,29},{6,30},{7,31},{8,0},{9,1... | collective-permute-start | bytes 344072 | tf_op jit(solution)/shard_map/ppermute | solution.py:122
  252.9 2.9 copy-start.3
  260.8 6.9 %collective-permute-start.19 = (f32[4,112,128]{2,1,0:T(8,128)S(1)}, f32[4,112,128]{2,1,0:T(8,128)S(1)}, u32[]{:S(2)}, u32[]{:S(2)}) collective-permute-start(f32[4,112,128]{2,1,0:T(8,128)S(1)} %slice_bitcast_fusion), channel_id=1, source_target_pairs={{0,1},{1,0},{2,3},{3,2},{4,5},{5,4},{6,7},{7,6},{8,9},{9,8},{10,11... | collective-permute-start | bytes 688136 | tf_op jit(solution)/shard_map/ppermute | solution.py:122
  277.8 2.8 copy-start.4
  280.6 1.8 copy-start.6
  286.0 9.9 %collective-permute-start.20 = (f32[4,112,384]{2,1,0:T(8,128)S(1)}, f32[4,112,384]{2,1,0:T(8,128)S(1)}, u32[]{:S(2)}, u32[]{:S(2)}) collective-permute-start(f32[4,112,384]{2,1,0:T(8,128)S(1)} %shard_map.47), channel_id=1, source_target_pairs={{0,1},{1,0},{2,3},{3,2},{4,5},{5,4},{6,7},{7,6},{8,9},{9,8},{10,11... | collective-permute-start | bytes 2064392 | tf_op jit(solution)/shard_map/ppermute | solution.py:122
  287.9 2.8 copy-start.5
  310.9 2.4 collective-permute-start.21
  354.1 5.7 %collective-permute-start.22 = (f32[256,512]{1,0:T(8,128)S(1)}, f32[256,512]{1,0:T(8,128)S(1)}, u32[]{:S(2)}, u32[]{:S(2)}) collective-permute-start(f32[256,512]{1,0:T(8,128)S(1)} %bitcast.38), channel_id=1, source_target_pairs={{0,1},{1,0},{2,3},{3,2},{4,5},{5,4},{6,7},{7,6},{8,9},{9,8},{10,11... | collective-permute-start | bytes 1572872 | tf_op jit(solution)/shard_map/ppermute | solution.py:122
Sparse Core Ops, SparseCore 0:
  23.5 77.9 all-gather.2
  225.4 41.2 all-gather.4
where the time goes:
time: 390 us; the launch traced here: 389 us
  blocking collectives  121 us (31%)
  starting transfers between devices  93.8 us (24%)
  Pallas kernels  66.5 us (17%)
  waiting for transfers between devices  63.9 us (16%)
  local copies, waits for them, and re-layouts  21.6 us (6%)
  between operations  14.5 us (4%)
  matrix products  5.09 us (1%)
    all_to_all x9, blocking collectives, exchange(): return lax.all_to_all(pieces, axes, 0, 0, tiled=True)  121 us
    ppermute x23, starting transfers between devices, permute(): lax.ppermute(values, AXES, [(index[p], index[where(*p)]) for p in places])  68.8 us
    pallas_call x2, Pallas kernels, inverse_factor(): pl.pallas_call(chol_inverse, out_shape=jax.ShapeDtypeStruct((K, K), jnp.f...  40.6 us
    ppermute x23, waiting for transfers between devices, permute(): lax.ppermute(values, AXES, [(index[p], index[where(*p)]) for p in places])  36.4 us
    all_to_all x2, starting transfers between devices, exchange(): return lax.all_to_all(pieces, axes, 0, 0, tiled=True)  24.9 us
    unnamed x21, local copies, waits for them, and re-layouts  19.2 us
    all_to_all x2, waiting for transfers between devices, exchange(): return lax.all_to_all(pieces, axes, 0, 0, tiled=True)  16.5 us
    pallas_call x4, Pallas kernels, product_many(): pl.pallas_call(many_step, out_shape=out_shape, grid_spec=pltpu.PrefetchSc...  15.9 us
  transfers between devices with their start and end apart: 27, of which 19 were waited for; matrix products, arithmetic and copies ran while one was open for 1% of the time, Pallas kernels for 5%

commit v1 on v0

--- a/solution.py
+++ b/solution.py
@@ -14,7 +14,8 @@
 AXES = ("z", "y", "x", "core")
 SIZES = (8, 4, 4, 2)
 HALF = K // 2
-FEW = 128
+FEW_FIRST = 256
+FEW_SECOND = 128
 ROWS = M // 256
 
 
@@ -111,7 +112,7 @@
         in_specs=[pl.BlockSpec(memory_space=pltpu.VMEM)],
         out_specs=pl.BlockSpec(memory_space=pltpu.VMEM),
         scratch_shapes=[pltpu.VMEM((K, K), jnp.float32)],
-        compiler_params=pltpu.CompilerParams(vmem_limit_bytes=32 * 1024 * 1024),
+        compiler_params=pltpu.CompilerParams(vmem_limit_bytes=12 * 1024 * 1024),
         cost_estimate=pl.CostEstimate(flops=2 * K ** 3, bytes_accessed=8 * K * K, transcendentals=0),
     )(gram)
 
@@ -167,22 +168,22 @@
     return lax.all_gather(many, "z", axis=0, tiled=True), few
 
 
-def basis_rows(basis):
-    sent = lax.dynamic_slice(basis, (lax.axis_index("core") * 4 * ROWS, FEW), (4 * ROWS, K - FEW))
+def basis_rows(basis, width):
+    sent = lax.dynamic_slice(basis, (lax.axis_index("core") * 4 * ROWS, width), (4 * ROWS, K - width))
     many = permute(sent, lambda z, y, x, c: (2 * y + c, x, z // 2, z % 2))
-    few = permute(basis[:, :FEW], column_block)
+    few = permute(basis[:, :width], column_block)
     many, few = spread(many, few)
     return many, gather_y(few)
 
 
-def middle_rows(rows):
+def middle_rows(rows, width):
     def chunk_place(z, y, x, c):
         chunk = 8 * y + 2 * x + c
         return chunk // 4, chunk % 4, z // 2, z % 2
-    many = permute(rows[:, FEW:], chunk_place)
-    few = permute(rows[:, :FEW], column_block)
+    many = permute(rows[:, width:], chunk_place)
+    few = permute(rows[:, :width], column_block)
     many, few = spread(gather_y_small(many), few)
-    return many, gather_y(exchange(copies(few, "z"), "z").reshape(8 * ROWS, FEW))
+    return many, gather_y(exchange(copies(few, "z"), "z").reshape(8 * ROWS, width))
 
 
 def few_step(place, a_ref, *refs):
@@ -191,7 +192,7 @@
     for j in range(4):
         @pl.when(pl.program_id(1) == j)
         def _():
-            term = jnp.dot(a, pieces[j][...], preferred_element_type=jnp.float32).reshape(4, ROWS, FEW)
+            term = jnp.dot(a, pieces[j][...], preferred_element_type=jnp.float32).reshape(out_ref.shape)
             if j == 0:
                 out_ref[...] = term
             else:
@@ -200,21 +201,22 @@
 
 def product_few(factor, pieces):
     core = lax.axis_index("core")
+    width = pieces[0].shape[1]
     place = jnp.stack([lax.axis_index("y"), core]).astype(jnp.int32)
     return pl.pallas_call(
         few_step,
-        out_shape=jax.ShapeDtypeStruct((2, 4, ROWS, FEW), jnp.float32),
+        out_shape=jax.ShapeDtypeStruct((2, 4, ROWS, width), jnp.float32),
         grid_spec=pltpu.PrefetchScalarGridSpec(
             num_scalar_prefetch=1,
             grid=(2, 4),
             in_specs=[
                 pl.BlockSpec((4, None, ROWS, 8 * ROWS),
                              lambda h, q, place: (0, lax.rem(place[1] + 1 + h, 2), 0, lax.rem(place[0] + q, 4))),
-            ] + [pl.BlockSpec((8 * ROWS, FEW), lambda h, q, place: (0, 0))] * 4,
-            out_specs=pl.BlockSpec((None, 4, ROWS, FEW), lambda h, q, place: (h, 0, 0, 0)),
+            ] + [pl.BlockSpec((8 * ROWS, width), lambda h, q, place: (0, 0))] * 4,
+            out_specs=pl.BlockSpec((None, 4, ROWS, width), lambda h, q, place: (h, 0, 0, 0)),
         ),
-        compiler_params=pltpu.CompilerParams(vmem_limit_bytes=40 * 1024 * 1024),
-        cost_estimate=pl.CostEstimate(flops=2 * 8 * ROWS * M // 8 * FEW, bytes_accessed=8 * 1024 * 1024, transcendentals=0),
+        compiler_params=pltpu.CompilerParams(vmem_limit_bytes=16 * 1024 * 1024),
+        cost_estimate=pl.CostEstimate(flops=2 * 8 * ROWS * M // 8 * width, bytes_accessed=8 * 1024 * 1024, transcendentals=0),
     )(place, factor.reshape(4, 2, ROWS, 32 * ROWS), *pieces)
 
 
@@ -224,11 +226,12 @@
     out_ref = refs[-1]
     if len(refs) > 1:
         pieces, out_ref, rows_ref = refs[:4], refs[4], refs[5]
-        rows_ref[:, FEW:] = b_ref[...]
+        few = pieces[0].shape[1]
+        rows_ref[:, few:] = b_ref[...]
         for j in range(4):
             @pl.when(lax.rem(place[1] + j, 4) == step)
             def _():
-                rows_ref[:, :FEW] = pieces[j][...]
+                rows_ref[:, :few] = pieces[j][...]
     term = jnp.dot(a, b_ref[...], preferred_element_type=jnp.float32).reshape(out_ref.shape)
 
     @pl.when(step == 0)
@@ -241,9 +244,10 @@
 
 
 def product_many(factor, many, core, pieces=()):
+    width = many.shape[1]
     place = jnp.stack([core, lax.axis_index("y")]).astype(jnp.int32)
-    out_shape = [jax.ShapeDtypeStruct((4, ROWS, K - FEW), jnp.float32)]
-    out_specs = [pl.BlockSpec((4, ROWS, K - FEW), lambda q, place: (0, 0, 0))]
+    out_shape = [jax.ShapeDtypeStruct((4, ROWS, width), jnp.float32)]
+    out_specs = [pl.BlockSpec((4, ROWS, width), lambda q, place: (0, 0, 0))]
     if pieces:
         out_shape.append(jax.ShapeDtypeStruct((32 * ROWS, K), jnp.bfloat16))
         out_specs.append(pl.BlockSpec((8 * ROWS, K), lambda q, place: (q, 0)))
@@ -255,24 +259,24 @@
             grid=(4,),
             in_specs=[
                 pl.BlockSpec((4, None, ROWS, 8 * ROWS), lambda q, place: (0, place[0], 0, q)),
-                pl.BlockSpec((8 * ROWS, K - FEW), lambda q, place: (q, 0)),
-            ] + [pl.BlockSpec((8 * ROWS, FEW), lambda q, place: (0, 0))] * len(pieces),
+                pl.BlockSpec((8 * ROWS, width), lambda q, place: (q, 0)),
+            ] + [pl.BlockSpec((8 * ROWS, K - width), lambda q, place: (0, 0))] * len(pieces),
             out_specs=out_specs,
         ),
-        compiler_params=pltpu.CompilerParams(vmem_limit_bytes=40 * 1024 * 1024),
-        cost_estimate=pl.CostEstimate(flops=2 * 4 * ROWS * M // 8 * (K - FEW), bytes_accessed=8 * 1024 * 1024, transcendentals=0),
+        compiler_params=pltpu.CompilerParams(vmem_limit_bytes=16 * 1024 * 1024),
+        cost_estimate=pl.CostEstimate(flops=2 * 4 * ROWS * M // 8 * (width), bytes_accessed=8 * 1024 * 1024, transcendentals=0),
     )(place, factor.reshape(4, 2, ROWS, 32 * ROWS), many, *pieces)
 
 
 def summed_product(factor, many, pieces, keep):
     core = lax.axis_index("core")
     both = product_few(factor, pieces)
-    few = jnp.sum(exchange(both[1] + permute(both[0], other_core), "x"), axis=0)
+    few = both[1] + permute(both[0], other_core)
     many, few = lax.optimization_barrier((many, few))
     came = permute(product_many(factor, many, 1 - core)[0], other_core)
     mine = product_many(factor, many, core, pieces if keep else [])
-    total = jnp.sum(exchange(mine[0] + came, "x"), axis=0)
-    return jnp.concatenate([few, total], axis=1), mine[-1]
+    total = jnp.concatenate([few, mine[0] + came], axis=2)
+    return jnp.sum(exchange(total, "x"), axis=0), mine[-1]
 
 
 def gram_inverse(values):
@@ -291,9 +295,9 @@
 
 def shards(factor, basis):
     scale = math.sqrt(M)
-    first, _ = summed_product(factor, *basis_rows(basis), False)
+    first, _ = summed_product(factor, *basis_rows(basis, FEW_FIRST), False)
     middle = (dot(first, gram_inverse(first), 1, 1) * scale).astype(jnp.bfloat16)
-    second, column_basis = summed_product(factor, *middle_rows(middle), True)
+    second, column_basis = summed_product(factor, *middle_rows(middle, FEW_SECOND), True)
     return dot(second, gram_inverse(second), 1, 1) * scale, column_basis
 
 

time: 390 us -> 384 us (0.985)
  waiting for transfers between devices: 63.9 us -> 81.2 us
  starting transfers between devices: 93.8 us -> 79.1 us
  blocking collectives: 121 us -> 115 us
    all_to_all x2 -> x1, starting transfers between devices: 24.9 us -> 3.76 us  [exchange(): return lax.all_to_all(pieces, axes, 0, 0, tiled=True)]
    all_gather x2, waiting for transfers between devices: 10.9 us -> 26.9 us  [spread(): return (lax.all_gather(many, 'z', axis=0, tiled=True), few)]
    ppermute x23, starting transfers between devices: 68.8 us -> 75.3 us  [permute(): lax.ppermute(values, AXES, [(index[p], index[where(*p)]) for p in places])]
    all_to_all x9 -> x8, blocking collectives: 121 us -> 115 us  [exchange(): return lax.all_to_all(pieces, axes, 0, 0, tiled=True)]
    ppermute x23, waiting for transfers between devices: 36.4 us -> 40.7 us  [permute(): lax.ppermute(values, AXES, [(index[p], index[where(*p)]) for p in places])]
    all_to_all x2 -> x1, waiting for transfers between devices: 16.5 us -> 13.5 us  [exchange(): return lax.all_to_all(pieces, axes, 0, 0, tiled=True)]
  transfers between devices with their start and end apart: 27 -> 26, of which waited for: 19 -> 17; matrix products, arithmetic and copies ran while one was open for 1% -> 0% of each run, Pallas kernels for 5% -> 5%
where the time goes in v1:
time: 384 us
  blocking collectives  115 us (30%)
  waiting for transfers between devices  81.2 us (21%)
  starting transfers between devices  79.1 us (21%)
  Pallas kernels  64.9 us (17%)
  local copies, waits for them, and re-layouts  21.4 us (6%)
  between operations  14.5 us (4%)
  matrix products  5.08 us (1%)
    all_to_all x8, blocking collectives, exchange(): return lax.all_to_all(pieces, axes, 0, 0, tiled=True)  115 us
    ppermute x23, starting transfers between devices, permute(): lax.ppermute(values, AXES, [(index[p], index[where(*p)]) for p in places])  75.3 us
    ppermute x23, waiting for transfers between devices, permute(): lax.ppermute(values, AXES, [(index[p], index[where(*p)]) for p in places])  40.7 us
    pallas_call x2, Pallas kernels, inverse_factor(): pl.pallas_call(chol_inverse, out_shape=jax.ShapeDtypeStruct((K, K), jnp.f...  40.6 us
    all_gather x2, waiting for transfers between devices, spread(): return (lax.all_gather(many, 'z', axis=0, tiled=True), few)  26.9 us
    unnamed x21, local copies, waits for them, and re-layouts  18.9 us
    pallas_call x4, Pallas kernels, product_many(): pl.pallas_call(many_step, out_shape=out_shape, grid_spec=pltpu.PrefetchSc...  14.1 us
    all_to_all x1, waiting for transfers between devices, exchange(): return lax.all_to_all(pieces, axes, 0, 0, tiled=True)  13.5 us
  transfers between devices with their start and end apart: 26, of which 17 were waited for; matrix products, arithmetic and copies ran while one was open for 0% of the time, Pallas kernels for 5%

profile of v1, /device:TPU:1, one launch (start us, length us, event | category | flops | bytes accessed | tf_op | source)
XLA Modules:
  0.0 383.6 jit_solution(7964897041600342081)
XLA Ops:
  8.3 4.9 %collective-permute-start.1 = (bf16[896,256]{1,0:T(8,128)(2,1)S(1)}, bf16[896,256]{1,0:T(8,128)(2,1)S(1)}, u32[]{:S(2)}, u32[]{:S(2)}) collective-permute-start(bf16[896,256]{1,0:T(8,128)(2,1)S(1)} %slice.33), channel_id=1, source_target_pairs={{0,0},{1,32},{2,64},{3,96},{4,128},{5,160},{6,192},{7,224},{8,8},{... | collective-permute-start | bytes 1376264 | tf_op jit(solution)/shard_map/ppermute | solution.py:123
  14.2 1.9 collective-permute-start
  16.1 7.7 %collective-permute-done = bf16[448,256]{1,0:T(8,128)(2,1)S(1)} collective-permute-done((bf16[448,256]{1,0:T(8,128)(2,1)S(1)}, bf16[448,256]{1,0:T(8,128)(2,1)S(1)}, u32[]{:S(2)}, u32[]{:S(2)}) %collective-permute-start) | collective-permute-done | bytes 229408 | tf_op jit(solution)/shard_map/ppermute | solution.py:123
  24.6 2.0 collective-permute-start.3
  26.5 24.9 %collective-permute-start.2 = (bf16[896,256]{1,0:T(8,128)(2,1)S(1)}, bf16[896,256]{1,0:T(8,128)(2,1)S(1)}, u32[]{:S(2)}, u32[]{:S(2)}) collective-permute-start(bf16[896,256]{1,0:T(8,128)(2,1)S(1)} %collective-permute-done.1.refs_0_), channel_id=1, source_target_pairs={{0,24},{1,25},{2,26},{3,27},{4,28},{5,29},{6,30},{7,31},{8,0},{9,1... | collective-permute-start | bytes 1376264 | tf_op jit(solution)/shard_map/ppermute | solution.py:123
  51.4 5.8 %collective-permute-done.3.refs_3_ = bf16[896,256]{1,0:T(8,128)(2,1)S(1)} collective-permute-done((bf16[896,256]{1,0:T(8,128)(2,1)S(1)}, bf16[896,256]{1,0:T(8,128)(2,1)S(1)}, u32[]{:S(2)}, u32[]{:S(2)}) %collective-permute-start.3) | collective-permute-done | bytes 458784 | tf_op jit(solution)/shard_map/ppermute | solution.py:123
  57.3 2.7 collective-permute-start.5
  60.1 3.2 collective-permute-done.4
  63.4 2.8 copy-done
  66.2 5.2 %shard_map.41 = f32[2,4,112,256]{3,2,1,0:T(8,128)S(1)} custom-call(s32[2]{0:T(128)S(1)} %pad_add_fusion.place, bf16[4,2,112,3584]{3,2,1,0:T(8,128)(2,1)S(1)} %bitcast.33, bf16[896,256]{1,0:T(8,128)(2,1)S(1)} %collective-permute-done.1.refs_0_, bf16[896,256]{1,0:T(8,128)(2,1)S(1)} %collective-permute-done.2.refs_1_, ...), custom_call_target="tpu_custom_call" | custom-call | flops 1644167168 | bytes 8388608 | tf_op jit(solution)/shard_map/pallas_call | solution.py:206
  71.6 1.7 collective-permute-done.6
  73.4 26.9 %all-gather.3.cloned.1.call-done.b_ref = bf16[3584,256]{1,0:T(8,128)(2,1)} async-done(((bf16[448,256]{1,0:T(8,128)(2,1)}), bf16[3584,256]{1,0:T(8,128)(2,1)}) %all-gather.3.cloned.1.call-update) | async-done | bytes 1835024 | tf_op jit(solution)/shard_map/all_gather | solution.py:168
  100.3 2.8 copy-done.1
  104.7 2.7 shard_map.43
  107.3 4.4 %collective-permute-start.7 = (f32[4,112,256]{2,1,0:T(8,128)S(1)}, f32[4,112,256]{2,1,0:T(8,128)S(1)}, u32[]{:S(2)}, u32[]{:S(2)}) collective-permute-start(f32[4,112,256]{2,1,0:T(8,128)S(1)} %shard_map.43), channel_id=1, source_target_pairs={{0,1},{1,0},{2,3},{3,2},{4,5},{5,4},{6,7},{7,6},{8,9},{9,8},{10,11... | collective-permute-start | bytes 1376264 | tf_op jit(solution)/shard_map/ppermute | solution.py:123
  111.8 2.7 shard_map.42
  115.6 3.8 all-to-all-start
  119.4 13.5 %all-to-all-done = f32[4,112,512]{2,1,0:T(8,128)S(1)} async-done(((f32[4,112,512]{2,1,0:T(8,128)}), f32[4,112,512]{2,1,0:T(8,128)S(1)}, u32[]{:S(2)}, u32[]{:S(2)}) %all-to-all-start) | async-done | bytes 917536 | tf_op jit(solution)/shard_map/all_to_all | solution.py:131
  136.9 15.2 %all_to_all.45 = f32[16,16,512]{2,1,0:T(8,128)S(1)} all-to-all(f32[16,16,512]{2,1,0:T(8,128)S(1)} %bitcast.46), channel_id=1, replica_groups=mesh['z'=8,'y'=4,'x'=4,'core'=2] {'y','x'}, dimensions={0} | all-to-all | bytes 1048576 | tf_op jit(solution)/shard_map/all_to_all | solution.py:131
  152.1 13.3 %all_to_all.46 = f32[8,16,512]{2,1,0:T(8,128)S(1)} all-to-all(f32[8,16,512]{2,1,0:T(8,128)S(1)} %broadcast_in_dim.13), channel_id=1, replica_groups=mesh['z'=8,'y'=4,'x'=4,'core'=2] {'z'}, dimensions={0} | all-to-all | bytes 524288 | tf_op jit(solution)/shard_map/all_to_all | solution.py:131
  165.5 13.2 %all_to_all.47 = f32[16,16,512]{2,1,0:T(8,128)S(1)} all-to-all(f32[16,16,512]{2,1,0:T(8,128)S(1)} %broadcast_in_dim.14), channel_id=1, replica_groups=mesh['z'=8,'y'=4,'x'=4,'core'=2] {'y','x'}, dimensions={0} | all-to-all | bytes 1048576 | tf_op jit(solution)/shard_map/all_to_all | solution.py:131
  178.8 4.1 %collective-permute-start.9 = (f32[256,512]{1,0:T(8,128)S(1)}, f32[256,512]{1,0:T(8,128)S(1)}, u32[]{:S(2)}, u32[]{:S(2)}) collective-permute-start(f32[256,512]{1,0:T(8,128)S(1)} %bitcast.43), channel_id=1, source_target_pairs={{0,1},{1,0},{2,3},{3,2},{4,5},{5,4},{6,7},{7,6},{8,9},{9,8},{10,11... | collective-permute-start | bytes 1572872 | tf_op jit(solution)/shard_map/ppermute | solution.py:123
  184.6 20.3 %shard_map.44 = f32[512,512]{1,0:T(8,128)S(1)} custom-call(f32[512,512]{1,0:T(8,128)S(1)} %pad_maximum_fusion.gram_ref), custom_call_target="tpu_custom_call" | custom-call | flops 268435456 | bytes 2097152 | tf_op jit(solution)/shard_map/pallas_call | solution.py:109
  206.1 1.9 collective-permute-start.10
  208.1 3.6 collective-permute-start.14
  211.8 3.8 collective-permute-done.10
  215.5 3.7 collective-permute-start.11
  222.2 2.0 collective-permute-done.12
  226.2 15.1 %all_to_all.48 = bf16[8,112,128]{2,1,0:T(8,128)(2,1)S(1)} all-to-all(bf16[8,112,128]{2,1,0:T(8,128)(2,1)S(1)} %broadcast_in_dim.15), channel_id=1, replica_groups=mesh['z'=8,'y'=4,'x'=4,'core'=2] {'z'}, dimensions={0} | all-to-all | bytes 458752 | tf_op jit(solution)/shard_map/all_to_all | solution.py:131
  241.4 2.7 collective-permute-start.15
  244.0 3.7 collective-permute-done.16.refs_3_
  247.9 3.0 collective-permute-start.18
  250.8 2.9 collective-permute-done.17
  253.8 2.9 copy-done.3
  256.7 5.0 %shard_map.45 = f32[2,4,112,128]{3,2,1,0:T(8,128)S(1)} custom-call(s32[2]{0:T(128)S(1)} %pad_add_fusion.place, bf16[4,2,112,3584]{3,2,1,0:T(8,128)(2,1)S(1)} %bitcast.36, bf16[896,128]{1,0:T(8,128)(2,1)S(1)} %bitcast.41, bf16[896,128]{1,0:T(8,128)(2,1)S(1)} %collective-permute-done.15.refs_1_, ...), custom_call_target="tpu_custom_call" | custom-call | flops 822083584 | bytes 8388608 | tf_op jit(solution)/shard_map/pallas_call | solution.py:206
  261.7 5.8 %collective-permute-start.19 = (f32[4,112,128]{2,1,0:T(8,128)S(1)}, f32[4,112,128]{2,1,0:T(8,128)S(1)}, u32[]{:S(2)}, u32[]{:S(2)}) collective-permute-start(f32[4,112,128]{2,1,0:T(8,128)S(1)} %slice_bitcast_fusion.2), channel_id=1, source_target_pairs={{0,1},{1,0},{2,3},{3,2},{4,5},{5,4},{6,7},{7,6},{8,9},{9,8},{10,11... | collective-permute-start | bytes 688136 | tf_op jit(solution)/shard_map/ppermute | solution.py:123
  268.7 2.8 copy-done.4
  271.5 1.8 copy-done.6
  273.3 3.6 shard_map.47
  278.2 2.8 copy-done.5
  281.1 5.2 %shard_map.46 = (f32[4,112,384]{2,1,0:T(8,128)S(1)}, bf16[3584,512]{1,0:T(8,128)(2,1)}) custom-call(s32[2]{0:T(128)S(1)} %pad_add_fusion.1.place, bf16[4,2,112,3584]{3,2,1,0:T(8,128)(2,1)S(1)} %bitcast.38, bf16[3584,384]{1,0:T(8,128)(2,1)S(1)} %copy-done.6, bf16[896,128]{1,0:T(8,128)(2,1)S(1)} %bitcast.42, ...), custom_call_target="tpu_custom_call" | custom-call | flops 1233125376 | bytes 8388608 | tf_op jit(solution)/shard_map/pallas_call | solution.py:254
  286.5 18.0 %all_to_all.49 = f32[4,112,512]{2,1,0:T(8,128)S(1)} all-to-all(f32[4,112,512]{2,1,0:T(8,128)S(1)} %pad_maximum_fusion.3), channel_id=1, replica_groups=mesh['z'=8,'y'=4,'x'=4,'core'=2] {'x'}, dimensions={0} | all-to-all | bytes 1835008 | tf_op jit(solution)/shard_map/all_to_all | solution.py:131
  308.5 14.9 %all_to_all.50 = f32[16,16,512]{2,1,0:T(8,128)S(1)} all-to-all(f32[16,16,512]{2,1,0:T(8,128)S(1)} %bitcast.45), channel_id=1, replica_groups=mesh['z'=8,'y'=4,'x'=4,'core'=2] {'y','x'}, dimensions={0} | all-to-all | bytes 1048576 | tf_op jit(solution)/shard_map/all_to_all | solution.py:131
  323.4 12.0 %all_to_all.51 = f32[8,16,512]{2,1,0:T(8,128)S(1)} all-to-all(f32[8,16,512]{2,1,0:T(8,128)S(1)} %broadcast_in_dim.16), channel_id=1, replica_groups=mesh['z'=8,'y'=4,'x'=4,'core'=2] {'z'}, dimensions={0} | all-to-all | bytes 524288 | tf_op jit(solution)/shard_map/all_to_all | solution.py:131
  335.5 13.2 %all_to_all.52 = f32[16,16,512]{2,1,0:T(8,128)S(1)} all-to-all(f32[16,16,512]{2,1,0:T(8,128)S(1)} %broadcast_in_dim.17), channel_id=1, replica_groups=mesh['z'=8,'y'=4,'x'=4,'core'=2] {'y','x'}, dimensions={0} | all-to-all | bytes 1048576 | tf_op jit(solution)/shard_map/all_to_all | solution.py:131
  348.7 4.1 %collective-permute-start.22 = (f32[256,512]{1,0:T(8,128)S(1)}, f32[256,512]{1,0:T(8,128)S(1)}, u32[]{:S(2)}, u32[]{:S(2)}) collective-permute-start(f32[256,512]{1,0:T(8,128)S(1)} %bitcast.44), channel_id=1, source_target_pairs={{0,1},{1,0},{2,3},{3,2},{4,5},{5,4},{6,7},{7,6},{8,9},{9,8},{10,11... | collective-permute-start | bytes 1572872 | tf_op jit(solution)/shard_map/ppermute | solution.py:123
  354.6 20.3 %shard_map.48 = f32[512,512]{1,0:T(8,128)S(1)} custom-call(f32[512,512]{1,0:T(8,128)S(1)} %pad_maximum_fusion.1.gram_ref), custom_call_target="tpu_custom_call" | custom-call | flops 268435456 | bytes 2097152 | tf_op jit(solution)/shard_map/pallas_call | solution.py:109
  374.9 1.9 convolution_multiply_fusion
  (92 shorter events, 26.6 us)
Async XLA Ops:
  7.2 93.2 %all-gather.3.cloned.1.call-start = ((), (), s32[]{:S(2)}) async-start(), calls=%async_computation.9 | async-start | bytes 2064384 | tf_op jit(solution)/shard_map/all_gather | solution.py:168
  8.3 15.6 %collective-permute-start.1 = (bf16[896,256]{1,0:T(8,128)(2,1)S(1)}, bf16[896,256]{1,0:T(8,128)(2,1)S(1)}, u32[]{:S(2)}, u32[]{:S(2)}) collective-permute-start(bf16[896,256]{1,0:T(8,128)(2,1)S(1)} %slice.33), channel_id=1, source_target_pairs={{0,0},{1,32},{2,64},{3,96},{4,128},{5,160},{6,192},{7,224},{8,8},{... | collective-permute-start | bytes 1376264 | tf_op jit(solution)/shard_map/ppermute | solution.py:123
  14.2 9.7 %collective-permute-start = (bf16[448,256]{1,0:T(8,128)(2,1)S(1)}, bf16[448,256]{1,0:T(8,128)(2,1)S(1)}, u32[]{:S(2)}, u32[]{:S(2)}) collective-permute-start(bf16[448,256]{1,0:T(8,128)(2,1)S(1)} %constant_dynamic-slice_fusion.2), channel_id=1, source_target_pairs={{0,0},{1,32},{2,8},{3,40},{4,16},{5,48},{6,24},{7,56},{8,64},{9,96... | collective-permute-start | bytes 688136 | tf_op jit(solution)/shard_map/ppermute | solution.py:123
  23.8 0.7 copy-start.9
  24.6 32.6 %collective-permute-start.3 = (bf16[896,256]{1,0:T(8,128)(2,1)S(1)}, bf16[896,256]{1,0:T(8,128)(2,1)S(1)}, u32[]{:S(2)}, u32[]{:S(2)}) collective-permute-start(bf16[896,256]{1,0:T(8,128)(2,1)S(1)} %collective-permute-done.1.refs_0_), channel_id=1, source_target_pairs={{0,8},{1,9},{2,10},{3,11},{4,12},{5,13},{6,14},{7,15},{8,16},{9,17... | collective-permute-start | bytes 1376264 | tf_op jit(solution)/shard_map/ppermute | solution.py:123
  26.5 30.8 %collective-permute-start.2 = (bf16[896,256]{1,0:T(8,128)(2,1)S(1)}, bf16[896,256]{1,0:T(8,128)(2,1)S(1)}, u32[]{:S(2)}, u32[]{:S(2)}) collective-permute-start(bf16[896,256]{1,0:T(8,128)(2,1)S(1)} %collective-permute-done.1.refs_0_), channel_id=1, source_target_pairs={{0,24},{1,25},{2,26},{3,27},{4,28},{5,29},{6,30},{7,31},{8,0},{9,1... | collective-permute-start | bytes 1376264 | tf_op jit(solution)/shard_map/ppermute | solution.py:123
  57.2 6.2 %collective-permute-start.4 = (bf16[448,256]{1,0:T(8,128)(2,1)S(1)}, bf16[448,256]{1,0:T(8,128)(2,1)S(1)}, u32[]{:S(2)}, u32[]{:S(2)}) collective-permute-start(bf16[448,256]{1,0:T(8,128)(2,1)S(1)} %slice.44), channel_id=1, source_target_pairs={{0,8},{1,9},{2,10},{3,11},{4,12},{5,13},{6,14},{7,15},{8,16},{9,17... | collective-permute-start | bytes 688136 | tf_op jit(solution)/shard_map/ppermute | solution.py:123
  57.3 6.0 %collective-permute-start.5 = (bf16[448,256]{1,0:T(8,128)(2,1)S(1)}, bf16[448,256]{1,0:T(8,128)(2,1)S(1)}, u32[]{:S(2)}, u32[]{:S(2)}) collective-permute-start(bf16[448,256]{1,0:T(8,128)(2,1)S(1)} %slice.45), channel_id=1, source_target_pairs={{0,24},{1,25},{2,26},{3,27},{4,28},{5,29},{6,30},{7,31},{8,0},{9,1... | collective-permute-start | bytes 688136 | tf_op jit(solution)/shard_map/ppermute | solution.py:123
  63.4 2.8 copy-start
  71.4 1.9 collective-permute-start.6
  100.3 2.8 copy-start.1
  103.2 1.5 copy-start.7
  104.7 7.2 %copy-start.2 = (bf16[896,3584]{1,0:T(8,128)(2,1)S(1)}, bf16[896,3584]{1,0:T(8,128)(2,1)}, u32[]{:S(2)}) copy-start(bf16[896,3584]{1,0:T(8,128)(2,1)} %param.2) | copy-start | bytes 19267588
  107.3 7.2 %collective-permute-start.7 = (f32[4,112,256]{2,1,0:T(8,128)S(1)}, f32[4,112,256]{2,1,0:T(8,128)S(1)}, u32[]{:S(2)}, u32[]{:S(2)}) collective-permute-start(f32[4,112,256]{2,1,0:T(8,128)S(1)} %shard_map.43), channel_id=1, source_target_pairs={{0,1},{1,0},{2,3},{3,2},{4,5},{5,4},{6,7},{7,6},{8,9},{9,8},{10,11... | collective-permute-start | bytes 1376264 | tf_op jit(solution)/shard_map/ppermute | solution.py:123
  115.6 17.3 %all-to-all-start = ((f32[4,112,512]{2,1,0:T(8,128)}), f32[4,112,512]{2,1,0:T(8,128)S(1)}, u32[]{:S(2)}, u32[]{:S(2)}) async-start(f32[4,112,512]{2,1,0:T(8,128)} %pad_maximum_fusion.2), calls=%async_computation | async-start | bytes 1835008 | tf_op jit(solution)/shard_map/all_to_all | solution.py:131
  119.4 149.3 %all-gather.5.cloned.1.call-start = ((), (), s32[]{:S(2)}) async-start(), calls=%async_computation.10 | async-start | bytes 3096576 | tf_op jit(solution)/shard_map/all_gather | solution.py:168
  134.1 2.7 collective-permute-start.8
  178.8 5.6 %collective-permute-start.9 = (f32[256,512]{1,0:T(8,128)S(1)}, f32[256,512]{1,0:T(8,128)S(1)}, u32[]{:S(2)}, u32[]{:S(2)}) collective-permute-start(f32[256,512]{1,0:T(8,128)S(1)} %bitcast.43), channel_id=1, source_target_pairs={{0,1},{1,0},{2,3},{3,2},{4,5},{5,4},{6,7},{7,6},{8,9},{9,8},{10,11... | collective-permute-start | bytes 1572872 | tf_op jit(solution)/shard_map/ppermute | solution.py:123
  206.1 9.4 %collective-permute-start.10 = (bf16[112,384]{1,0:T(8,128)(2,1)S(1)}, bf16[112,384]{1,0:T(8,128)(2,1)S(1)}, u32[]{:S(2)}, u32[]{:S(2)}) collective-permute-start(bf16[112,384]{1,0:T(8,128)(2,1)S(1)} %slice.48), channel_id=1, source_target_pairs={{0,0},{1,8},{2,16},{3,24},{4,32},{5,40},{6,48},{7,56},{8,64},{9,72... | collective-permute-start | bytes 258056 | tf_op jit(solution)/shard_map/ppermute | solution.py:123
  208.1 17.4 %collective-permute-start.14 = (bf16[112,128]{1,0:T(8,128)(2,1)S(1)}, bf16[112,128]{1,0:T(8,128)(2,1)S(1)}, u32[]{:S(2)}, u32[]{:S(2)}) collective-permute-start(bf16[112,128]{1,0:T(8,128)(2,1)S(1)} %slice.49), channel_id=1, source_target_pairs={{0,0},{1,32},{2,64},{3,96},{4,128},{5,160},{6,192},{7,224},{8,8},{... | collective-permute-start | bytes 86024 | tf_op jit(solution)/shard_map/ppermute | solution.py:123
  215.5 6.6 %collective-permute-start.11 = (bf16[112,384]{1,0:T(8,128)(2,1)S(1)}, bf16[112,384]{1,0:T(8,128)(2,1)S(1)}, u32[]{:S(2)}, u32[]{:S(2)}) collective-permute-start(bf16[112,384]{1,0:T(8,128)(2,1)S(1)} %collective-permute-done.10), channel_id=1, source_target_pairs={{0,24},{1,25},{2,26},{3,27},{4,28},{5,29},{6,30},{7,31},{8,0},{9,1... | collective-permute-start | bytes 258056 | tf_op jit(solution)/shard_map/ppermute | solution.py:123
  219.2 5.0 %collective-permute-start.12 = (bf16[112,384]{1,0:T(8,128)(2,1)S(1)}, bf16[112,384]{1,0:T(8,128)(2,1)S(1)}, u32[]{:S(2)}, u32[]{:S(2)}) collective-permute-start(bf16[112,384]{1,0:T(8,128)(2,1)S(1)} %collective-permute-done.10), channel_id=1, source_target_pairs={{0,16},{1,17},{2,18},{3,19},{4,20},{5,21},{6,22},{7,23},{8,24},{9,... | collective-permute-start | bytes 258056 | tf_op jit(solution)/shard_map/ppermute | solution.py:123
  219.9 5.6 %collective-permute-start.13 = (bf16[112,384]{1,0:T(8,128)(2,1)S(1)}, bf16[112,384]{1,0:T(8,128)(2,1)S(1)}, u32[]{:S(2)}, u32[]{:S(2)}) collective-permute-start(bf16[112,384]{1,0:T(8,128)(2,1)S(1)} %collective-permute-done.10), channel_id=1, source_target_pairs={{0,8},{1,9},{2,10},{3,11},{4,12},{5,13},{6,14},{7,15},{8,16},{9,17... | collective-permute-start | bytes 258056 | tf_op jit(solution)/shard_map/ppermute | solution.py:123
  225.4 0.7 copy-start.8
  241.4 6.3 %collective-permute-start.16 = (bf16[896,128]{1,0:T(8,128)(2,1)S(1)}, bf16[896,128]{1,0:T(8,128)(2,1)S(1)}, u32[]{:S(2)}, u32[]{:S(2)}) collective-permute-start(bf16[896,128]{1,0:T(8,128)(2,1)S(1)} %bitcast.39), channel_id=1, source_target_pairs={{0,8},{1,9},{2,10},{3,11},{4,12},{5,13},{6,14},{7,15},{8,16},{9,17... | collective-permute-start | bytes 688136 | tf_op jit(solution)/shard_map/ppermute | solution.py:123
  241.4 6.5 %collective-permute-start.15 = (bf16[896,128]{1,0:T(8,128)(2,1)S(1)}, bf16[896,128]{1,0:T(8,128)(2,1)S(1)}, u32[]{:S(2)}, u32[]{:S(2)}) collective-permute-start(bf16[896,128]{1,0:T(8,128)(2,1)S(1)} %bitcast.40), channel_id=1, source_target_pairs={{0,24},{1,25},{2,26},{3,27},{4,28},{5,29},{6,30},{7,31},{8,0},{9,1... | collective-permute-start | bytes 688136 | tf_op jit(solution)/shard_map/ppermute | solution.py:123
  247.7 6.0 %collective-permute-start.17 = (bf16[448,128]{1,0:T(8,128)(2,1)S(1)}, bf16[448,128]{1,0:T(8,128)(2,1)S(1)}, u32[]{:S(2)}, u32[]{:S(2)}) collective-permute-start(bf16[448,128]{1,0:T(8,128)(2,1)S(1)} %slice.50), channel_id=1, source_target_pairs={{0,8},{1,9},{2,10},{3,11},{4,12},{5,13},{6,14},{7,15},{8,16},{9,17... | collective-permute-start | bytes 344072 | tf_op jit(solution)/shard_map/ppermute | solution.py:123
  247.9 5.9 %collective-permute-start.18 = (bf16[448,128]{1,0:T(8,128)(2,1)S(1)}, bf16[448,128]{1,0:T(8,128)(2,1)S(1)}, u32[]{:S(2)}, u32[]{:S(2)}) collective-permute-start(bf16[448,128]{1,0:T(8,128)(2,1)S(1)} %slice.51), channel_id=1, source_target_pairs={{0,24},{1,25},{2,26},{3,27},{4,28},{5,29},{6,30},{7,31},{8,0},{9,1... | collective-permute-start | bytes 344072 | tf_op jit(solution)/shard_map/ppermute | solution.py:123
  253.8 2.9 copy-start.3
  261.7 6.9 %collective-permute-start.19 = (f32[4,112,128]{2,1,0:T(8,128)S(1)}, f32[4,112,128]{2,1,0:T(8,128)S(1)}, u32[]{:S(2)}, u32[]{:S(2)}) collective-permute-start(f32[4,112,128]{2,1,0:T(8,128)S(1)} %slice_bitcast_fusion.2), channel_id=1, source_target_pairs={{0,1},{1,0},{2,3},{3,2},{4,5},{5,4},{6,7},{7,6},{8,9},{9,8},{10,11... | collective-permute-start | bytes 688136 | tf_op jit(solution)/shard_map/ppermute | solution.py:123
  268.7 2.8 copy-start.4
  271.5 1.8 copy-start.6
  276.9 9.4 %collective-permute-start.20 = (f32[4,112,384]{2,1,0:T(8,128)S(1)}, f32[4,112,384]{2,1,0:T(8,128)S(1)}, u32[]{:S(2)}, u32[]{:S(2)}) collective-permute-start(f32[4,112,384]{2,1,0:T(8,128)S(1)} %shard_map.47), channel_id=1, source_target_pairs={{0,1},{1,0},{2,3},{3,2},{4,5},{5,4},{6,7},{7,6},{8,9},{9,8},{10,11... | collective-permute-start | bytes 2064392 | tf_op jit(solution)/shard_map/ppermute | solution.py:123
  278.2 2.8 copy-start.5
  305.7 2.7 collective-permute-start.21
  348.7 5.6 %collective-permute-start.22 = (f32[256,512]{1,0:T(8,128)S(1)}, f32[256,512]{1,0:T(8,128)S(1)}, u32[]{:S(2)}, u32[]{:S(2)}) collective-permute-start(f32[256,512]{1,0:T(8,128)S(1)} %bitcast.44), channel_id=1, source_target_pairs={{0,1},{1,0},{2,3},{3,2},{4,5},{5,4},{6,7},{7,6},{8,9},{9,8},{10,11... | collective-permute-start | bytes 1572872 | tf_op jit(solution)/shard_map/ppermute | solution.py:123
Sparse Core Ops, SparseCore 0:
  24.7 75.6 all-gather.2
  226.3 41.1 all-gather.4

commit v2 on v0

--- a/solution.py
+++ b/solution.py
@@ -111,7 +111,7 @@
         in_specs=[pl.BlockSpec(memory_space=pltpu.VMEM)],
         out_specs=pl.BlockSpec(memory_space=pltpu.VMEM),
         scratch_shapes=[pltpu.VMEM((K, K), jnp.float32)],
-        compiler_params=pltpu.CompilerParams(vmem_limit_bytes=32 * 1024 * 1024),
+        compiler_params=pltpu.CompilerParams(vmem_limit_bytes=12 * 1024 * 1024),
         cost_estimate=pl.CostEstimate(flops=2 * K ** 3, bytes_accessed=8 * K * K, transcendentals=0),
     )(gram)
 
@@ -158,62 +158,59 @@
     return out
 
 
-def column_block(z, y, x, c):
-    return 2 * x + c, y, z // 2, z % 2
-
-
-def spread(many, few):
-    many, few = lax.optimization_barrier((many, few))
-    return lax.all_gather(many, "z", axis=0, tiled=True), few
-
-
-def basis_rows(basis):
-    sent = lax.dynamic_slice(basis, (lax.axis_index("core") * 4 * ROWS, FEW), (4 * ROWS, K - FEW))
-    many = permute(sent, lambda z, y, x, c: (2 * y + c, x, z // 2, z % 2))
-    few = permute(basis[:, :FEW], column_block)
-    many, few = spread(many, few)
-    return many, gather_y(few)
-
-
-def middle_rows(rows):
-    def chunk_place(z, y, x, c):
-        chunk = 8 * y + 2 * x + c
-        return chunk // 4, chunk % 4, z // 2, z % 2
-    many = permute(rows[:, FEW:], chunk_place)
-    few = permute(rows[:, :FEW], column_block)
-    many, few = spread(gather_y_small(many), few)
-    return many, gather_y(exchange(copies(few, "z"), "z").reshape(8 * ROWS, FEW))
+def chunk_place(z, y, x, c):
+    chunk = 8 * y + 2 * x + c
+    return chunk // 4, chunk % 4, z // 2, z % 2
+
+
+def gathered_rows(rows):
+    own = permute(rows, chunk_place)
+    many, few = lax.optimization_barrier((gather_y_small(own[:, FEW:]), own[:, :FEW]))
+    return lax.all_gather(many, "z", axis=0, tiled=True), gather_y(exchange(copies(few, "z"), "z"))
 
 
 def few_step(place, a_ref, *refs):
-    pieces, out_ref = refs[:4], refs[4]
+    pieces, out_ref, rows_ref = refs[:4], refs[4], refs[5]
+    step = pl.program_id(1)
+
+    @pl.when((pl.program_id(0) == 0) & (step == 0))
+    def _():
+        for j in range(4):
+            rows_ref[:, lax.rem(place[0] + j, 4)] = pieces[j][...]
+
     a = a_ref[...].reshape(4 * ROWS, 8 * ROWS)
-    for j in range(4):
-        @pl.when(pl.program_id(1) == j)
-        def _():
-            term = jnp.dot(a, pieces[j][...], preferred_element_type=jnp.float32).reshape(4, ROWS, FEW)
-            if j == 0:
-                out_ref[...] = term
-            else:
-                out_ref[...] += term
+    b = rows_ref[pl.ds(2 * step, 2)].reshape(8 * ROWS, FEW)
+    term = jnp.dot(a, b, preferred_element_type=jnp.float32).reshape(out_ref.shape)
+
+    @pl.when(step == 0)
+    def _():
+        out_ref[...] = term
+
+    @pl.when(step > 0)
+    def _():
+        out_ref[...] += term
 
 
 def product_few(factor, pieces):
-    core = lax.axis_index("core")
-    place = jnp.stack([lax.axis_index("y"), core]).astype(jnp.int32)
+    place = jnp.stack([lax.axis_index("y"), lax.axis_index("core")]).astype(jnp.int32)
     return pl.pallas_call(
         few_step,
-        out_shape=jax.ShapeDtypeStruct((2, 4, ROWS, FEW), jnp.float32),
+        out_shape=[
+            jax.ShapeDtypeStruct((2, 4, ROWS, FEW), jnp.float32),
+            jax.ShapeDtypeStruct((8, 4, ROWS, FEW), jnp.bfloat16),
+        ],
         grid_spec=pltpu.PrefetchScalarGridSpec(
             num_scalar_prefetch=1,
             grid=(2, 4),
             in_specs=[
-                pl.BlockSpec((4, None, ROWS, 8 * ROWS),
-                             lambda h, q, place: (0, lax.rem(place[1] + 1 + h, 2), 0, lax.rem(place[0] + q, 4))),
-            ] + [pl.BlockSpec((8 * ROWS, FEW), lambda h, q, place: (0, 0))] * 4,
-            out_specs=pl.BlockSpec((None, 4, ROWS, FEW), lambda h, q, place: (h, 0, 0, 0)),
+                pl.BlockSpec((4, None, ROWS, 8 * ROWS), lambda h, q, place: (0, lax.rem(place[1] + 1 + h, 2), 0, q)),
+            ] + [pl.BlockSpec((8, ROWS, FEW), lambda h, q, place: (0, 0, 0))] * 4,
+            out_specs=[
+                pl.BlockSpec((None, 4, ROWS, FEW), lambda h, q, place: (h, 0, 0, 0)),
+                pl.BlockSpec((8, 4, ROWS, FEW), lambda h, q, place: (0, 0, 0, 0)),
+            ],
         ),
-        compiler_params=pltpu.CompilerParams(vmem_limit_bytes=40 * 1024 * 1024),
+        compiler_params=pltpu.CompilerParams(vmem_limit_bytes=16 * 1024 * 1024),
         cost_estimate=pl.CostEstimate(flops=2 * 8 * ROWS * M // 8 * FEW, bytes_accessed=8 * 1024 * 1024, transcendentals=0),
     )(place, factor.reshape(4, 2, ROWS, 32 * ROWS), *pieces)
 
@@ -223,12 +220,9 @@
     a = a_ref[...].reshape(4 * ROWS, 8 * ROWS)
     out_ref = refs[-1]
     if len(refs) > 1:
-        pieces, out_ref, rows_ref = refs[:4], refs[4], refs[5]
+        few_ref, out_ref, rows_ref = refs
+        rows_ref[:, :FEW] = few_ref[...]
         rows_ref[:, FEW:] = b_ref[...]
-        for j in range(4):
-            @pl.when(lax.rem(place[1] + j, 4) == step)
-            def _():
-                rows_ref[:, :FEW] = pieces[j][...]
     term = jnp.dot(a, b_ref[...], preferred_element_type=jnp.float32).reshape(out_ref.shape)
 
     @pl.when(step == 0)
@@ -240,11 +234,11 @@
         out_ref[...] += term
 
 
-def product_many(factor, many, core, pieces=()):
-    place = jnp.stack([core, lax.axis_index("y")]).astype(jnp.int32)
+def product_many(factor, many, core, few=None):
+    operands = [many] if few is None else [many, few]
     out_shape = [jax.ShapeDtypeStruct((4, ROWS, K - FEW), jnp.float32)]
     out_specs = [pl.BlockSpec((4, ROWS, K - FEW), lambda q, place: (0, 0, 0))]
-    if pieces:
+    if few is not None:
         out_shape.append(jax.ShapeDtypeStruct((32 * ROWS, K), jnp.bfloat16))
         out_specs.append(pl.BlockSpec((8 * ROWS, K), lambda q, place: (q, 0)))
     return pl.pallas_call(
@@ -253,26 +247,25 @@
         grid_spec=pltpu.PrefetchScalarGridSpec(
             num_scalar_prefetch=1,
             grid=(4,),
-            in_specs=[
-                pl.BlockSpec((4, None, ROWS, 8 * ROWS), lambda q, place: (0, place[0], 0, q)),
-                pl.BlockSpec((8 * ROWS, K - FEW), lambda q, place: (q, 0)),
-            ] + [pl.BlockSpec((8 * ROWS, FEW), lambda q, place: (0, 0))] * len(pieces),
+            in_specs=[pl.BlockSpec((4, None, ROWS, 8 * ROWS), lambda q, place: (0, place[0], 0, q))]
+            + [pl.BlockSpec((8 * ROWS, operand.shape[1]), lambda q, place: (q, 0)) for operand in operands],
             out_specs=out_specs,
         ),
-        compiler_params=pltpu.CompilerParams(vmem_limit_bytes=40 * 1024 * 1024),
+        compiler_params=pltpu.CompilerParams(vmem_limit_bytes=16 * 1024 * 1024),
         cost_estimate=pl.CostEstimate(flops=2 * 4 * ROWS * M // 8 * (K - FEW), bytes_accessed=8 * 1024 * 1024, transcendentals=0),
-    )(place, factor.reshape(4, 2, ROWS, 32 * ROWS), many, *pieces)
-
-
-def summed_product(factor, many, pieces, keep):
+    )(core.astype(jnp.int32).reshape(1), factor.reshape(4, 2, ROWS, 32 * ROWS), *operands)
+
+
+def summed_product(factor, rows, keep):
     core = lax.axis_index("core")
-    both = product_few(factor, pieces)
-    few = jnp.sum(exchange(both[1] + permute(both[0], other_core), "x"), axis=0)
+    many, pieces = gathered_rows(rows)
+    both, ordered = product_few(factor, pieces)
+    few = both[1] + permute(both[0], other_core)
     many, few = lax.optimization_barrier((many, few))
     came = permute(product_many(factor, many, 1 - core)[0], other_core)
-    mine = product_many(factor, many, core, pieces if keep else [])
-    total = jnp.sum(exchange(mine[0] + came, "x"), axis=0)
-    return jnp.concatenate([few, total], axis=1), mine[-1]
+    mine = product_many(factor, many, core, ordered.reshape(32 * ROWS, FEW) if keep else None)
+    total = jnp.concatenate([few, mine[0] + came], axis=2)
+    return jnp.sum(exchange(total, "x"), axis=0), mine[-1]
 
 
 def gram_inverse(values):
@@ -291,9 +284,10 @@
 
 def shards(factor, basis):
     scale = math.sqrt(M)
-    first, _ = summed_product(factor, *basis_rows(basis), False)
+    own = lax.dynamic_slice_in_dim(basis, lax.axis_index(("x", "core")) * ROWS, ROWS, 0)
+    first, _ = summed_product(factor, own, False)
     middle = (dot(first, gram_inverse(first), 1, 1) * scale).astype(jnp.bfloat16)
-    second, column_basis = summed_product(factor, *middle_rows(middle), True)
+    second, column_basis = summed_product(factor, middle, True)
     return dot(second, gram_inverse(second), 1, 1) * scale, column_basis
 
 

time: 390 us -> 371 us (0.951)
  starting transfers between devices: 93.8 us -> 58.9 us
  blocking collectives: 121 us -> 135 us
    all_to_all x2 -> x1, starting transfers between devices: 24.9 us -> 3.51 us  [exchange(): return lax.all_to_all(pieces, axes, 0, 0, tiled=True)]
    all_to_all x9, blocking collectives: 121 us -> 135 us  [exchange(): return lax.all_to_all(pieces, axes, 0, 0, tiled=True)]
    ppermute x23 -> x24, waiting for transfers between devices: 36.4 us -> 50.6 us  [permute(): lax.ppermute(values, AXES, [(index[p], index[where(*p)]) for p in places])]
    ppermute x23 -> x24, starting transfers between devices: 68.8 us -> 55.3 us  [permute(): lax.ppermute(values, AXES, [(index[p], index[where(*p)]) for p in places])]
    all_gather x2, waiting for transfers between devices: 10.9 us -> 0.04 us  [gathered_rows(): lax.all_gather(many, 'z', axis=0, tiled=True)]
    unnamed x21 -> x26, local copies, waits for them, and re-layouts: 19.2 us -> 23.2 us
    all_to_all x2 -> x1, waiting for transfers between devices: 16.5 us -> 13.5 us  [exchange(): return lax.all_to_all(pieces, axes, 0, 0, tiled=True)]
  transfers between devices with their start and end apart: 27 -> 27, of which waited for: 19 -> 18; matrix products, arithmetic and copies ran while one was open for 1% -> 0% of each run, Pallas kernels for 5% -> 5%
where the time goes in v2:
time: 371 us; the launch traced here: 370 us
  blocking collectives  135 us (36%)
  Pallas kernels  64.2 us (17%)
  waiting for transfers between devices  64.1 us (17%)
  starting transfers between devices  58.9 us (16%)
  local copies, waits for them, and re-layouts  24.6 us (7%)
  between operations  14.5 us (4%)
  matrix products  5.09 us (1%)
    all_to_all x9, blocking collectives, exchange(): return lax.all_to_all(pieces, axes, 0, 0, tiled=True)  135 us
    ppermute x24, starting transfers between devices, permute(): lax.ppermute(values, AXES, [(index[p], index[where(*p)]) for p in places])  55.3 us
    ppermute x24, waiting for transfers between devices, permute(): lax.ppermute(values, AXES, [(index[p], index[where(*p)]) for p in places])  50.6 us
    pallas_call x2, Pallas kernels, inverse_factor(): pl.pallas_call(chol_inverse, out_shape=jax.ShapeDtypeStruct((K, K), jnp.f...  40.6 us
    unnamed x26, local copies, waits for them, and re-layouts  23.2 us
    all_to_all x1, waiting for transfers between devices, exchange(): return lax.all_to_all(pieces, axes, 0, 0, tiled=True)  13.5 us
    pallas_call x4, Pallas kernels, product_many(): pl.pallas_call(many_step, out_shape=out_shape, grid_spec=pltpu.PrefetchSc...  13.5 us
    pallas_call x2, Pallas kernels, product_few(): pl.pallas_call(few_step, out_shape=[jax.ShapeDtypeStruct((2, 4, ROWS, FEW...  10.1 us
  transfers between devices with their start and end apart: 27, of which 18 were waited for; matrix products, arithmetic and copies ran while one was open for 0% of the time, Pallas kernels for 5%

profile of v2, /device:TPU:1, one launch (start us, length us, event | category | flops | bytes accessed | tf_op | source)
XLA Modules:
  0.0 370.2 jit_solution(8814736118084843872)
XLA Ops:
  8.4 4.6 %collective-permute-start = (bf16[112,512]{1,0:T(8,128)(2,1)S(1)}, bf16[112,512]{1,0:T(8,128)(2,1)S(1)}, u32[]{:S(2)}, u32[]{:S(2)}) collective-permute-start(bf16[112,512]{1,0:T(8,128)(2,1)S(1)} %constant_dynamic-slice_fusion.2), channel_id=1, source_target_pairs={{0,0},{1,8},{2,16},{3,24},{4,32},{5,40},{6,48},{7,56},{8,64},{9,72... | collective-permute-start | bytes 344072 | tf_op jit(solution)/shard_map/ppermute | solution.py:122
  13.0 8.8 %collective-permute-done = bf16[112,512]{1,0:T(8,128)(2,1)S(1)} collective-permute-done((bf16[112,512]{1,0:T(8,128)(2,1)S(1)}, bf16[112,512]{1,0:T(8,128)(2,1)S(1)}, u32[]{:S(2)}, u32[]{:S(2)}) %collective-permute-start) | collective-permute-done | bytes 114720 | tf_op jit(solution)/shard_map/ppermute | solution.py:122
  21.9 4.4 %collective-permute-start.1 = (bf16[112,384]{1,0:T(8,128)(2,1)S(1)}, bf16[112,384]{1,0:T(8,128)(2,1)S(1)}, u32[]{:S(2)}, u32[]{:S(2)}) collective-permute-start(bf16[112,384]{1,0:T(8,128)(2,1)S(1)} %get-tuple-element.34), channel_id=1, source_target_pairs={{0,24},{1,25},{2,26},{3,27},{4,28},{5,29},{6,30},{7,31},{8,0},{9,1... | collective-permute-start | bytes 258056 | tf_op jit(solution)/shard_map/ppermute | solution.py:122
  31.6 2.5 collective-permute-done.3
  34.9 20.3 %all_to_all.50.refs_0_ = bf16[8,112,128]{2,1,0:T(8,128)(2,1)S(1)} all-to-all(bf16[8,112,128]{2,1,0:T(8,128)(2,1)S(1)} %broadcast_in_dim.12), channel_id=1, replica_groups=mesh['z'=8,'y'=4,'x'=4,'core'=2] {'z'}, dimensions={0} | all-to-all | bytes 458752 | tf_op jit(solution)/shard_map/all_to_all | solution.py:130
  55.2 2.7 collective-permute-start.4
  57.9 3.8 %collective-permute-done.5.refs_3_ = bf16[8,112,128]{2,1,0:T(8,128)(2,1)S(1)} collective-permute-done((bf16[8,112,128]{2,1,0:T(8,128)(2,1)S(1)}, bf16[8,112,128]{2,1,0:T(8,128)(2,1)S(1)}, u32[]{:S(2)}, u32[]{:S(2)}) %collective-permute-start.5) | collective-permute-done | bytes 229408 | tf_op jit(solution)/shard_map/ppermute | solution.py:122
  61.8 2.7 collective-permute-start.7
  64.6 2.6 collective-permute-done.6
  67.3 2.9 copy-done.1
  70.2 5.5 %shard_map.41 = (f32[2,4,112,128]{3,2,1,0:T(8,128)S(1)}, bf16[8,4,112,128]{3,2,1,0:T(8,128)(2,1)}) custom-call(s32[2]{0:T(128)S(1)} %pad_add_fusion.place, bf16[4,2,112,3584]{3,2,1,0:T(8,128)(2,1)S(1)} %bitcast.29, bf16[8,112,128]{2,1,0:T(8,128)(2,1)S(1)} %all_to_all.50.refs_0_, bf16[8,112,128]{2,1,0:T(8,128)(2,1)S(1)} %collective-permute-done.4.refs_1_, ...), custom_call_target="tpu_custom_call" | custom-call | flops 822083584 | bytes 8388608 | tf_op jit(solution)/shard_map/pallas_call | solution.py:196
  75.7 5.7 %collective-permute-start.8 = (f32[4,112,128]{2,1,0:T(8,128)S(1)}, f32[4,112,128]{2,1,0:T(8,128)S(1)}, u32[]{:S(2)}, u32[]{:S(2)}) collective-permute-start(f32[4,112,128]{2,1,0:T(8,128)S(1)} %slice_bitcast_fusion.1), channel_id=1, source_target_pairs={{0,1},{1,0},{2,3},{3,2},{4,5},{5,4},{6,7},{7,6},{8,9},{9,8},{10,11... | collective-permute-start | bytes 688136 | tf_op jit(solution)/shard_map/ppermute | solution.py:122
  82.6 2.8 copy-done.2
  87.1 3.0 shard_map.43
  90.2 2.0 collective-permute-start.9
  92.2 2.8 copy-done.3
  95.0 3.0 shard_map.42
  99.2 3.5 all-to-all-start.1
  102.8 13.5 %all-to-all-done.1 = f32[4,112,512]{2,1,0:T(8,128)S(1)} async-done(((f32[4,112,512]{2,1,0:T(8,128)}), f32[4,112,512]{2,1,0:T(8,128)S(1)}, u32[]{:S(2)}, u32[]{:S(2)}) %all-to-all-start.1) | async-done | bytes 917536 | tf_op jit(solution)/shard_map/all_to_all | solution.py:130
  121.1 15.2 %all_to_all.51 = f32[16,16,512]{2,1,0:T(8,128)S(1)} all-to-all(f32[16,16,512]{2,1,0:T(8,128)S(1)} %bitcast.39), channel_id=1, replica_groups=mesh['z'=8,'y'=4,'x'=4,'core'=2] {'y','x'}, dimensions={0} | all-to-all | bytes 1048576 | tf_op jit(solution)/shard_map/all_to_all | solution.py:130
  136.4 12.9 %all_to_all.52 = f32[8,16,512]{2,1,0:T(8,128)S(1)} all-to-all(f32[8,16,512]{2,1,0:T(8,128)S(1)} %broadcast_in_dim.13), channel_id=1, replica_groups=mesh['z'=8,'y'=4,'x'=4,'core'=2] {'z'}, dimensions={0} | all-to-all | bytes 524288 | tf_op jit(solution)/shard_map/all_to_all | solution.py:130
  149.4 13.2 %all_to_all.53 = f32[16,16,512]{2,1,0:T(8,128)S(1)} all-to-all(f32[16,16,512]{2,1,0:T(8,128)S(1)} %broadcast_in_dim.14), channel_id=1, replica_groups=mesh['z'=8,'y'=4,'x'=4,'core'=2] {'y','x'}, dimensions={0} | all-to-all | bytes 1048576 | tf_op jit(solution)/shard_map/all_to_all | solution.py:130
  162.6 4.1 %collective-permute-start.11 = (f32[256,512]{1,0:T(8,128)S(1)}, f32[256,512]{1,0:T(8,128)}, u32[]{:S(2)}, u32[]{:S(2)}) collective-permute-start(f32[256,512]{1,0:T(8,128)S(1)} %bitcast.36), channel_id=1, source_target_pairs={{0,1},{1,0},{2,3},{3,2},{4,5},{5,4},{6,7},{7,6},{8,9},{9,8},{10,11... | collective-permute-start | bytes 1572872 | tf_op jit(solution)/shard_map/ppermute | solution.py:122
  169.6 20.3 %shard_map.44 = f32[512,512]{1,0:T(8,128)S(1)} custom-call(f32[512,512]{1,0:T(8,128)S(1)} %pad_maximum_fusion.gram_ref), custom_call_target="tpu_custom_call" | custom-call | flops 268435456 | bytes 2097152 | tf_op jit(solution)/shard_map/pallas_call | solution.py:108
  191.1 1.9 collective-permute-start.12
  193.0 9.0 %collective-permute-done.12 = bf16[112,512]{1,0:T(8,128)(2,1)S(1)} collective-permute-done((bf16[112,512]{1,0:T(8,128)(2,1)S(1)}, bf16[112,512]{1,0:T(8,128)(2,1)S(1)}, u32[]{:S(2)}, u32[]{:S(2)}) %collective-permute-start.12) | collective-permute-done | bytes 114720 | tf_op jit(solution)/shard_map/ppermute | solution.py:122
  202.1 4.7 %collective-permute-start.13 = (bf16[112,384]{1,0:T(8,128)(2,1)S(1)}, bf16[112,384]{1,0:T(8,128)(2,1)S(1)}, u32[]{:S(2)}, u32[]{:S(2)}) collective-permute-start(bf16[112,384]{1,0:T(8,128)(2,1)S(1)} %get-tuple-element.32), channel_id=1, source_target_pairs={{0,24},{1,25},{2,26},{3,27},{4,28},{5,29},{6,30},{7,31},{8,0},{9,1... | collective-permute-start | bytes 258056 | tf_op jit(solution)/shard_map/ppermute | solution.py:122
  208.6 3.7 collective-permute-done.14
  212.2 1.8 collective-permute-done.15
  214.9 17.3 %all_to_all.54.refs_0_ = bf16[8,112,128]{2,1,0:T(8,128)(2,1)S(1)} all-to-all(bf16[8,112,128]{2,1,0:T(8,128)(2,1)S(1)} %broadcast_in_dim.15), channel_id=1, replica_groups=mesh['z'=8,'y'=4,'x'=4,'core'=2] {'z'}, dimensions={0} | all-to-all | bytes 458752 | tf_op jit(solution)/shard_map/all_to_all | solution.py:130
  232.2 2.7 collective-permute-start.16
  234.9 3.8 %collective-permute-done.17.refs_3_ = bf16[8,112,128]{2,1,0:T(8,128)(2,1)S(1)} collective-permute-done((bf16[8,112,128]{2,1,0:T(8,128)(2,1)S(1)}, bf16[8,112,128]{2,1,0:T(8,128)(2,1)S(1)}, u32[]{:S(2)}, u32[]{:S(2)}) %collective-permute-start.17) | collective-permute-done | bytes 229408 | tf_op jit(solution)/shard_map/ppermute | solution.py:122
  238.8 2.7 collective-permute-start.19
  241.6 2.6 collective-permute-done.18
  244.2 2.9 copy-done.4
  247.1 4.6 %shard_map.45 = (f32[2,4,112,128]{3,2,1,0:T(8,128)S(1)}, bf16[8,4,112,128]{3,2,1,0:T(8,128)(2,1)S(1)}) custom-call(s32[2]{0:T(128)S(1)} %pad_add_fusion.place, bf16[4,2,112,3584]{3,2,1,0:T(8,128)(2,1)S(1)} %bitcast.32, bf16[8,112,128]{2,1,0:T(8,128)(2,1)S(1)} %all_to_all.54.refs_0_, bf16[8,112,128]{2,1,0:T(8,128)(2,1)S(1)} %collective-permute-done.16.refs_1_, ...), custom_call_target="tpu_custom_call" | custom-call | flops 822083584 | bytes 8388608 | tf_op jit(solution)/shard_map/pallas_call | solution.py:196
  251.7 5.5 %collective-permute-start.20 = (f32[4,112,128]{2,1,0:T(8,128)S(1)}, f32[4,112,128]{2,1,0:T(8,128)S(1)}, u32[]{:S(2)}, u32[]{:S(2)}) collective-permute-start(f32[4,112,128]{2,1,0:T(8,128)S(1)} %slice_bitcast_fusion), channel_id=1, source_target_pairs={{0,1},{1,0},{2,3},{3,2},{4,5},{5,4},{6,7},{7,6},{8,9},{9,8},{10,11... | collective-permute-start | bytes 688136 | tf_op jit(solution)/shard_map/ppermute | solution.py:122
  258.4 2.8 copy-done.5
  263.0 3.0 shard_map.47
  267.3 2.8 copy-done.6
  270.1 4.4 %shard_map.46 = (f32[4,112,384]{2,1,0:T(8,128)S(1)}, bf16[3584,512]{1,0:T(8,128)(2,1)}) custom-call(s32[1]{0:T(128)} %bitcast.1.place, bf16[4,2,112,3584]{3,2,1,0:T(8,128)(2,1)S(1)} %bitcast.34, bf16[3584,384]{1,0:T(8,128)(2,1)S(1)} %copy-done.8, bf16[3584,128]{1,0:T(8,128)(2,1)S(1)} %bitcast.35), custom_call_target="tpu_custom_call" | custom-call | flops 1233125376 | bytes 8388608 | tf_op jit(solution)/shard_map/pallas_call | solution.py:244
  274.7 16.2 %all_to_all.55 = f32[4,112,512]{2,1,0:T(8,128)S(1)} all-to-all(f32[4,112,512]{2,1,0:T(8,128)S(1)} %pad_maximum_fusion.3), channel_id=1, replica_groups=mesh['z'=8,'y'=4,'x'=4,'core'=2] {'x'}, dimensions={0} | all-to-all | bytes 1835008 | tf_op jit(solution)/shard_map/all_to_all | solution.py:130
  294.9 14.7 %all_to_all.56 = f32[16,16,512]{2,1,0:T(8,128)S(1)} all-to-all(f32[16,16,512]{2,1,0:T(8,128)S(1)} %bitcast.38), channel_id=1, replica_groups=mesh['z'=8,'y'=4,'x'=4,'core'=2] {'y','x'}, dimensions={0} | all-to-all | bytes 1048576 | tf_op jit(solution)/shard_map/all_to_all | solution.py:130
  309.6 12.5 %all_to_all.57 = f32[8,16,512]{2,1,0:T(8,128)S(1)} all-to-all(f32[8,16,512]{2,1,0:T(8,128)S(1)} %broadcast_in_dim.16), channel_id=1, replica_groups=mesh['z'=8,'y'=4,'x'=4,'core'=2] {'z'}, dimensions={0} | all-to-all | bytes 524288 | tf_op jit(solution)/shard_map/all_to_all | solution.py:130
  322.1 13.2 %all_to_all.58 = f32[16,16,512]{2,1,0:T(8,128)S(1)} all-to-all(f32[16,16,512]{2,1,0:T(8,128)S(1)} %broadcast_in_dim.17), channel_id=1, replica_groups=mesh['z'=8,'y'=4,'x'=4,'core'=2] {'y','x'}, dimensions={0} | all-to-all | bytes 1048576 | tf_op jit(solution)/shard_map/all_to_all | solution.py:130
  335.3 4.1 %collective-permute-start.23 = (f32[256,512]{1,0:T(8,128)S(1)}, f32[256,512]{1,0:T(8,128)S(1)}, u32[]{:S(2)}, u32[]{:S(2)}) collective-permute-start(f32[256,512]{1,0:T(8,128)S(1)} %bitcast.37), channel_id=1, source_target_pairs={{0,1},{1,0},{2,3},{3,2},{4,5},{5,4},{6,7},{7,6},{8,9},{9,8},{10,11... | collective-permute-start | bytes 1572872 | tf_op jit(solution)/shard_map/ppermute | solution.py:122
  341.2 20.3 %shard_map.48 = f32[512,512]{1,0:T(8,128)S(1)} custom-call(f32[512,512]{1,0:T(8,128)S(1)} %pad_maximum_fusion.1.gram_ref), custom_call_target="tpu_custom_call" | custom-call | flops 268435456 | bytes 2097152 | tf_op jit(solution)/shard_map/pallas_call | solution.py:108
  361.5 1.9 convolution_multiply_fusion
  (103 shorter events, 33.6 us)
Async XLA Ops:
  7.2 1.2 copy-start
  7.2 75.4 %all-gather.3.cloned.1.call-start = ((), (), s32[]{:S(2)}) async-start(), calls=%async_computation.10 | async-start | bytes 3096576 | tf_op jit(solution)/shard_map/all_gather | solution.py:169
  8.4 13.4 %collective-permute-start = (bf16[112,512]{1,0:T(8,128)(2,1)S(1)}, bf16[112,512]{1,0:T(8,128)(2,1)S(1)}, u32[]{:S(2)}, u32[]{:S(2)}) collective-permute-start(bf16[112,512]{1,0:T(8,128)(2,1)S(1)} %constant_dynamic-slice_fusion.2), channel_id=1, source_target_pairs={{0,0},{1,8},{2,16},{3,24},{4,32},{5,40},{6,48},{7,56},{8,64},{9,72... | collective-permute-start | bytes 344072 | tf_op jit(solution)/shard_map/ppermute | solution.py:122
  21.9 8.0 %collective-permute-start.1 = (bf16[112,384]{1,0:T(8,128)(2,1)S(1)}, bf16[112,384]{1,0:T(8,128)(2,1)S(1)}, u32[]{:S(2)}, u32[]{:S(2)}) collective-permute-start(bf16[112,384]{1,0:T(8,128)(2,1)S(1)} %get-tuple-element.34), channel_id=1, source_target_pairs={{0,24},{1,25},{2,26},{3,27},{4,28},{5,29},{6,30},{7,31},{8,0},{9,1... | collective-permute-start | bytes 258056 | tf_op jit(solution)/shard_map/ppermute | solution.py:122
  26.2 5.3 %collective-permute-start.2 = (bf16[112,384]{1,0:T(8,128)(2,1)S(1)}, bf16[112,384]{1,0:T(8,128)(2,1)S(1)}, u32[]{:S(2)}, u32[]{:S(2)}) collective-permute-start(bf16[112,384]{1,0:T(8,128)(2,1)S(1)} %get-tuple-element.34), channel_id=1, source_target_pairs={{0,16},{1,17},{2,18},{3,19},{4,20},{5,21},{6,22},{7,23},{8,24},{9,... | collective-permute-start | bytes 258056 | tf_op jit(solution)/shard_map/ppermute | solution.py:122
  27.6 6.5 %collective-permute-start.3 = (bf16[112,384]{1,0:T(8,128)(2,1)S(1)}, bf16[112,384]{1,0:T(8,128)(2,1)S(1)}, u32[]{:S(2)}, u32[]{:S(2)}) collective-permute-start(bf16[112,384]{1,0:T(8,128)(2,1)S(1)} %get-tuple-element.34), channel_id=1, source_target_pairs={{0,8},{1,9},{2,10},{3,11},{4,12},{5,13},{6,14},{7,15},{8,16},{9,17... | collective-permute-start | bytes 258056 | tf_op jit(solution)/shard_map/ppermute | solution.py:122
  34.1 0.7 copy-start.12
  55.2 6.5 %collective-permute-start.5 = (bf16[8,112,128]{2,1,0:T(8,128)(2,1)S(1)}, bf16[8,112,128]{2,1,0:T(8,128)(2,1)S(1)}, u32[]{:S(2)}, u32[]{:S(2)}) collective-permute-start(bf16[8,112,128]{2,1,0:T(8,128)(2,1)S(1)} %all_to_all.50.refs_0_), channel_id=1, source_target_pairs={{0,8},{1,9},{2,10},{3,11},{4,12},{5,13},{6,14},{7,15},{8,16},{9,17... | collective-permute-start | bytes 688136 | tf_op jit(solution)/shard_map/ppermute | solution.py:122
  55.2 6.6 %collective-permute-start.4 = (bf16[8,112,128]{2,1,0:T(8,128)(2,1)S(1)}, bf16[8,112,128]{2,1,0:T(8,128)(2,1)S(1)}, u32[]{:S(2)}, u32[]{:S(2)}) collective-permute-start(bf16[8,112,128]{2,1,0:T(8,128)(2,1)S(1)} %all_to_all.50.refs_0_), channel_id=1, source_target_pairs={{0,24},{1,25},{2,26},{3,27},{4,28},{5,29},{6,30},{7,31},{8,0},{9,1... | collective-permute-start | bytes 688136 | tf_op jit(solution)/shard_map/ppermute | solution.py:122
  61.7 5.5 %collective-permute-start.6 = (bf16[4,112,128]{2,1,0:T(8,128)(2,1)S(1)}, bf16[4,112,128]{2,1,0:T(8,128)(2,1)S(1)}, u32[]{:S(2)}, u32[]{:S(2)}) collective-permute-start(bf16[4,112,128]{2,1,0:T(8,128)(2,1)S(1)} %slice.50), channel_id=1, source_target_pairs={{0,8},{1,9},{2,10},{3,11},{4,12},{5,13},{6,14},{7,15},{8,16},{9,17... | collective-permute-start | bytes 344072 | tf_op jit(solution)/shard_map/ppermute | solution.py:122
  61.8 5.4 %collective-permute-start.7 = (bf16[4,112,128]{2,1,0:T(8,128)(2,1)S(1)}, bf16[4,112,128]{2,1,0:T(8,128)(2,1)S(1)}, u32[]{:S(2)}, u32[]{:S(2)}) collective-permute-start(bf16[4,112,128]{2,1,0:T(8,128)(2,1)S(1)} %slice.51), channel_id=1, source_target_pairs={{0,24},{1,25},{2,26},{3,27},{4,28},{5,29},{6,30},{7,31},{8,0},{9,1... | collective-permute-start | bytes 344072 | tf_op jit(solution)/shard_map/ppermute | solution.py:122
  67.2 2.9 copy-start.1
  75.7 6.8 %collective-permute-start.8 = (f32[4,112,128]{2,1,0:T(8,128)S(1)}, f32[4,112,128]{2,1,0:T(8,128)S(1)}, u32[]{:S(2)}, u32[]{:S(2)}) collective-permute-start(f32[4,112,128]{2,1,0:T(8,128)S(1)} %slice_bitcast_fusion.1), channel_id=1, source_target_pairs={{0,1},{1,0},{2,3},{3,2},{4,5},{5,4},{6,7},{7,6},{8,9},{9,8},{10,11... | collective-permute-start | bytes 688136 | tf_op jit(solution)/shard_map/ppermute | solution.py:122
  82.5 2.8 copy-start.2
  85.4 1.8 copy-start.9
  87.1 5.1 %copy-start.10 = (bf16[3584,384]{1,0:T(8,128)(2,1)S(1)}, bf16[3584,384]{1,0:T(8,128)(2,1)}, u32[]{:S(2)}) copy-start(bf16[3584,384]{1,0:T(8,128)(2,1)} %all-gather.3.cloned.1.call-done.b_ref) | copy-start | bytes 8257540
  90.2 7.9 %collective-permute-start.9 = (f32[4,112,384]{2,1,0:T(8,128)S(1)}, f32[4,112,384]{2,1,0:T(8,128)S(1)}, u32[]{:S(2)}, u32[]{:S(2)}) collective-permute-start(f32[4,112,384]{2,1,0:T(8,128)S(1)} %shard_map.43), channel_id=1, source_target_pairs={{0,1},{1,0},{2,3},{3,2},{4,5},{5,4},{6,7},{7,6},{8,9},{9,8},{10,11... | collective-permute-start | bytes 2064392 | tf_op jit(solution)/shard_map/ppermute | solution.py:122
  92.2 2.8 copy-start.3
  99.2 17.0 %all-to-all-start.1 = ((f32[4,112,512]{2,1,0:T(8,128)}), f32[4,112,512]{2,1,0:T(8,128)S(1)}, u32[]{:S(2)}, u32[]{:S(2)}) async-start(f32[4,112,512]{2,1,0:T(8,128)} %pad_maximum_fusion.2), calls=%async_computation.1 | async-start | bytes 1835008 | tf_op jit(solution)/shard_map/all_to_all | solution.py:130
  102.7 155.7 %all-gather.5.cloned.1.call-start = ((), (), s32[]{:S(2)}) async-start(), calls=%async_computation.11 | async-start | bytes 3096576 | tf_op jit(solution)/shard_map/all_gather | solution.py:169
  118.2 2.9 collective-permute-start.10
  162.6 5.8 %collective-permute-start.11 = (f32[256,512]{1,0:T(8,128)S(1)}, f32[256,512]{1,0:T(8,128)}, u32[]{:S(2)}, u32[]{:S(2)}) collective-permute-start(f32[256,512]{1,0:T(8,128)S(1)} %bitcast.36), channel_id=1, source_target_pairs={{0,1},{1,0},{2,3},{3,2},{4,5},{5,4},{6,7},{7,6},{8,9},{9,8},{10,11... | collective-permute-start | bytes 1572872 | tf_op jit(solution)/shard_map/ppermute | solution.py:122
  191.1 11.0 %collective-permute-start.12 = (bf16[112,512]{1,0:T(8,128)(2,1)S(1)}, bf16[112,512]{1,0:T(8,128)(2,1)S(1)}, u32[]{:S(2)}, u32[]{:S(2)}) collective-permute-start(bf16[112,512]{1,0:T(8,128)(2,1)S(1)} %fusion), channel_id=1, source_target_pairs={{0,0},{1,8},{2,16},{3,24},{4,32},{5,40},{6,48},{7,56},{8,64},{9,72... | collective-permute-start | bytes 344072 | tf_op jit(solution)/shard_map/ppermute | solution.py:122
  202.1 6.4 %collective-permute-start.13 = (bf16[112,384]{1,0:T(8,128)(2,1)S(1)}, bf16[112,384]{1,0:T(8,128)(2,1)S(1)}, u32[]{:S(2)}, u32[]{:S(2)}) collective-permute-start(bf16[112,384]{1,0:T(8,128)(2,1)S(1)} %get-tuple-element.32), channel_id=1, source_target_pairs={{0,24},{1,25},{2,26},{3,27},{4,28},{5,29},{6,30},{7,31},{8,0},{9,1... | collective-permute-start | bytes 258056 | tf_op jit(solution)/shard_map/ppermute | solution.py:122
  206.9 5.3 %collective-permute-start.14 = (bf16[112,384]{1,0:T(8,128)(2,1)S(1)}, bf16[112,384]{1,0:T(8,128)(2,1)S(1)}, u32[]{:S(2)}, u32[]{:S(2)}) collective-permute-start(bf16[112,384]{1,0:T(8,128)(2,1)S(1)} %get-tuple-element.32), channel_id=1, source_target_pairs={{0,16},{1,17},{2,18},{3,19},{4,20},{5,21},{6,22},{7,23},{8,24},{9,... | collective-permute-start | bytes 258056 | tf_op jit(solution)/shard_map/ppermute | solution.py:122
  207.8 6.3 %collective-permute-start.15 = (bf16[112,384]{1,0:T(8,128)(2,1)S(1)}, bf16[112,384]{1,0:T(8,128)(2,1)S(1)}, u32[]{:S(2)}, u32[]{:S(2)}) collective-permute-start(bf16[112,384]{1,0:T(8,128)(2,1)S(1)} %get-tuple-element.32), channel_id=1, source_target_pairs={{0,8},{1,9},{2,10},{3,11},{4,12},{5,13},{6,14},{7,15},{8,16},{9,17... | collective-permute-start | bytes 258056 | tf_op jit(solution)/shard_map/ppermute | solution.py:122
  214.1 0.7 copy-start.11
  232.2 6.5 %collective-permute-start.17 = (bf16[8,112,128]{2,1,0:T(8,128)(2,1)S(1)}, bf16[8,112,128]{2,1,0:T(8,128)(2,1)S(1)}, u32[]{:S(2)}, u32[]{:S(2)}) collective-permute-start(bf16[8,112,128]{2,1,0:T(8,128)(2,1)S(1)} %all_to_all.54.refs_0_), channel_id=1, source_target_pairs={{0,8},{1,9},{2,10},{3,11},{4,12},{5,13},{6,14},{7,15},{8,16},{9,17... | collective-permute-start | bytes 688136 | tf_op jit(solution)/shard_map/ppermute | solution.py:122
  232.2 6.6 %collective-permute-start.16 = (bf16[8,112,128]{2,1,0:T(8,128)(2,1)S(1)}, bf16[8,112,128]{2,1,0:T(8,128)(2,1)S(1)}, u32[]{:S(2)}, u32[]{:S(2)}) collective-permute-start(bf16[8,112,128]{2,1,0:T(8,128)(2,1)S(1)} %all_to_all.54.refs_0_), channel_id=1, source_target_pairs={{0,24},{1,25},{2,26},{3,27},{4,28},{5,29},{6,30},{7,31},{8,0},{9,1... | collective-permute-start | bytes 688136 | tf_op jit(solution)/shard_map/ppermute | solution.py:122
  238.7 5.5 %collective-permute-start.18 = (bf16[4,112,128]{2,1,0:T(8,128)(2,1)S(1)}, bf16[4,112,128]{2,1,0:T(8,128)(2,1)S(1)}, u32[]{:S(2)}, u32[]{:S(2)}) collective-permute-start(bf16[4,112,128]{2,1,0:T(8,128)(2,1)S(1)} %slice.54), channel_id=1, source_target_pairs={{0,8},{1,9},{2,10},{3,11},{4,12},{5,13},{6,14},{7,15},{8,16},{9,17... | collective-permute-start | bytes 344072 | tf_op jit(solution)/shard_map/ppermute | solution.py:122
  238.8 5.4 %collective-permute-start.19 = (bf16[4,112,128]{2,1,0:T(8,128)(2,1)S(1)}, bf16[4,112,128]{2,1,0:T(8,128)(2,1)S(1)}, u32[]{:S(2)}, u32[]{:S(2)}) collective-permute-start(bf16[4,112,128]{2,1,0:T(8,128)(2,1)S(1)} %slice.55), channel_id=1, source_target_pairs={{0,24},{1,25},{2,26},{3,27},{4,28},{5,29},{6,30},{7,31},{8,0},{9,1... | collective-permute-start | bytes 344072 | tf_op jit(solution)/shard_map/ppermute | solution.py:122
  244.2 2.9 copy-start.4
  251.7 6.6 %collective-permute-start.20 = (f32[4,112,128]{2,1,0:T(8,128)S(1)}, f32[4,112,128]{2,1,0:T(8,128)S(1)}, u32[]{:S(2)}, u32[]{:S(2)}) collective-permute-start(f32[4,112,128]{2,1,0:T(8,128)S(1)} %slice_bitcast_fusion), channel_id=1, source_target_pairs={{0,1},{1,0},{2,3},{3,2},{4,5},{5,4},{6,7},{7,6},{8,9},{9,8},{10,11... | collective-permute-start | bytes 688136 | tf_op jit(solution)/shard_map/ppermute | solution.py:122
  258.4 2.8 copy-start.5
  261.3 1.8 copy-start.7
  263.0 4.3 %copy-start.8 = (bf16[3584,384]{1,0:T(8,128)(2,1)S(1)}, bf16[3584,384]{1,0:T(8,128)(2,1)}, u32[]{:S(2)}) copy-start(bf16[3584,384]{1,0:T(8,128)(2,1)} %all-gather.5.cloned.1.call-done.b_ref) | copy-start | bytes 8257540
  266.1 8.4 %collective-permute-start.21 = (f32[4,112,384]{2,1,0:T(8,128)S(1)}, f32[4,112,384]{2,1,0:T(8,128)S(1)}, u32[]{:S(2)}, u32[]{:S(2)}) collective-permute-start(f32[4,112,384]{2,1,0:T(8,128)S(1)} %shard_map.47), channel_id=1, source_target_pairs={{0,1},{1,0},{2,3},{3,2},{4,5},{5,4},{6,7},{7,6},{8,9},{9,8},{10,11... | collective-permute-start | bytes 2064392 | tf_op jit(solution)/shard_map/ppermute | solution.py:122
  267.3 2.8 copy-start.6
  292.0 2.7 collective-permute-start.22
  335.3 5.6 %collective-permute-start.23 = (f32[256,512]{1,0:T(8,128)S(1)}, f32[256,512]{1,0:T(8,128)S(1)}, u32[]{:S(2)}, u32[]{:S(2)}) collective-permute-start(f32[256,512]{1,0:T(8,128)S(1)} %bitcast.37), channel_id=1, source_target_pairs={{0,1},{1,0},{2,3},{3,2},{4,5},{5,4},{6,7},{7,6},{8,9},{9,8},{10,11... | collective-permute-start | bytes 1572872 | tf_op jit(solution)/shard_map/ppermute | solution.py:122
Sparse Core Ops, SparseCore 0:
  35.0 46.8 all-gather.2
  215.0 42.0 all-gather.4

commit v3 on v2

--- a/solution.py
+++ b/solution.py
@@ -80,8 +80,28 @@
     return lax.broadcasted_iota(jnp.int32, (n, n), 0) == lax.broadcasted_iota(jnp.int32, (n, n), 1)
 
 
-def chol_inverse(gram_ref, out_ref, work):
-    gram = gram_ref[...]
+def halves():
+    lower = [(i, j) for i in range(K // B) for j in range(i + 1)]
+    return lower[:5], lower[5:]
+
+
+def gram_step(place, parts_ref, sum_ref, packed_ref):
+    total = (parts_ref[0] + parts_ref[1]) + (parts_ref[2] + parts_ref[3])
+    sum_ref[...] = total
+    for half, blocks in enumerate(halves()):
+        slot = jnp.where(place[0] == half, 1, 0)
+        for at, (i, j) in enumerate(blocks):
+            packed_ref[slot, at] = dot(total[:, B * i:B * i + B], total[:, B * j:B * j + B], 0, 0)
+
+
+def chol_inverse(place, own_ref, came_ref, out_ref, work):
+    for half, blocks in enumerate(halves()):
+        for at, (i, j) in enumerate(blocks):
+            entry = jnp.where(place[0] == half, own_ref[at], came_ref[at])
+            work[B * i:B * i + B, B * j:B * j + B] = entry
+            if i != j:
+                work[B * j:B * j + B, B * i:B * i + B] = entry.T
+    gram = work[...]
     diagonal = jnp.where(unit(K), gram, 0.0)
     along = lax.rsqrt(jnp.sum(diagonal, axis=0, keepdims=True))
     work[...] = gram * along * lax.rsqrt(jnp.sum(diagonal, axis=1, keepdims=True))
@@ -104,16 +124,39 @@
     lax.fori_loop(0, K // B, block, 0)
 
 
-def inverse_factor(gram):
+VMEM = pl.BlockSpec(memory_space=pltpu.VMEM)
+SMEM = pl.BlockSpec(memory_space=pltpu.SMEM)
+HBM = pl.BlockSpec(memory_space=pl.ANY)
+
+
+def core_place():
+    return lax.axis_index("core").astype(jnp.int32).reshape(1)
+
+
+def summed_gram(place, parts):
+    return pl.pallas_call(
+        gram_step,
+        out_shape=[
+            jax.ShapeDtypeStruct((ROWS, K), jnp.float32),
+            jax.ShapeDtypeStruct((2, 5, B, B), jnp.float32),
+        ],
+        in_specs=[SMEM, VMEM],
+        out_specs=[VMEM, VMEM],
+        compiler_params=pltpu.CompilerParams(vmem_limit_bytes=12 * 1024 * 1024),
+        cost_estimate=pl.CostEstimate(flops=2 * ROWS * K * K, bytes_accessed=8 * K * K, transcendentals=0),
+    )(place, parts)
+
+
+def inverse_factor(place, own, came):
     return pl.pallas_call(
         chol_inverse,
         out_shape=jax.ShapeDtypeStruct((K, K), jnp.float32),
-        in_specs=[pl.BlockSpec(memory_space=pltpu.VMEM)],
-        out_specs=pl.BlockSpec(memory_space=pltpu.VMEM),
+        in_specs=[SMEM, VMEM, VMEM],
+        out_specs=VMEM,
         scratch_shapes=[pltpu.VMEM((K, K), jnp.float32)],
         compiler_params=pltpu.CompilerParams(vmem_limit_bytes=12 * 1024 * 1024),
         cost_estimate=pl.CostEstimate(flops=2 * K ** 3, bytes_accessed=8 * K * K, transcendentals=0),
-    )(gram)
+    )(place, own, came)
 
 
 def permute(values, where):
@@ -216,79 +259,98 @@
 
 
 def many_step(place, a_ref, b_ref, *refs):
-    step = pl.program_id(0)
-    a = a_ref[...].reshape(4 * ROWS, 8 * ROWS)
-    out_ref = refs[-1]
-    if len(refs) > 1:
-        few_ref, out_ref, rows_ref = refs
-        rows_ref[:, :FEW] = few_ref[...]
-        rows_ref[:, FEW:] = b_ref[...]
-    term = jnp.dot(a, b_ref[...], preferred_element_type=jnp.float32).reshape(out_ref.shape)
-
-    @pl.when(step == 0)
-    def _():
-        out_ref[...] = term
-
-    @pl.when(step > 0)
-    def _():
-        out_ref[...] += term
-
-
-def product_many(factor, many, core, few=None):
-    operands = [many] if few is None else [many, few]
-    out_shape = [jax.ShapeDtypeStruct((4, ROWS, K - FEW), jnp.float32)]
-    out_specs = [pl.BlockSpec((4, ROWS, K - FEW), lambda q, place: (0, 0, 0))]
-    if few is not None:
-        out_shape.append(jax.ShapeDtypeStruct((32 * ROWS, K), jnp.bfloat16))
-        out_specs.append(pl.BlockSpec((8 * ROWS, K), lambda q, place: (q, 0)))
+    few_ref = rows_ref = None
+    if len(refs) > 8:
+        few_ref, theirs_ref, mine_ref, rows_ref = refs[:4]
+    else:
+        theirs_ref, mine_ref = refs[:2]
+    a_held, b_held, total, a_sem, b_sem, rows_sem = refs[-6:]
+    steps, deep = a_held.shape[0], a_held.shape[2]
+    inward = [
+        (
+            pltpu.make_async_copy(a_ref.at[:, pl.ds(q * deep, deep)], a_held.at[q], a_sem.at[q]),
+            pltpu.make_async_copy(b_ref.at[pl.ds(q * deep, deep)], b_held.at[q], b_sem.at[q]),
+        )
+        for q in range(steps)
+    ]
+    outward = []
+
+    def start(copies):
+        for copy in copies:
+            copy.start()
+
+    for q in range(steps):
+        start(inward[q])
+    if rows_ref is not None:
+        outward.append(pltpu.make_async_copy(few_ref, rows_ref.at[:, pl.ds(0, FEW)], rows_sem.at[steps]))
+        start(outward)
+    for q in range(steps):
+        for copy in inward[q]:
+            copy.wait()
+        if rows_ref is not None:
+            outward.append(pltpu.make_async_copy(
+                b_held.at[q], rows_ref.at[pl.ds(q * deep, deep), pl.ds(FEW, K - FEW)], rows_sem.at[q]))
+            start(outward[-1:])
+        term = jnp.dot(a_held[q], b_held[q], preferred_element_type=jnp.float32).reshape(total.shape)
+        if q == 0:
+            total[...] = term
+        else:
+            total[...] += term
+    theirs_ref[...] = total[:, 1 - place[0]]
+    mine_ref[...] = total[:, place[0]]
+    for copy in outward:
+        copy.wait()
+
+
+def product_many(factor, many, place, few=None):
+    steps = 7
+    deep = 32 * ROWS // steps
+    operands = [factor, many] if few is None else [factor, many, few]
+    part = jax.ShapeDtypeStruct((4, ROWS, K - FEW), jnp.float32)
     return pl.pallas_call(
         many_step,
-        out_shape=out_shape,
-        grid_spec=pltpu.PrefetchScalarGridSpec(
-            num_scalar_prefetch=1,
-            grid=(4,),
-            in_specs=[pl.BlockSpec((4, None, ROWS, 8 * ROWS), lambda q, place: (0, place[0], 0, q))]
-            + [pl.BlockSpec((8 * ROWS, operand.shape[1]), lambda q, place: (q, 0)) for operand in operands],
-            out_specs=out_specs,
-        ),
-        compiler_params=pltpu.CompilerParams(vmem_limit_bytes=16 * 1024 * 1024),
-        cost_estimate=pl.CostEstimate(flops=2 * 4 * ROWS * M // 8 * (K - FEW), bytes_accessed=8 * 1024 * 1024, transcendentals=0),
-    )(core.astype(jnp.int32).reshape(1), factor.reshape(4, 2, ROWS, 32 * ROWS), *operands)
+        out_shape=[part, part] + [jax.ShapeDtypeStruct((32 * ROWS, K), jnp.bfloat16)] * (len(operands) - 2),
+        in_specs=[SMEM, HBM, HBM] + [VMEM] * (len(operands) - 2),
+        out_specs=[VMEM, VMEM] + [HBM] * (len(operands) - 2),
+        scratch_shapes=[
+            pltpu.VMEM((steps, 8 * ROWS, deep), jnp.bfloat16),
+            pltpu.VMEM((steps, deep, K - FEW), jnp.bfloat16),
+            pltpu.VMEM((4, 2, ROWS, K - FEW), jnp.float32),
+            pltpu.SemaphoreType.DMA((steps,)),
+            pltpu.SemaphoreType.DMA((steps,)),
+            pltpu.SemaphoreType.DMA((steps + 1,)),
+        ],
+        compiler_params=pltpu.CompilerParams(vmem_limit_bytes=60 * 1024 * 1024),
+        cost_estimate=pl.CostEstimate(flops=2 * 8 * ROWS * M // 8 * (K - FEW), bytes_accessed=12 * 1024 * 1024, transcendentals=0),
+    )(place, *operands)
 
 
 def summed_product(factor, rows, keep):
-    core = lax.axis_index("core")
+    place = core_place()
     many, pieces = gathered_rows(rows)
     both, ordered = product_few(factor, pieces)
     few = both[1] + permute(both[0], other_core)
     many, few = lax.optimization_barrier((many, few))
-    came = permute(product_many(factor, many, 1 - core)[0], other_core)
-    mine = product_many(factor, many, core, ordered.reshape(32 * ROWS, FEW) if keep else None)
-    total = jnp.concatenate([few, mine[0] + came], axis=2)
-    return jnp.sum(exchange(total, "x"), axis=0), mine[-1]
-
-
-def gram_inverse(values):
-    gram = dot(values, values, 0, 0)
-    core = lax.axis_index("core")
-    half = lambda which: lax.dynamic_slice_in_dim(gram, which * HALF, HALF, 0)
-    share = half(core) + permute(half(1 - core), other_core)
-    share = jnp.sum(exchange(share.reshape(16, HALF // 16, K), ("y", "x")), axis=0)
+    theirs, mine, *rest = product_many(factor, many, place, ordered.reshape(32 * ROWS, FEW) if keep else None)
+    total = jnp.concatenate([few, mine + permute(theirs, other_core)], axis=2)
+    return summed_gram(place, exchange(total, "x")), rest
+
+
+def gram_inverse(packed):
+    share = packed[1] + permute(packed[0], other_core)
+    share = jnp.sum(exchange(share.reshape(16, 5 * B // 16, B), ("y", "x")), axis=0)
     share = jnp.sum(exchange(copies(share, "z"), "z"), axis=0)
-    share = exchange(copies(share, ("y", "x")), ("y", "x")).reshape(HALF, K)
-    came = permute(share, other_core)
-    first = jnp.where(core == 0, share, came)
-    second = jnp.where(core == 0, came, share)
-    return inverse_factor(jnp.concatenate([first, second], axis=0))
+    share = exchange(copies(share, ("y", "x")), ("y", "x")).reshape(5, B, B)
+    return inverse_factor(core_place(), share, permute(share, other_core))
 
 
 def shards(factor, basis):
     scale = math.sqrt(M)
     own = lax.dynamic_slice_in_dim(basis, lax.axis_index(("x", "core")) * ROWS, ROWS, 0)
-    first, _ = summed_product(factor, own, False)
-    middle = (dot(first, gram_inverse(first), 1, 1) * scale).astype(jnp.bfloat16)
-    second, column_basis = summed_product(factor, middle, True)
-    return dot(second, gram_inverse(second), 1, 1) * scale, column_basis
+    (first, packed), _ = summed_product(factor, own, False)
+    middle = (dot(first, gram_inverse(packed), 1, 1) * scale).astype(jnp.bfloat16)
+    (second, packed), (column_basis,) = summed_product(factor, middle, True)
+    return dot(second, gram_inverse(packed), 1, 1) * scale, column_basis
 
 
 def solution(mesh):

time: 371 us -> 347 us (0.935)
  local copies, waits for them, and re-layouts: 24.6 us -> 9.81 us
  waiting for transfers between devices: 64.1 us -> 53.2 us
  blocking collectives: 135 us -> 141 us
  starting transfers between devices: 58.9 us -> 55.1 us
    unnamed x26 -> x12, local copies, waits for them, and re-layouts: 23.2 us -> 9.31 us
    all_to_all x1 -> x0, waiting for transfers between devices: 13.5 us -> none  [exchange(): return lax.all_to_all(pieces, axes, 0, 0, tiled=True)]
    all_to_all x9 -> x10, blocking collectives: 135 us -> 141 us  [exchange(): return lax.all_to_all(pieces, axes, 0, 0, tiled=True)]
  transfers between devices with their start and end apart: 27 -> 26, of which waited for: 18 -> 19; matrix products, arithmetic and copies ran while one was open for 0% -> 0% of each run, Pallas kernels for 5% -> 3%
where the time goes in v3:
time: 347 us; the launch traced here: 346 us
  blocking collectives  141 us (41%)
  Pallas kernels  66.8 us (19%)
  starting transfers between devices  55.1 us (16%)
  waiting for transfers between devices  53.2 us (15%)
  between operations  14.4 us (4%)
  local copies, waits for them, and re-layouts  9.81 us (3%)
    all_to_all x10, blocking collectives, exchange(): return lax.all_to_all(pieces, axes, 0, 0, tiled=True)  141 us
    ppermute x24, starting transfers between devices, permute(): lax.ppermute(values, AXES, [(index[p], index[where(*p)]) for p in places])  55 us
    ppermute x24, waiting for transfers between devices, permute(): lax.ppermute(values, AXES, [(index[p], index[where(*p)]) for p in places])  53.1 us
    pallas_call x2, Pallas kernels, inverse_factor(): pl.pallas_call(chol_inverse, out_shape=jax.ShapeDtypeStruct((K, K), jnp.f...  40.9 us
    pallas_call x2, Pallas kernels, product_many(): pl.pallas_call(many_step, out_shape=[part, part] + [jax.ShapeDtypeStruct(...  14.3 us
    pallas_call x2, Pallas kernels, product_few(): pl.pallas_call(few_step, out_shape=[jax.ShapeDtypeStruct((2, 4, ROWS, FEW...  10.1 us
    unnamed x12, local copies, waits for them, and re-layouts  9.31 us
  transfers between devices with their start and end apart: 26, of which 19 were waited for; matrix products, arithmetic and copies ran while one was open for 0% of the time, Pallas kernels for 3%

profile of v3, /device:TPU:1, one launch (start us, length us, event | category | flops | bytes accessed | tf_op | source)
XLA Modules:
  0.0 346.2 jit_solution(7955005368258102740)
XLA Ops:
  8.4 4.6 %collective-permute-start = (bf16[112,512]{1,0:T(8,128)(2,1)S(1)}, bf16[112,512]{1,0:T(8,128)(2,1)S(1)}, u32[]{:S(2)}, u32[]{:S(2)}) collective-permute-start(bf16[112,512]{1,0:T(8,128)(2,1)S(1)} %constant_dynamic-slice_fusion), channel_id=1, source_target_pairs={{0,0},{1,8},{2,16},{3,24},{4,32},{5,40},{6,48},{7,56},{8,64},{9,72... | collective-permute-start | bytes 344072 | tf_op jit(solution)/shard_map/ppermute | solution.py:165
  13.0 8.8 %collective-permute-done = bf16[112,512]{1,0:T(8,128)(2,1)S(1)} collective-permute-done((bf16[112,512]{1,0:T(8,128)(2,1)S(1)}, bf16[112,512]{1,0:T(8,128)(2,1)S(1)}, u32[]{:S(2)}, u32[]{:S(2)}) %collective-permute-start) | collective-permute-done | bytes 114720 | tf_op jit(solution)/shard_map/ppermute | solution.py:165
  21.9 4.4 %collective-permute-start.1 = (bf16[112,384]{1,0:T(8,128)(2,1)S(1)}, bf16[112,384]{1,0:T(8,128)(2,1)S(1)}, u32[]{:S(2)}, u32[]{:S(2)}) collective-permute-start(bf16[112,384]{1,0:T(8,128)(2,1)S(1)} %get-tuple-element.44), channel_id=1, source_target_pairs={{0,24},{1,25},{2,26},{3,27},{4,28},{5,29},{6,30},{7,31},{8,0},{9,1... | collective-permute-start | bytes 258056 | tf_op jit(solution)/shard_map/ppermute | solution.py:165
  26.2 1.4 collective-permute-start.2
  28.3 1.5 collective-permute-done.1
  29.9 1.7 collective-permute-done.2
  31.6 2.5 collective-permute-done.3
  35.0 20.3 %all_to_all.50.refs_0_ = bf16[8,112,128]{2,1,0:T(8,128)(2,1)S(1)} all-to-all(bf16[8,112,128]{2,1,0:T(8,128)(2,1)S(1)} %broadcast_in_dim.12), channel_id=1, replica_groups=mesh['z'=8,'y'=4,'x'=4,'core'=2] {'z'}, dimensions={0} | all-to-all | bytes 458752 | tf_op jit(solution)/shard_map/all_to_all | solution.py:173
  55.2 2.7 collective-permute-start.4
  57.9 3.8 %collective-permute-done.5.refs_3_ = bf16[8,112,128]{2,1,0:T(8,128)(2,1)S(1)} collective-permute-done((bf16[8,112,128]{2,1,0:T(8,128)(2,1)S(1)}, bf16[8,112,128]{2,1,0:T(8,128)(2,1)S(1)}, u32[]{:S(2)}, u32[]{:S(2)}) %collective-permute-start.5) | collective-permute-done | bytes 229408 | tf_op jit(solution)/shard_map/ppermute | solution.py:165
  61.9 2.7 collective-permute-start.7
  64.7 2.6 collective-permute-done.6
  67.3 2.9 copy-done.1
  70.2 5.5 %shard_map.41 = (f32[2,4,112,128]{3,2,1,0:T(8,128)S(1)}, bf16[8,4,112,128]{3,2,1,0:T(8,128)(2,1)}) custom-call(s32[2]{0:T(128)S(1)} %pad_add_fusion.place, bf16[4,2,112,3584]{3,2,1,0:T(8,128)(2,1)S(1)} %bitcast.28, bf16[8,112,128]{2,1,0:T(8,128)(2,1)S(1)} %all_to_all.50.refs_0_, bf16[8,112,128]{2,1,0:T(8,128)(2,1)S(1)} %collective-permute-done.4.refs_1_, ...), custom_call_target="tpu_custom_call" | custom-call | flops 822083584 | bytes 8388608 | tf_op jit(solution)/shard_map/pallas_call | solution.py:239
  75.7 5.9 %collective-permute-start.8 = (f32[4,112,128]{2,1,0:T(8,128)S(1)}, f32[4,112,128]{2,1,0:T(8,128)S(1)}, u32[]{:S(2)}, u32[]{:S(2)}) collective-permute-start(f32[4,112,128]{2,1,0:T(8,128)S(1)} %slice_bitcast_fusion.3), channel_id=1, source_target_pairs={{0,1},{1,0},{2,3},{3,2},{4,5},{5,4},{6,7},{7,6},{8,9},{9,8},{10,11... | collective-permute-start | bytes 688136 | tf_op jit(solution)/shard_map/ppermute | solution.py:165
  82.8 6.4 %shard_map.42 = (f32[4,112,384]{2,1,0:T(8,128)}, f32[4,112,384]{2,1,0:T(8,128)}) custom-call(s32[1]{0:T(128)} %bitcast.place, bf16[896,3584]{1,0:T(8,128)(2,1)} %a_ref.3, bf16[3584,384]{1,0:T(8,128)(2,1)} %all-gather.3.cloned.1.call-done.b_ref), custom_call_target="tpu_custom_call" | custom-call | flops 2466250752 | bytes 12582912 | tf_op jit(solution)/shard_map/pallas_call | solution.py:310
  89.1 1.9 collective-permute-start.9
  91.0 2.0 collective-permute-done.9
  94.3 16.1 %all_to_all.51.parts_ref = f32[4,112,512]{2,1,0:T(8,128)S(1)} all-to-all(f32[4,112,512]{2,1,0:T(8,128)S(1)} %pad_maximum_fusion), channel_id=1, replica_groups=mesh['z'=8,'y'=4,'x'=4,'core'=2] {'x'}, dimensions={0} | all-to-all | bytes 1835008 | tf_op jit(solution)/shard_map/all_to_all | solution.py:173
  111.1 1.9 collective-permute-start.10
  114.3 13.3 %all_to_all.52 = f32[16,40,128]{2,1,0:T(8,128)S(1)} all-to-all(f32[16,40,128]{2,1,0:T(8,128)S(1)} %bitcast.35), channel_id=1, replica_groups=mesh['z'=8,'y'=4,'x'=4,'core'=2] {'y','x'}, dimensions={0} | all-to-all | bytes 655360 | tf_op jit(solution)/shard_map/all_to_all | solution.py:173
  127.7 12.0 %all_to_all.53 = f32[8,40,128]{2,1,0:T(8,128)S(1)} all-to-all(f32[8,40,128]{2,1,0:T(8,128)S(1)} %broadcast_in_dim.13), channel_id=1, replica_groups=mesh['z'=8,'y'=4,'x'=4,'core'=2] {'z'}, dimensions={0} | all-to-all | bytes 327680 | tf_op jit(solution)/shard_map/all_to_all | solution.py:173
  139.7 10.9 %all_to_all.54 = f32[16,40,128]{2,1,0:T(8,128)S(1)} all-to-all(f32[16,40,128]{2,1,0:T(8,128)S(1)} %broadcast_in_dim.14), channel_id=1, replica_groups=mesh['z'=8,'y'=4,'x'=4,'core'=2] {'y','x'}, dimensions={0} | all-to-all | bytes 655360 | tf_op jit(solution)/shard_map/all_to_all | solution.py:173
  150.6 3.9 %collective-permute-start.11 = (f32[5,128,128]{2,1,0:T(8,128)S(1)}, f32[5,128,128]{2,1,0:T(8,128)S(1)}, u32[]{:S(2)}, u32[]{:S(2)}) collective-permute-start(f32[5,128,128]{2,1,0:T(8,128)S(1)} %bitcast.32), channel_id=1, source_target_pairs={{0,1},{1,0},{2,3},{3,2},{4,5},{5,4},{6,7},{7,6},{8,9},{9,8},{10,11... | collective-permute-start | bytes 983048 | tf_op jit(solution)/shard_map/ppermute | solution.py:165
  155.8 20.4 %shard_map.44 = f32[512,512]{1,0:T(8,128)S(1)} custom-call(s32[1]{0:T(128)} %bitcast.place, f32[5,128,128]{2,1,0:T(8,128)S(1)} %bitcast.33, f32[5,128,128]{2,1,0:T(8,128)S(1)} %collective-permute-done.11.came_ref), custom_call_target="tpu_custom_call" | custom-call | flops 268435456 | bytes 2097152 | tf_op jit(solution)/shard_map/pallas_call | solution.py:151
  177.4 1.9 collective-permute-start.12
  179.3 9.1 %collective-permute-done.12 = bf16[112,512]{1,0:T(8,128)(2,1)S(1)} collective-permute-done((bf16[112,512]{1,0:T(8,128)(2,1)S(1)}, bf16[112,512]{1,0:T(8,128)(2,1)S(1)}, u32[]{:S(2)}, u32[]{:S(2)}) %collective-permute-start.12) | collective-permute-done | bytes 114720 | tf_op jit(solution)/shard_map/ppermute | solution.py:165
  188.6 4.7 %collective-permute-start.13 = (bf16[112,384]{1,0:T(8,128)(2,1)S(1)}, bf16[112,384]{1,0:T(8,128)(2,1)S(1)}, u32[]{:S(2)}, u32[]{:S(2)}) collective-permute-start(bf16[112,384]{1,0:T(8,128)(2,1)S(1)} %get-tuple-element.42), channel_id=1, source_target_pairs={{0,24},{1,25},{2,26},{3,27},{4,28},{5,29},{6,30},{7,31},{8,0},{9,1... | collective-permute-start | bytes 258056 | tf_op jit(solution)/shard_map/ppermute | solution.py:165
  194.9 3.6 %collective-permute-done.14 = bf16[112,384]{1,0:T(8,128)(2,1)S(1)} collective-permute-done((bf16[112,384]{1,0:T(8,128)(2,1)S(1)}, bf16[112,384]{1,0:T(8,128)(2,1)S(1)}, u32[]{:S(2)}, u32[]{:S(2)}) %collective-permute-start.14) | collective-permute-done | bytes 86048 | tf_op jit(solution)/shard_map/ppermute | solution.py:165
  198.5 1.8 collective-permute-done.15
  201.2 17.3 %all_to_all.55.refs_0_ = bf16[8,112,128]{2,1,0:T(8,128)(2,1)S(1)} all-to-all(bf16[8,112,128]{2,1,0:T(8,128)(2,1)S(1)} %broadcast_in_dim.15), channel_id=1, replica_groups=mesh['z'=8,'y'=4,'x'=4,'core'=2] {'z'}, dimensions={0} | all-to-all | bytes 458752 | tf_op jit(solution)/shard_map/all_to_all | solution.py:173
  218.5 2.7 collective-permute-start.16
  221.1 3.8 %collective-permute-done.17.refs_3_ = bf16[8,112,128]{2,1,0:T(8,128)(2,1)S(1)} collective-permute-done((bf16[8,112,128]{2,1,0:T(8,128)(2,1)S(1)}, bf16[8,112,128]{2,1,0:T(8,128)(2,1)S(1)}, u32[]{:S(2)}, u32[]{:S(2)}) %collective-permute-start.17) | collective-permute-done | bytes 229408 | tf_op jit(solution)/shard_map/ppermute | solution.py:165
  225.1 2.7 collective-permute-start.19
  227.8 2.6 collective-permute-done.18
  230.5 2.9 copy-done.2
  233.4 4.6 %shard_map.45 = (f32[2,4,112,128]{3,2,1,0:T(8,128)S(1)}, bf16[8,4,112,128]{3,2,1,0:T(8,128)(2,1)S(1)}) custom-call(s32[2]{0:T(128)S(1)} %pad_add_fusion.place, bf16[4,2,112,3584]{3,2,1,0:T(8,128)(2,1)S(1)} %bitcast.29, bf16[8,112,128]{2,1,0:T(8,128)(2,1)S(1)} %all_to_all.55.refs_0_, bf16[8,112,128]{2,1,0:T(8,128)(2,1)S(1)} %collective-permute-done.16.refs_1_, ...), custom_call_target="tpu_custom_call" | custom-call | flops 822083584 | bytes 8388608 | tf_op jit(solution)/shard_map/pallas_call | solution.py:239
  238.9 5.5 %collective-permute-start.20 = (f32[4,112,128]{2,1,0:T(8,128)S(1)}, f32[4,112,128]{2,1,0:T(8,128)S(1)}, u32[]{:S(2)}, u32[]{:S(2)}) collective-permute-start(f32[4,112,128]{2,1,0:T(8,128)S(1)} %slice_bitcast_fusion.2), channel_id=1, source_target_pairs={{0,1},{1,0},{2,3},{3,2},{4,5},{5,4},{6,7},{7,6},{8,9},{9,8},{10,11... | collective-permute-start | bytes 688136 | tf_op jit(solution)/shard_map/ppermute | solution.py:165
  245.6 8.0 %shard_map.46 = (f32[4,112,384]{2,1,0:T(8,128)}, f32[4,112,384]{2,1,0:T(8,128)}, bf16[3584,512]{1,0:T(8,128)(2,1)}) custom-call(s32[1]{0:T(128)} %bitcast.place, bf16[896,3584]{1,0:T(8,128)(2,1)} %a_ref.3, bf16[3584,384]{1,0:T(8,128)(2,1)} %all-gather.5.cloned.1.call-done.b_ref, bf16[3584,128]{1,0:T(8,128)(2,1)} %bitcast.34), custom_call_target="tpu_custom_call" | custom-call | flops 2466250752 | bytes 12582912 | tf_op jit(solution)/shard_map/pallas_call | solution.py:310
  254.1 2.0 collective-permute-done.21
  257.3 15.9 %all_to_all.56.parts_ref = f32[4,112,512]{2,1,0:T(8,128)S(1)} all-to-all(f32[4,112,512]{2,1,0:T(8,128)S(1)} %pad_maximum_fusion.1), channel_id=1, replica_groups=mesh['z'=8,'y'=4,'x'=4,'core'=2] {'x'}, dimensions={0} | all-to-all | bytes 1835008 | tf_op jit(solution)/shard_map/all_to_all | solution.py:173
  274.0 1.3 collective-permute-start.22
  276.6 13.7 %all_to_all.57 = f32[16,40,128]{2,1,0:T(8,128)S(1)} all-to-all(f32[16,40,128]{2,1,0:T(8,128)S(1)} %bitcast.36), channel_id=1, replica_groups=mesh['z'=8,'y'=4,'x'=4,'core'=2] {'y','x'}, dimensions={0} | all-to-all | bytes 655360 | tf_op jit(solution)/shard_map/all_to_all | solution.py:173
  290.3 10.8 %all_to_all.58 = f32[8,40,128]{2,1,0:T(8,128)S(1)} all-to-all(f32[8,40,128]{2,1,0:T(8,128)S(1)} %broadcast_in_dim.16), channel_id=1, replica_groups=mesh['z'=8,'y'=4,'x'=4,'core'=2] {'z'}, dimensions={0} | all-to-all | bytes 327680 | tf_op jit(solution)/shard_map/all_to_all | solution.py:173
  301.2 10.8 %all_to_all.59 = f32[16,40,128]{2,1,0:T(8,128)S(1)} all-to-all(f32[16,40,128]{2,1,0:T(8,128)S(1)} %broadcast_in_dim.17), channel_id=1, replica_groups=mesh['z'=8,'y'=4,'x'=4,'core'=2] {'y','x'}, dimensions={0} | all-to-all | bytes 655360 | tf_op jit(solution)/shard_map/all_to_all | solution.py:173
  311.9 3.9 %collective-permute-start.23 = (f32[5,128,128]{2,1,0:T(8,128)S(1)}, f32[5,128,128]{2,1,0:T(8,128)S(1)}, u32[]{:S(2)}, u32[]{:S(2)}) collective-permute-start(f32[5,128,128]{2,1,0:T(8,128)S(1)} %bitcast.30), channel_id=1, source_target_pairs={{0,1},{1,0},{2,3},{3,2},{4,5},{5,4},{6,7},{7,6},{8,9},{9,8},{10,11... | collective-permute-start | bytes 983048 | tf_op jit(solution)/shard_map/ppermute | solution.py:165
  317.1 20.4 %shard_map.48 = f32[512,512]{1,0:T(8,128)S(1)} custom-call(s32[1]{0:T(128)} %bitcast.place, f32[5,128,128]{2,1,0:T(8,128)S(1)} %bitcast.31, f32[5,128,128]{2,1,0:T(8,128)S(1)} %collective-permute-done.23.came_ref), custom_call_target="tpu_custom_call" | custom-call | flops 268435456 | bytes 2097152 | tf_op jit(solution)/shard_map/pallas_call | solution.py:151
  337.5 1.9 convolution_multiply_fusion
  (80 shorter events, 19.9 us)
Async XLA Ops:
  7.2 1.2 copy-start
  7.2 75.6 %all-gather.3.cloned.1.call-start = ((), (), s32[]{:S(2)}) async-start(), calls=%async_computation.10 | async-start | bytes 3096576 | tf_op jit(solution)/shard_map/all_gather | solution.py:212
  8.4 13.4 %collective-permute-start = (bf16[112,512]{1,0:T(8,128)(2,1)S(1)}, bf16[112,512]{1,0:T(8,128)(2,1)S(1)}, u32[]{:S(2)}, u32[]{:S(2)}) collective-permute-start(bf16[112,512]{1,0:T(8,128)(2,1)S(1)} %constant_dynamic-slice_fusion), channel_id=1, source_target_pairs={{0,0},{1,8},{2,16},{3,24},{4,32},{5,40},{6,48},{7,56},{8,64},{9,72... | collective-permute-start | bytes 344072 | tf_op jit(solution)/shard_map/ppermute | solution.py:165
  21.9 8.0 %collective-permute-start.1 = (bf16[112,384]{1,0:T(8,128)(2,1)S(1)}, bf16[112,384]{1,0:T(8,128)(2,1)S(1)}, u32[]{:S(2)}, u32[]{:S(2)}) collective-permute-start(bf16[112,384]{1,0:T(8,128)(2,1)S(1)} %get-tuple-element.44), channel_id=1, source_target_pairs={{0,24},{1,25},{2,26},{3,27},{4,28},{5,29},{6,30},{7,31},{8,0},{9,1... | collective-permute-start | bytes 258056 | tf_op jit(solution)/shard_map/ppermute | solution.py:165
  26.2 5.3 %collective-permute-start.2 = (bf16[112,384]{1,0:T(8,128)(2,1)S(1)}, bf16[112,384]{1,0:T(8,128)(2,1)S(1)}, u32[]{:S(2)}, u32[]{:S(2)}) collective-permute-start(bf16[112,384]{1,0:T(8,128)(2,1)S(1)} %get-tuple-element.44), channel_id=1, source_target_pairs={{0,16},{1,17},{2,18},{3,19},{4,20},{5,21},{6,22},{7,23},{8,24},{9,... | collective-permute-start | bytes 258056 | tf_op jit(solution)/shard_map/ppermute | solution.py:165
  27.6 6.5 %collective-permute-start.3 = (bf16[112,384]{1,0:T(8,128)(2,1)S(1)}, bf16[112,384]{1,0:T(8,128)(2,1)S(1)}, u32[]{:S(2)}, u32[]{:S(2)}) collective-permute-start(bf16[112,384]{1,0:T(8,128)(2,1)S(1)} %get-tuple-element.44), channel_id=1, source_target_pairs={{0,8},{1,9},{2,10},{3,11},{4,12},{5,13},{6,14},{7,15},{8,16},{9,17... | collective-permute-start | bytes 258056 | tf_op jit(solution)/shard_map/ppermute | solution.py:165
  34.1 0.7 copy-start.5
  34.9 210.8 %all-gather.5.cloned.1.call-start = ((), (), s32[]{:S(2)}) async-start(), calls=%async_computation.11 | async-start | bytes 3096576 | tf_op jit(solution)/shard_map/all_gather | solution.py:212
  55.2 6.5 %collective-permute-start.5 = (bf16[8,112,128]{2,1,0:T(8,128)(2,1)S(1)}, bf16[8,112,128]{2,1,0:T(8,128)(2,1)S(1)}, u32[]{:S(2)}, u32[]{:S(2)}) collective-permute-start(bf16[8,112,128]{2,1,0:T(8,128)(2,1)S(1)} %all_to_all.50.refs_0_), channel_id=1, source_target_pairs={{0,8},{1,9},{2,10},{3,11},{4,12},{5,13},{6,14},{7,15},{8,16},{9,17... | collective-permute-start | bytes 688136 | tf_op jit(solution)/shard_map/ppermute | solution.py:165
  55.2 6.6 %collective-permute-start.4 = (bf16[8,112,128]{2,1,0:T(8,128)(2,1)S(1)}, bf16[8,112,128]{2,1,0:T(8,128)(2,1)S(1)}, u32[]{:S(2)}, u32[]{:S(2)}) collective-permute-start(bf16[8,112,128]{2,1,0:T(8,128)(2,1)S(1)} %all_to_all.50.refs_0_), channel_id=1, source_target_pairs={{0,24},{1,25},{2,26},{3,27},{4,28},{5,29},{6,30},{7,31},{8,0},{9,1... | collective-permute-start | bytes 688136 | tf_op jit(solution)/shard_map/ppermute | solution.py:165
  61.7 5.5 %collective-permute-start.6 = (bf16[4,112,128]{2,1,0:T(8,128)(2,1)S(1)}, bf16[4,112,128]{2,1,0:T(8,128)(2,1)S(1)}, u32[]{:S(2)}, u32[]{:S(2)}) collective-permute-start(bf16[4,112,128]{2,1,0:T(8,128)(2,1)S(1)} %slice.66), channel_id=1, source_target_pairs={{0,8},{1,9},{2,10},{3,11},{4,12},{5,13},{6,14},{7,15},{8,16},{9,17... | collective-permute-start | bytes 344072 | tf_op jit(solution)/shard_map/ppermute | solution.py:165
  61.9 5.4 %collective-permute-start.7 = (bf16[4,112,128]{2,1,0:T(8,128)(2,1)S(1)}, bf16[4,112,128]{2,1,0:T(8,128)(2,1)S(1)}, u32[]{:S(2)}, u32[]{:S(2)}) collective-permute-start(bf16[4,112,128]{2,1,0:T(8,128)(2,1)S(1)} %slice.67), channel_id=1, source_target_pairs={{0,24},{1,25},{2,26},{3,27},{4,28},{5,29},{6,30},{7,31},{8,0},{9,1... | collective-permute-start | bytes 344072 | tf_op jit(solution)/shard_map/ppermute | solution.py:165
  67.3 2.9 copy-start.1
  75.7 7.0 %collective-permute-start.8 = (f32[4,112,128]{2,1,0:T(8,128)S(1)}, f32[4,112,128]{2,1,0:T(8,128)S(1)}, u32[]{:S(2)}, u32[]{:S(2)}) collective-permute-start(f32[4,112,128]{2,1,0:T(8,128)S(1)} %slice_bitcast_fusion.3), channel_id=1, source_target_pairs={{0,1},{1,0},{2,3},{3,2},{4,5},{5,4},{6,7},{7,6},{8,9},{9,8},{10,11... | collective-permute-start | bytes 688136 | tf_op jit(solution)/shard_map/ppermute | solution.py:165
  89.1 3.8 %collective-permute-start.9 = (f32[4,112,384]{2,1,0:T(8,128)}, f32[4,112,384]{2,1,0:T(8,128)S(1)}, u32[]{:S(2)}, u32[]{:S(2)}) collective-permute-start(f32[4,112,384]{2,1,0:T(8,128)} %get-tuple-element.28), channel_id=1, source_target_pairs={{0,1},{1,0},{2,3},{3,2},{4,5},{5,4},{6,7},{7,6},{8,9},{9,8},{10,11... | collective-permute-start | bytes 2064392 | tf_op jit(solution)/shard_map/ppermute | solution.py:165
  111.1 3.2 collective-permute-start.10
  150.6 5.2 %collective-permute-start.11 = (f32[5,128,128]{2,1,0:T(8,128)S(1)}, f32[5,128,128]{2,1,0:T(8,128)S(1)}, u32[]{:S(2)}, u32[]{:S(2)}) collective-permute-start(f32[5,128,128]{2,1,0:T(8,128)S(1)} %bitcast.32), channel_id=1, source_target_pairs={{0,1},{1,0},{2,3},{3,2},{4,5},{5,4},{6,7},{7,6},{8,9},{9,8},{10,11... | collective-permute-start | bytes 983048 | tf_op jit(solution)/shard_map/ppermute | solution.py:165
  177.4 11.1 %collective-permute-start.12 = (bf16[112,512]{1,0:T(8,128)(2,1)S(1)}, bf16[112,512]{1,0:T(8,128)(2,1)S(1)}, u32[]{:S(2)}, u32[]{:S(2)}) collective-permute-start(bf16[112,512]{1,0:T(8,128)(2,1)S(1)} %fusion), channel_id=1, source_target_pairs={{0,0},{1,8},{2,16},{3,24},{4,32},{5,40},{6,48},{7,56},{8,64},{9,72... | collective-permute-start | bytes 344072 | tf_op jit(solution)/shard_map/ppermute | solution.py:165
  188.6 6.3 %collective-permute-start.13 = (bf16[112,384]{1,0:T(8,128)(2,1)S(1)}, bf16[112,384]{1,0:T(8,128)(2,1)S(1)}, u32[]{:S(2)}, u32[]{:S(2)}) collective-permute-start(bf16[112,384]{1,0:T(8,128)(2,1)S(1)} %get-tuple-element.42), channel_id=1, source_target_pairs={{0,24},{1,25},{2,26},{3,27},{4,28},{5,29},{6,30},{7,31},{8,0},{9,1... | collective-permute-start | bytes 258056 | tf_op jit(solution)/shard_map/ppermute | solution.py:165
  193.2 5.2 %collective-permute-start.14 = (bf16[112,384]{1,0:T(8,128)(2,1)S(1)}, bf16[112,384]{1,0:T(8,128)(2,1)S(1)}, u32[]{:S(2)}, u32[]{:S(2)}) collective-permute-start(bf16[112,384]{1,0:T(8,128)(2,1)S(1)} %get-tuple-element.42), channel_id=1, source_target_pairs={{0,16},{1,17},{2,18},{3,19},{4,20},{5,21},{6,22},{7,23},{8,24},{9,... | collective-permute-start | bytes 258056 | tf_op jit(solution)/shard_map/ppermute | solution.py:165
  194.1 6.2 %collective-permute-start.15 = (bf16[112,384]{1,0:T(8,128)(2,1)S(1)}, bf16[112,384]{1,0:T(8,128)(2,1)S(1)}, u32[]{:S(2)}, u32[]{:S(2)}) collective-permute-start(bf16[112,384]{1,0:T(8,128)(2,1)S(1)} %get-tuple-element.42), channel_id=1, source_target_pairs={{0,8},{1,9},{2,10},{3,11},{4,12},{5,13},{6,14},{7,15},{8,16},{9,17... | collective-permute-start | bytes 258056 | tf_op jit(solution)/shard_map/ppermute | solution.py:165
  200.4 0.7 copy-start.4
  218.5 6.5 %collective-permute-start.17 = (bf16[8,112,128]{2,1,0:T(8,128)(2,1)S(1)}, bf16[8,112,128]{2,1,0:T(8,128)(2,1)S(1)}, u32[]{:S(2)}, u32[]{:S(2)}) collective-permute-start(bf16[8,112,128]{2,1,0:T(8,128)(2,1)S(1)} %all_to_all.55.refs_0_), channel_id=1, source_target_pairs={{0,8},{1,9},{2,10},{3,11},{4,12},{5,13},{6,14},{7,15},{8,16},{9,17... | collective-permute-start | bytes 688136 | tf_op jit(solution)/shard_map/ppermute | solution.py:165
  218.5 6.6 %collective-permute-start.16 = (bf16[8,112,128]{2,1,0:T(8,128)(2,1)S(1)}, bf16[8,112,128]{2,1,0:T(8,128)(2,1)S(1)}, u32[]{:S(2)}, u32[]{:S(2)}) collective-permute-start(bf16[8,112,128]{2,1,0:T(8,128)(2,1)S(1)} %all_to_all.55.refs_0_), channel_id=1, source_target_pairs={{0,24},{1,25},{2,26},{3,27},{4,28},{5,29},{6,30},{7,31},{8,0},{9,1... | collective-permute-start | bytes 688136 | tf_op jit(solution)/shard_map/ppermute | solution.py:165
  225.0 5.5 %collective-permute-start.18 = (bf16[4,112,128]{2,1,0:T(8,128)(2,1)S(1)}, bf16[4,112,128]{2,1,0:T(8,128)(2,1)S(1)}, u32[]{:S(2)}, u32[]{:S(2)}) collective-permute-start(bf16[4,112,128]{2,1,0:T(8,128)(2,1)S(1)} %slice.70), channel_id=1, source_target_pairs={{0,8},{1,9},{2,10},{3,11},{4,12},{5,13},{6,14},{7,15},{8,16},{9,17... | collective-permute-start | bytes 344072 | tf_op jit(solution)/shard_map/ppermute | solution.py:165
  225.1 5.4 %collective-permute-start.19 = (bf16[4,112,128]{2,1,0:T(8,128)(2,1)S(1)}, bf16[4,112,128]{2,1,0:T(8,128)(2,1)S(1)}, u32[]{:S(2)}, u32[]{:S(2)}) collective-permute-start(bf16[4,112,128]{2,1,0:T(8,128)(2,1)S(1)} %slice.71), channel_id=1, source_target_pairs={{0,24},{1,25},{2,26},{3,27},{4,28},{5,29},{6,30},{7,31},{8,0},{9,1... | collective-permute-start | bytes 344072 | tf_op jit(solution)/shard_map/ppermute | solution.py:165
  230.5 2.9 copy-start.2
  238.0 0.9 copy-start.3
  238.9 6.6 %collective-permute-start.20 = (f32[4,112,128]{2,1,0:T(8,128)S(1)}, f32[4,112,128]{2,1,0:T(8,128)S(1)}, u32[]{:S(2)}, u32[]{:S(2)}) collective-permute-start(f32[4,112,128]{2,1,0:T(8,128)S(1)} %slice_bitcast_fusion.2), channel_id=1, source_target_pairs={{0,1},{1,0},{2,3},{3,2},{4,5},{5,4},{6,7},{7,6},{8,9},{9,8},{10,11... | collective-permute-start | bytes 688136 | tf_op jit(solution)/shard_map/ppermute | solution.py:165
  253.6 2.4 collective-permute-start.21
  274.0 2.5 collective-permute-start.22
  311.9 5.2 %collective-permute-start.23 = (f32[5,128,128]{2,1,0:T(8,128)S(1)}, f32[5,128,128]{2,1,0:T(8,128)S(1)}, u32[]{:S(2)}, u32[]{:S(2)}) collective-permute-start(f32[5,128,128]{2,1,0:T(8,128)S(1)} %bitcast.30), channel_id=1, source_target_pairs={{0,1},{1,0},{2,3},{3,2},{4,5},{5,4},{6,7},{7,6},{8,9},{9,8},{10,11... | collective-permute-start | bytes 983048 | tf_op jit(solution)/shard_map/ppermute | solution.py:165
Sparse Core Ops, SparseCore 0:
  35.0 46.6 all-gather.2
  201.2 42.0 all-gather.4

commit v4 on v3

--- a/solution.py
+++ b/solution.py
@@ -14,7 +14,7 @@
 AXES = ("z", "y", "x", "core")
 SIZES = (8, 4, 4, 2)
 HALF = K // 2
-FEW = 128
+FEW = 256
 ROWS = M // 256
 
 
@@ -39,7 +39,12 @@
             ratio[i, k + 1] = (e[i, k + 1] * a - e[i, k] * b) * over
         for i in range(k + 2, R):
             for j in range(k + 2, i + 1):
-                e[i, j] = e[i, j] - (ratio[i, k] * e[j, k] + ratio[i, k + 1] * e[j, k + 1])
+                if i < k + 4:
+                    one = (e[i, k] * c - e[i, k + 1] * b) * e[j, k]
+                    two = (e[i, k + 1] * a - e[i, k] * b) * e[j, k + 1]
+                    e[i, j] = e[i, j] - (one + two) * over
+                else:
+                    e[i, j] = e[i, j] - (ratio[i, k] * e[j, k] + ratio[i, k + 1] * e[j, k + 1])
             row[i] = row[i] - (ratio[i, k] * row[k] + ratio[i, k + 1] * row[k + 1])
         solved[k] = (c * row[k] - b * row[k + 1]) * over
         solved[k + 1] = (a * row[k + 1] - b * row[k]) * over
@@ -208,8 +213,9 @@
 
 def gathered_rows(rows):
     own = permute(rows, chunk_place)
-    many, few = lax.optimization_barrier((gather_y_small(own[:, FEW:]), own[:, :FEW]))
-    return lax.all_gather(many, "z", axis=0, tiled=True), gather_y(exchange(copies(few, "z"), "z"))
+    many, few = gather_y_small(own[:, FEW:]), exchange(copies(own[:, :FEW], "z"), "z")
+    many, few = lax.optimization_barrier((many, few))
+    return lax.all_gather(many, "z", axis=0, tiled=True), gather_y(few)
 
 
 def few_step(place, a_ref, *refs):

time: 347 us -> 358 us (1.032)
  blocking collectives: 141 us -> 106 us
  waiting for transfers between devices: 53.2 us -> 79.2 us
  starting transfers between devices: 55.1 us -> 74.6 us
    all_to_all x10 -> x8, blocking collectives: 141 us -> 106 us  [exchange(): return lax.all_to_all(pieces, axes, 0, 0, tiled=True)]
    all_to_all x0 -> x2, starting transfers between devices: none -> 25.3 us  [exchange(): return lax.all_to_all(pieces, axes, 0, 0, tiled=True)]
    all_to_all x0 -> x2, waiting for transfers between devices: none -> 12.7 us  [exchange(): return lax.all_to_all(pieces, axes, 0, 0, tiled=True)]
    ppermute x24, waiting for transfers between devices: 53.1 us -> 65 us  [permute(): lax.ppermute(values, AXES, [(index[p], index[where(*p)]) for p in places])]
    ppermute x24, starting transfers between devices: 55 us -> 49.3 us  [permute(): lax.ppermute(values, AXES, [(index[p], index[where(*p)]) for p in places])]
  transfers between devices with their start and end apart: 26 -> 28, of which waited for: 19 -> 24; matrix products, arithmetic and copies ran while one was open for 0% -> 0% of each run, Pallas kernels for 3% -> 3%
where the time goes in v4:
time: 358 us; the launch traced here: 357 us
  blocking collectives  106 us (30%)
  waiting for transfers between devices  79.2 us (22%)
  starting transfers between devices  74.6 us (21%)
  Pallas kernels  67 us (19%)
  between operations  14.4 us (4%)
  local copies, waits for them, and re-layouts  10.1 us (3%)
    all_to_all x8, blocking collectives, exchange(): return lax.all_to_all(pieces, axes, 0, 0, tiled=True)  106 us
    ppermute x24, waiting for transfers between devices, permute(): lax.ppermute(values, AXES, [(index[p], index[where(*p)]) for p in places])  65 us
    ppermute x24, starting transfers between devices, permute(): lax.ppermute(values, AXES, [(index[p], index[where(*p)]) for p in places])  49.3 us
    pallas_call x2, Pallas kernels, inverse_factor(): pl.pallas_call(chol_inverse, out_shape=jax.ShapeDtypeStruct((K, K), jnp.f...  40.1 us
    all_to_all x2, starting transfers between devices, exchange(): return lax.all_to_all(pieces, axes, 0, 0, tiled=True)  25.3 us
    pallas_call x2, Pallas kernels, product_many(): pl.pallas_call(many_step, out_shape=[part, part] + [jax.ShapeDtypeStruct(...  14.1 us
    all_to_all x2, waiting for transfers between devices, exchange(): return lax.all_to_all(pieces, axes, 0, 0, tiled=True)  12.7 us
    pallas_call x2, Pallas kernels, product_few(): pl.pallas_call(few_step, out_shape=[jax.ShapeDtypeStruct((2, 4, ROWS, FEW...  11.3 us
  transfers between devices with their start and end apart: 28, of which 24 were waited for; matrix products, arithmetic and copies ran while one was open for 0% of the time, Pallas kernels for 3%

profile of v4, /device:TPU:1, one launch (start us, length us, event | category | flops | bytes accessed | tf_op | source)
XLA Modules:
  0.0 357.3 jit_solution(5764178982697336100)
XLA Ops:
  8.4 4.6 %collective-permute-start = (bf16[112,512]{1,0:T(8,128)(2,1)S(1)}, bf16[112,512]{1,0:T(8,128)(2,1)S(1)}, u32[]{:S(2)}, u32[]{:S(2)}) collective-permute-start(bf16[112,512]{1,0:T(8,128)(2,1)S(1)} %constant_dynamic-slice_fusion), channel_id=1, source_target_pairs={{0,0},{1,8},{2,16},{3,24},{4,32},{5,40},{6,48},{7,56},{8,64},{9,72... | collective-permute-start | bytes 344072 | tf_op jit(solution)/shard_map/ppermute | solution.py:170
  13.0 8.5 %collective-permute-done = bf16[112,512]{1,0:T(8,128)(2,1)S(1)} collective-permute-done((bf16[112,512]{1,0:T(8,128)(2,1)S(1)}, bf16[112,512]{1,0:T(8,128)(2,1)S(1)}, u32[]{:S(2)}, u32[]{:S(2)}) %collective-permute-start) | collective-permute-done | bytes 114720 | tf_op jit(solution)/shard_map/ppermute | solution.py:170
  22.3 14.3 %all-to-all-start = ((bf16[8,112,256]{2,1,0:T(8,128)(2,1)}), bf16[8,112,256]{2,1,0:T(8,128)(2,1)S(1)}, u32[]{:S(2)}, u32[]{:S(2)}) async-start(bf16[8,112,256]{2,1,0:T(8,128)(2,1)} %broadcast_in_dim.12), calls=%async_computation | async-start | bytes 917504 | tf_op jit(solution)/shard_map/all_to_all | solution.py:178
  36.7 2.2 collective-permute-start.1
  40.1 3.3 collective-permute-done.2
  44.0 4.0 %all-to-all-done.refs_0_ = bf16[8,112,256]{2,1,0:T(8,128)(2,1)S(1)} async-done(((bf16[8,112,256]{2,1,0:T(8,128)(2,1)}), bf16[8,112,256]{2,1,0:T(8,128)(2,1)S(1)}, u32[]{:S(2)}, u32[]{:S(2)}) %all-to-all-start) | async-done | bytes 458784 | tf_op jit(solution)/shard_map/all_to_all | solution.py:178
  48.0 3.5 collective-permute-start.5
  51.4 6.3 %collective-permute-done.5.refs_3_ = bf16[8,112,256]{2,1,0:T(8,128)(2,1)S(1)} collective-permute-done((bf16[8,112,256]{2,1,0:T(8,128)(2,1)S(1)}, bf16[8,112,256]{2,1,0:T(8,128)(2,1)S(1)}, u32[]{:S(2)}, u32[]{:S(2)}) %collective-permute-start.5) | collective-permute-done | bytes 458784 | tf_op jit(solution)/shard_map/ppermute | solution.py:170
  57.7 2.3 collective-permute-start.6
  60.7 5.2 %collective-permute-done.6 = bf16[4,112,256]{2,1,0:T(8,128)(2,1)S(1)} collective-permute-done((bf16[4,112,256]{2,1,0:T(8,128)(2,1)S(1)}, bf16[4,112,256]{2,1,0:T(8,128)(2,1)S(1)}, u32[]{:S(2)}, u32[]{:S(2)}) %collective-permute-start.6) | collective-permute-done | bytes 229408 | tf_op jit(solution)/shard_map/ppermute | solution.py:170
  66.6 2.9 copy-done.1
  69.5 6.2 %shard_map.41 = (f32[2,4,112,256]{3,2,1,0:T(8,128)S(1)}, bf16[8,4,112,256]{3,2,1,0:T(8,128)(2,1)}) custom-call(s32[2]{0:T(128)S(1)} %pad_add_fusion.place, bf16[4,2,112,3584]{3,2,1,0:T(8,128)(2,1)S(1)} %bitcast.28, bf16[8,112,256]{2,1,0:T(8,128)(2,1)S(1)} %all-to-all-done.refs_0_, bf16[8,112,256]{2,1,0:T(8,128)(2,1)S(1)} %collective-permute-done.4.refs_1_, ...), custom_call_target="tpu_custom_call" | custom-call | flops 1644167168 | bytes 8388608 | tf_op jit(solution)/shard_map/pallas_call | solution.py:245
  75.7 6.0 %collective-permute-start.8 = (f32[4,112,256]{2,1,0:T(8,128)S(1)}, f32[4,112,256]{2,1,0:T(8,128)S(1)}, u32[]{:S(2)}, u32[]{:S(2)}) collective-permute-start(f32[4,112,256]{2,1,0:T(8,128)S(1)} %slice_bitcast_fusion.1), channel_id=1, source_target_pairs={{0,1},{1,0},{2,3},{3,2},{4,5},{5,4},{6,7},{7,6},{8,9},{9,8},{10,11... | collective-permute-start | bytes 1376264 | tf_op jit(solution)/shard_map/ppermute | solution.py:170
  83.3 1.5 all-gather.3.cloned.1.call-done.b_ref
  84.8 6.0 %shard_map.42 = (f32[4,112,256]{2,1,0:T(8,128)}, f32[4,112,256]{2,1,0:T(8,128)}) custom-call(s32[1]{0:T(128)} %bitcast.place, bf16[896,3584]{1,0:T(8,128)(2,1)} %a_ref.3, bf16[3584,256]{1,0:T(8,128)(2,1)} %all-gather.3.cloned.1.call-done.b_ref), custom_call_target="tpu_custom_call" | custom-call | flops 1644167168 | bytes 12582912 | tf_op jit(solution)/shard_map/pallas_call | solution.py:316
  90.7 4.9 %collective-permute-start.9 = (f32[4,112,256]{2,1,0:T(8,128)}, f32[4,112,256]{2,1,0:T(8,128)S(1)}, u32[]{:S(2)}, u32[]{:S(2)}) collective-permute-start(f32[4,112,256]{2,1,0:T(8,128)} %get-tuple-element.28), channel_id=1, source_target_pairs={{0,1},{1,0},{2,3},{3,2},{4,5},{5,4},{6,7},{7,6},{8,9},{9,8},{10,11... | collective-permute-start | bytes 1376264 | tf_op jit(solution)/shard_map/ppermute | solution.py:170
  95.6 1.7 collective-permute-done.9
  98.5 16.6 %all_to_all.50.parts_ref = f32[4,112,512]{2,1,0:T(8,128)S(1)} all-to-all(f32[4,112,512]{2,1,0:T(8,128)S(1)} %pad_maximum_fusion), channel_id=1, replica_groups=mesh['z'=8,'y'=4,'x'=4,'core'=2] {'x'}, dimensions={0} | all-to-all | bytes 1835008 | tf_op jit(solution)/shard_map/all_to_all | solution.py:178
  115.9 1.9 collective-permute-start.10
  119.1 13.0 %all_to_all.51 = f32[16,40,128]{2,1,0:T(8,128)S(1)} all-to-all(f32[16,40,128]{2,1,0:T(8,128)S(1)} %bitcast.35), channel_id=1, replica_groups=mesh['z'=8,'y'=4,'x'=4,'core'=2] {'y','x'}, dimensions={0} | all-to-all | bytes 655360 | tf_op jit(solution)/shard_map/all_to_all | solution.py:178
  132.2 12.4 %all_to_all.52 = f32[8,40,128]{2,1,0:T(8,128)S(1)} all-to-all(f32[8,40,128]{2,1,0:T(8,128)S(1)} %broadcast_in_dim.13), channel_id=1, replica_groups=mesh['z'=8,'y'=4,'x'=4,'core'=2] {'z'}, dimensions={0} | all-to-all | bytes 327680 | tf_op jit(solution)/shard_map/all_to_all | solution.py:178
  144.7 10.9 %all_to_all.53 = f32[16,40,128]{2,1,0:T(8,128)S(1)} all-to-all(f32[16,40,128]{2,1,0:T(8,128)S(1)} %broadcast_in_dim.14), channel_id=1, replica_groups=mesh['z'=8,'y'=4,'x'=4,'core'=2] {'y','x'}, dimensions={0} | all-to-all | bytes 655360 | tf_op jit(solution)/shard_map/all_to_all | solution.py:178
  155.6 3.9 %collective-permute-start.11 = (f32[5,128,128]{2,1,0:T(8,128)S(1)}, f32[5,128,128]{2,1,0:T(8,128)S(1)}, u32[]{:S(2)}, u32[]{:S(2)}) collective-permute-start(f32[5,128,128]{2,1,0:T(8,128)S(1)} %bitcast.33), channel_id=1, source_target_pairs={{0,1},{1,0},{2,3},{3,2},{4,5},{5,4},{6,7},{7,6},{8,9},{9,8},{10,11... | collective-permute-start | bytes 983048 | tf_op jit(solution)/shard_map/ppermute | solution.py:170
  160.8 20.0 %shard_map.44 = f32[512,512]{1,0:T(8,128)S(1)} custom-call(s32[1]{0:T(128)} %bitcast.place, f32[5,128,128]{2,1,0:T(8,128)S(1)} %bitcast.34, f32[5,128,128]{2,1,0:T(8,128)S(1)} %collective-permute-done.11.came_ref), custom_call_target="tpu_custom_call" | custom-call | flops 268435456 | bytes 2097152 | tf_op jit(solution)/shard_map/pallas_call | solution.py:156
  182.0 1.9 collective-permute-start.12
  183.9 9.1 %collective-permute-done.12 = bf16[112,512]{1,0:T(8,128)(2,1)S(1)} collective-permute-done((bf16[112,512]{1,0:T(8,128)(2,1)S(1)}, bf16[112,512]{1,0:T(8,128)(2,1)S(1)}, u32[]{:S(2)}, u32[]{:S(2)}) %collective-permute-start.12) | collective-permute-done | bytes 114720 | tf_op jit(solution)/shard_map/ppermute | solution.py:170
  193.9 11.0 %all-to-all-start.5 = ((bf16[8,112,256]{2,1,0:T(8,128)(2,1)}), bf16[8,112,256]{2,1,0:T(8,128)(2,1)S(1)}, u32[]{:S(2)}, u32[]{:S(2)}) async-start(bf16[8,112,256]{2,1,0:T(8,128)(2,1)} %broadcast_in_dim.15), calls=%async_computation.5 | async-start | bytes 917504 | tf_op jit(solution)/shard_map/all_to_all | solution.py:178
  205.7 1.5 collective-permute-start.14
  208.1 2.1 collective-permute-done.14
  210.2 2.4 collective-permute-done.15
  212.7 8.7 %all-to-all-done.5.refs_0_ = bf16[8,112,256]{2,1,0:T(8,128)(2,1)S(1)} async-done(((bf16[8,112,256]{2,1,0:T(8,128)(2,1)}), bf16[8,112,256]{2,1,0:T(8,128)(2,1)S(1)}, u32[]{:S(2)}, u32[]{:S(2)}) %all-to-all-start.5) | async-done | bytes 458784 | tf_op jit(solution)/shard_map/all_to_all | solution.py:178
  221.5 2.7 collective-permute-start.16
  224.2 10.1 %collective-permute-done.17.refs_3_ = bf16[8,112,256]{2,1,0:T(8,128)(2,1)S(1)} collective-permute-done((bf16[8,112,256]{2,1,0:T(8,128)(2,1)S(1)}, bf16[8,112,256]{2,1,0:T(8,128)(2,1)S(1)}, u32[]{:S(2)}, u32[]{:S(2)}) %collective-permute-start.17) | collective-permute-done | bytes 458784 | tf_op jit(solution)/shard_map/ppermute | solution.py:170
  234.5 2.7 collective-permute-start.19
  237.2 4.3 %collective-permute-done.18 = bf16[4,112,256]{2,1,0:T(8,128)(2,1)S(1)} collective-permute-done((bf16[4,112,256]{2,1,0:T(8,128)(2,1)S(1)}, bf16[4,112,256]{2,1,0:T(8,128)(2,1)S(1)}, u32[]{:S(2)}, u32[]{:S(2)}) %collective-permute-start.18) | collective-permute-done | bytes 229408 | tf_op jit(solution)/shard_map/ppermute | solution.py:170
  241.5 2.9 copy-done.2
  244.4 5.0 %shard_map.45 = (f32[2,4,112,256]{3,2,1,0:T(8,128)S(1)}, bf16[8,4,112,256]{3,2,1,0:T(8,128)(2,1)S(1)}) custom-call(s32[2]{0:T(128)S(1)} %pad_add_fusion.place, bf16[4,2,112,3584]{3,2,1,0:T(8,128)(2,1)S(1)} %bitcast.29, bf16[8,112,256]{2,1,0:T(8,128)(2,1)S(1)} %all-to-all-done.5.refs_0_, bf16[8,112,256]{2,1,0:T(8,128)(2,1)S(1)} %collective-permute-done.16.refs_1_, ...), custom_call_target="tpu_custom_call" | custom-call | flops 1644167168 | bytes 8388608 | tf_op jit(solution)/shard_map/pallas_call | solution.py:245
  250.7 2.5 collective-permute-start.20
  254.7 8.2 %shard_map.46 = (f32[4,112,256]{2,1,0:T(8,128)}, f32[4,112,256]{2,1,0:T(8,128)}, bf16[3584,512]{1,0:T(8,128)(2,1)}) custom-call(s32[1]{0:T(128)} %bitcast.place, bf16[896,3584]{1,0:T(8,128)(2,1)} %a_ref.3, bf16[3584,256]{1,0:T(8,128)(2,1)} %all-gather.5.cloned.1.call-done.b_ref, bf16[3584,256]{1,0:T(8,128)(2,1)} %bitcast.30), custom_call_target="tpu_custom_call" | custom-call | flops 1644167168 | bytes 12582912 | tf_op jit(solution)/shard_map/pallas_call | solution.py:316
  263.3 1.7 collective-permute-done.21
  266.2 16.6 %all_to_all.54.parts_ref = f32[4,112,512]{2,1,0:T(8,128)S(1)} all-to-all(f32[4,112,512]{2,1,0:T(8,128)S(1)} %pad_maximum_fusion.1), channel_id=1, replica_groups=mesh['z'=8,'y'=4,'x'=4,'core'=2] {'x'}, dimensions={0} | all-to-all | bytes 1835008 | tf_op jit(solution)/shard_map/all_to_all | solution.py:178
  283.6 1.9 collective-permute-start.22
  286.8 12.9 %all_to_all.55 = f32[16,40,128]{2,1,0:T(8,128)S(1)} all-to-all(f32[16,40,128]{2,1,0:T(8,128)S(1)} %bitcast.36), channel_id=1, replica_groups=mesh['z'=8,'y'=4,'x'=4,'core'=2] {'y','x'}, dimensions={0} | all-to-all | bytes 655360 | tf_op jit(solution)/shard_map/all_to_all | solution.py:178
  299.8 12.7 %all_to_all.56 = f32[8,40,128]{2,1,0:T(8,128)S(1)} all-to-all(f32[8,40,128]{2,1,0:T(8,128)S(1)} %broadcast_in_dim.16), channel_id=1, replica_groups=mesh['z'=8,'y'=4,'x'=4,'core'=2] {'z'}, dimensions={0} | all-to-all | bytes 327680 | tf_op jit(solution)/shard_map/all_to_all | solution.py:178
  312.5 10.9 %all_to_all.57 = f32[16,40,128]{2,1,0:T(8,128)S(1)} all-to-all(f32[16,40,128]{2,1,0:T(8,128)S(1)} %broadcast_in_dim.17), channel_id=1, replica_groups=mesh['z'=8,'y'=4,'x'=4,'core'=2] {'y','x'}, dimensions={0} | all-to-all | bytes 655360 | tf_op jit(solution)/shard_map/all_to_all | solution.py:178
  323.4 3.9 %collective-permute-start.23 = (f32[5,128,128]{2,1,0:T(8,128)S(1)}, f32[5,128,128]{2,1,0:T(8,128)S(1)}, u32[]{:S(2)}, u32[]{:S(2)}) collective-permute-start(f32[5,128,128]{2,1,0:T(8,128)S(1)} %bitcast.31), channel_id=1, source_target_pairs={{0,1},{1,0},{2,3},{3,2},{4,5},{5,4},{6,7},{7,6},{8,9},{9,8},{10,11... | collective-permute-start | bytes 983048 | tf_op jit(solution)/shard_map/ppermute | solution.py:170
  328.6 20.0 %shard_map.48 = f32[512,512]{1,0:T(8,128)S(1)} custom-call(s32[1]{0:T(128)} %bitcast.place, f32[5,128,128]{2,1,0:T(8,128)S(1)} %bitcast.32, f32[5,128,128]{2,1,0:T(8,128)S(1)} %collective-permute-done.23.came_ref), custom_call_target="tpu_custom_call" | custom-call | flops 268435456 | bytes 2097152 | tf_op jit(solution)/shard_map/pallas_call | solution.py:156
  348.6 1.9 convolution_multiply_fusion
  (80 shorter events, 23.3 us)
Async XLA Ops:
  7.2 1.2 copy-start
  8.4 13.1 %collective-permute-start = (bf16[112,512]{1,0:T(8,128)(2,1)S(1)}, bf16[112,512]{1,0:T(8,128)(2,1)S(1)}, u32[]{:S(2)}, u32[]{:S(2)}) collective-permute-start(bf16[112,512]{1,0:T(8,128)(2,1)S(1)} %constant_dynamic-slice_fusion), channel_id=1, source_target_pairs={{0,0},{1,8},{2,16},{3,24},{4,32},{5,40},{6,48},{7,56},{8,64},{9,72... | collective-permute-start | bytes 344072 | tf_op jit(solution)/shard_map/ppermute | solution.py:170
  22.3 25.6 %all-to-all-start = ((bf16[8,112,256]{2,1,0:T(8,128)(2,1)}), bf16[8,112,256]{2,1,0:T(8,128)(2,1)S(1)}, u32[]{:S(2)}, u32[]{:S(2)}) async-start(bf16[8,112,256]{2,1,0:T(8,128)(2,1)} %broadcast_in_dim.12), calls=%async_computation | async-start | bytes 917504 | tf_op jit(solution)/shard_map/all_to_all | solution.py:178
  36.6 48.1 %all-gather.3.cloned.1.call-start = ((), (), s32[]{:S(2)}) async-start(), calls=%async_computation.10 | async-start | bytes 2064384 | tf_op jit(solution)/shard_map/all_gather | solution.py:218
  36.7 3.4 collective-permute-start.1
  38.8 4.5 %collective-permute-start.2 = (bf16[112,256]{1,0:T(8,128)(2,1)S(1)}, bf16[112,256]{1,0:T(8,128)(2,1)S(1)}, u32[]{:S(2)}, u32[]{:S(2)}) collective-permute-start(bf16[112,256]{1,0:T(8,128)(2,1)S(1)} %get-tuple-element.47), channel_id=1, source_target_pairs={{0,16},{1,17},{2,18},{3,19},{4,20},{5,21},{6,22},{7,23},{8,24},{9,... | collective-permute-start | bytes 172040 | tf_op jit(solution)/shard_map/ppermute | solution.py:170
  39.7 4.2 %collective-permute-start.3 = (bf16[112,256]{1,0:T(8,128)(2,1)S(1)}, bf16[112,256]{1,0:T(8,128)(2,1)S(1)}, u32[]{:S(2)}, u32[]{:S(2)}) collective-permute-start(bf16[112,256]{1,0:T(8,128)(2,1)S(1)} %get-tuple-element.47), channel_id=1, source_target_pairs={{0,8},{1,9},{2,10},{3,11},{4,12},{5,13},{6,14},{7,15},{8,16},{9,17... | collective-permute-start | bytes 172040 | tf_op jit(solution)/shard_map/ppermute | solution.py:170
  44.0 4.0 %copy-start.5 = (bf16[448,256]{1,0:T(8,128)(2,1)}, bf16[448,256]{1,0:T(8,128)(2,1)S(1)}, u32[]{:S(2)}) copy-start(bf16[448,256]{1,0:T(8,128)(2,1)S(1)} %constant_dynamic-update-slice_fusion.4) | copy-start | bytes 688132
  48.0 9.7 %collective-permute-start.5 = (bf16[8,112,256]{2,1,0:T(8,128)(2,1)S(1)}, bf16[8,112,256]{2,1,0:T(8,128)(2,1)S(1)}, u32[]{:S(2)}, u32[]{:S(2)}) collective-permute-start(bf16[8,112,256]{2,1,0:T(8,128)(2,1)S(1)} %all-to-all-done.refs_0_), channel_id=1, source_target_pairs={{0,8},{1,9},{2,10},{3,11},{4,12},{5,13},{6,14},{7,15},{8,16},{9,17... | collective-permute-start | bytes 1376264 | tf_op jit(solution)/shard_map/ppermute | solution.py:170
  51.4 8.6 %collective-permute-start.4 = (bf16[8,112,256]{2,1,0:T(8,128)(2,1)S(1)}, bf16[8,112,256]{2,1,0:T(8,128)(2,1)S(1)}, u32[]{:S(2)}, u32[]{:S(2)}) collective-permute-start(bf16[8,112,256]{2,1,0:T(8,128)(2,1)S(1)} %all-to-all-done.refs_0_), channel_id=1, source_target_pairs={{0,24},{1,25},{2,26},{3,27},{4,28},{5,29},{6,30},{7,31},{8,0},{9,1... | collective-permute-start | bytes 1376264 | tf_op jit(solution)/shard_map/ppermute | solution.py:170
  57.7 8.1 %collective-permute-start.6 = (bf16[4,112,256]{2,1,0:T(8,128)(2,1)S(1)}, bf16[4,112,256]{2,1,0:T(8,128)(2,1)S(1)}, u32[]{:S(2)}, u32[]{:S(2)}) collective-permute-start(bf16[4,112,256]{2,1,0:T(8,128)(2,1)S(1)} %slice.66), channel_id=1, source_target_pairs={{0,8},{1,9},{2,10},{3,11},{4,12},{5,13},{6,14},{7,15},{8,16},{9,17... | collective-permute-start | bytes 688136 | tf_op jit(solution)/shard_map/ppermute | solution.py:170
  60.0 6.5 %collective-permute-start.7 = (bf16[4,112,256]{2,1,0:T(8,128)(2,1)S(1)}, bf16[4,112,256]{2,1,0:T(8,128)(2,1)S(1)}, u32[]{:S(2)}, u32[]{:S(2)}) collective-permute-start(bf16[4,112,256]{2,1,0:T(8,128)(2,1)S(1)} %slice.67), channel_id=1, source_target_pairs={{0,24},{1,25},{2,26},{3,27},{4,28},{5,29},{6,30},{7,31},{8,0},{9,1... | collective-permute-start | bytes 688136 | tf_op jit(solution)/shard_map/ppermute | solution.py:170
  66.6 2.9 copy-start.1
  75.7 7.5 %collective-permute-start.8 = (f32[4,112,256]{2,1,0:T(8,128)S(1)}, f32[4,112,256]{2,1,0:T(8,128)S(1)}, u32[]{:S(2)}, u32[]{:S(2)}) collective-permute-start(f32[4,112,256]{2,1,0:T(8,128)S(1)} %slice_bitcast_fusion.1), channel_id=1, source_target_pairs={{0,1},{1,0},{2,3},{3,2},{4,5},{5,4},{6,7},{7,6},{8,9},{9,8},{10,11... | collective-permute-start | bytes 1376264 | tf_op jit(solution)/shard_map/ppermute | solution.py:170
  90.7 6.6 %collective-permute-start.9 = (f32[4,112,256]{2,1,0:T(8,128)}, f32[4,112,256]{2,1,0:T(8,128)S(1)}, u32[]{:S(2)}, u32[]{:S(2)}) collective-permute-start(f32[4,112,256]{2,1,0:T(8,128)} %get-tuple-element.28), channel_id=1, source_target_pairs={{0,1},{1,0},{2,3},{3,2},{4,5},{5,4},{6,7},{7,6},{8,9},{9,8},{10,11... | collective-permute-start | bytes 1376264 | tf_op jit(solution)/shard_map/ppermute | solution.py:170
  115.9 3.2 collective-permute-start.10
  155.6 5.2 %collective-permute-start.11 = (f32[5,128,128]{2,1,0:T(8,128)S(1)}, f32[5,128,128]{2,1,0:T(8,128)S(1)}, u32[]{:S(2)}, u32[]{:S(2)}) collective-permute-start(f32[5,128,128]{2,1,0:T(8,128)S(1)} %bitcast.33), channel_id=1, source_target_pairs={{0,1},{1,0},{2,3},{3,2},{4,5},{5,4},{6,7},{7,6},{8,9},{9,8},{10,11... | collective-permute-start | bytes 983048 | tf_op jit(solution)/shard_map/ppermute | solution.py:170
  182.0 11.1 %collective-permute-start.12 = (bf16[112,512]{1,0:T(8,128)(2,1)S(1)}, bf16[112,512]{1,0:T(8,128)(2,1)S(1)}, u32[]{:S(2)}, u32[]{:S(2)}) collective-permute-start(bf16[112,512]{1,0:T(8,128)(2,1)S(1)} %fusion), channel_id=1, source_target_pairs={{0,0},{1,8},{2,16},{3,24},{4,32},{5,40},{6,48},{7,56},{8,64},{9,72... | collective-permute-start | bytes 344072 | tf_op jit(solution)/shard_map/ppermute | solution.py:170
  193.9 27.5 %all-to-all-start.5 = ((bf16[8,112,256]{2,1,0:T(8,128)(2,1)}), bf16[8,112,256]{2,1,0:T(8,128)(2,1)S(1)}, u32[]{:S(2)}, u32[]{:S(2)}) async-start(bf16[8,112,256]{2,1,0:T(8,128)(2,1)} %broadcast_in_dim.15), calls=%async_computation.5 | async-start | bytes 917504 | tf_op jit(solution)/shard_map/all_to_all | solution.py:178
  204.9 49.8 %all-gather.5.cloned.1.call-start = ((), (), s32[]{:S(2)}) async-start(), calls=%async_computation.11 | async-start | bytes 2064384 | tf_op jit(solution)/shard_map/all_gather | solution.py:218
  205.0 3.1 collective-permute-start.13
  205.7 4.5 %collective-permute-start.14 = (bf16[112,256]{1,0:T(8,128)(2,1)S(1)}, bf16[112,256]{1,0:T(8,128)(2,1)S(1)}, u32[]{:S(2)}, u32[]{:S(2)}) collective-permute-start(bf16[112,256]{1,0:T(8,128)(2,1)S(1)} %get-tuple-element.44), channel_id=1, source_target_pairs={{0,16},{1,17},{2,18},{3,19},{4,20},{5,21},{6,22},{7,23},{8,24},{9,... | collective-permute-start | bytes 172040 | tf_op jit(solution)/shard_map/ppermute | solution.py:170
  207.2 5.5 %collective-permute-start.15 = (bf16[112,256]{1,0:T(8,128)(2,1)S(1)}, bf16[112,256]{1,0:T(8,128)(2,1)S(1)}, u32[]{:S(2)}, u32[]{:S(2)}) collective-permute-start(bf16[112,256]{1,0:T(8,128)(2,1)S(1)} %get-tuple-element.44), channel_id=1, source_target_pairs={{0,8},{1,9},{2,10},{3,11},{4,12},{5,13},{6,14},{7,15},{8,16},{9,17... | collective-permute-start | bytes 172040 | tf_op jit(solution)/shard_map/ppermute | solution.py:170
  212.6 8.7 %copy-start.4 = (bf16[448,256]{1,0:T(8,128)(2,1)}, bf16[448,256]{1,0:T(8,128)(2,1)S(1)}, u32[]{:S(2)}) copy-start(bf16[448,256]{1,0:T(8,128)(2,1)S(1)} %constant_dynamic-update-slice_fusion) | copy-start | bytes 688132
  221.4 12.9 %collective-permute-start.17 = (bf16[8,112,256]{2,1,0:T(8,128)(2,1)S(1)}, bf16[8,112,256]{2,1,0:T(8,128)(2,1)S(1)}, u32[]{:S(2)}, u32[]{:S(2)}) collective-permute-start(bf16[8,112,256]{2,1,0:T(8,128)(2,1)S(1)} %all-to-all-done.5.refs_0_), channel_id=1, source_target_pairs={{0,8},{1,9},{2,10},{3,11},{4,12},{5,13},{6,14},{7,15},{8,16},{9,17... | collective-permute-start | bytes 1376264 | tf_op jit(solution)/shard_map/ppermute | solution.py:170
  221.5 12.9 %collective-permute-start.16 = (bf16[8,112,256]{2,1,0:T(8,128)(2,1)S(1)}, bf16[8,112,256]{2,1,0:T(8,128)(2,1)S(1)}, u32[]{:S(2)}, u32[]{:S(2)}) collective-permute-start(bf16[8,112,256]{2,1,0:T(8,128)(2,1)S(1)} %all-to-all-done.5.refs_0_), channel_id=1, source_target_pairs={{0,24},{1,25},{2,26},{3,27},{4,28},{5,29},{6,30},{7,31},{8,0},{9,1... | collective-permute-start | bytes 1376264 | tf_op jit(solution)/shard_map/ppermute | solution.py:170
  234.3 7.2 %collective-permute-start.18 = (bf16[4,112,256]{2,1,0:T(8,128)(2,1)S(1)}, bf16[4,112,256]{2,1,0:T(8,128)(2,1)S(1)}, u32[]{:S(2)}, u32[]{:S(2)}) collective-permute-start(bf16[4,112,256]{2,1,0:T(8,128)(2,1)S(1)} %slice.70), channel_id=1, source_target_pairs={{0,8},{1,9},{2,10},{3,11},{4,12},{5,13},{6,14},{7,15},{8,16},{9,17... | collective-permute-start | bytes 688136 | tf_op jit(solution)/shard_map/ppermute | solution.py:170
  234.5 7.0 %collective-permute-start.19 = (bf16[4,112,256]{2,1,0:T(8,128)(2,1)S(1)}, bf16[4,112,256]{2,1,0:T(8,128)(2,1)S(1)}, u32[]{:S(2)}, u32[]{:S(2)}) collective-permute-start(bf16[4,112,256]{2,1,0:T(8,128)(2,1)S(1)} %slice.71), channel_id=1, source_target_pairs={{0,24},{1,25},{2,26},{3,27},{4,28},{5,29},{6,30},{7,31},{8,0},{9,1... | collective-permute-start | bytes 688136 | tf_op jit(solution)/shard_map/ppermute | solution.py:170
  241.5 2.9 copy-start.2
  249.4 1.2 copy-start.3
  250.7 3.9 %collective-permute-start.20 = (f32[4,112,256]{2,1,0:T(8,128)S(1)}, f32[4,112,256]{2,1,0:T(8,128)S(1)}, u32[]{:S(2)}, u32[]{:S(2)}) collective-permute-start(f32[4,112,256]{2,1,0:T(8,128)S(1)} %slice_bitcast_fusion), channel_id=1, source_target_pairs={{0,1},{1,0},{2,3},{3,2},{4,5},{5,4},{6,7},{7,6},{8,9},{9,8},{10,11... | collective-permute-start | bytes 1376264 | tf_op jit(solution)/shard_map/ppermute | solution.py:170
  262.9 2.1 collective-permute-start.21
  283.6 3.2 collective-permute-start.22
  323.4 5.2 %collective-permute-start.23 = (f32[5,128,128]{2,1,0:T(8,128)S(1)}, f32[5,128,128]{2,1,0:T(8,128)S(1)}, u32[]{:S(2)}, u32[]{:S(2)}) collective-permute-start(f32[5,128,128]{2,1,0:T(8,128)S(1)} %bitcast.31), channel_id=1, source_target_pairs={{0,1},{1,0},{2,3},{3,2},{4,5},{5,4},{6,7},{7,6},{8,9},{9,8},{10,11... | collective-permute-start | bytes 983048 | tf_op jit(solution)/shard_map/ppermute | solution.py:170
Sparse Core Ops, SparseCore 0:
  48.1 36.6 all-gather.2
  221.5 29.2 all-gather.4

commit v5 on v4

--- a/solution.py
+++ b/solution.py
@@ -14,7 +14,7 @@
 AXES = ("z", "y", "x", "core")
 SIZES = (8, 4, 4, 2)
 HALF = K // 2
-FEW = 256
+FEW = 128
 ROWS = M // 256
 
 
@@ -211,11 +211,9 @@
     return chunk // 4, chunk % 4, z // 2, z % 2
 
 
-def gathered_rows(rows):
-    own = permute(rows, chunk_place)
-    many, few = gather_y_small(own[:, FEW:]), exchange(copies(own[:, :FEW], "z"), "z")
+def gathered_rows(few, many):
     many, few = lax.optimization_barrier((many, few))
-    return lax.all_gather(many, "z", axis=0, tiled=True), gather_y(few)
+    return lax.all_gather(many, "z", axis=0, tiled=True), gather_y(exchange(copies(few, "z"), "z"))
 
 
 def few_step(place, a_ref, *refs):
@@ -331,9 +329,9 @@
     )(place, *operands)
 
 
-def summed_product(factor, rows, keep):
+def summed_product(factor, few, many, keep):
     place = core_place()
-    many, pieces = gathered_rows(rows)
+    many, pieces = gathered_rows(few, many)
     both, ordered = product_few(factor, pieces)
     few = both[1] + permute(both[0], other_core)
     many, few = lax.optimization_barrier((many, few))
@@ -342,21 +340,26 @@
     return summed_gram(place, exchange(total, "x")), rest
 
 
-def gram_inverse(packed):
+def gram_inverse(packed, moved=None):
     share = packed[1] + permute(packed[0], other_core)
     share = jnp.sum(exchange(share.reshape(16, 5 * B // 16, B), ("y", "x")), axis=0)
+    share, moved = lax.optimization_barrier((share, moved))
     share = jnp.sum(exchange(copies(share, "z"), "z"), axis=0)
     share = exchange(copies(share, ("y", "x")), ("y", "x")).reshape(5, B, B)
-    return inverse_factor(core_place(), share, permute(share, other_core))
+    return inverse_factor(core_place(), share, permute(share, other_core)), moved
 
 
 def shards(factor, basis):
     scale = math.sqrt(M)
-    own = lax.dynamic_slice_in_dim(basis, lax.axis_index(("x", "core")) * ROWS, ROWS, 0)
-    (first, packed), _ = summed_product(factor, own, False)
-    middle = (dot(first, gram_inverse(packed), 1, 1) * scale).astype(jnp.bfloat16)
-    (second, packed), (column_basis,) = summed_product(factor, middle, True)
-    return dot(second, gram_inverse(packed), 1, 1) * scale, column_basis
+    rows = lax.dynamic_slice_in_dim(basis, lax.axis_index(("x", "core")) * ROWS, ROWS, 0)
+    own = permute(rows, chunk_place)
+    (first, packed), _ = summed_product(factor, own[:, :FEW], gather_y_small(own[:, FEW:]), False)
+    inverse, moved = gram_inverse(packed, permute(first, chunk_place))
+    middle = (dot(gather_y_small(moved), inverse, 1, 1) * scale).astype(jnp.bfloat16)
+    own = lax.dynamic_slice_in_dim(middle, lax.axis_index("y") * ROWS, ROWS, 0)
+    (second, packed), (column_basis,) = summed_product(factor, own[:, :FEW], middle[:, FEW:], True)
+    inverse, _ = gram_inverse(packed)
+    return dot(second, inverse, 1, 1) * scale, column_basis
 
 
 def solution(mesh):

time: 358 us -> 353 us (0.986)
  waiting for transfers between devices: 79.2 us -> 52.3 us
  blocking collectives: 106 us -> 130 us
    all_to_all x8, blocking collectives: 106 us -> 130 us  [exchange(): return lax.all_to_all(pieces, axes, 0, 0, tiled=True)]
    ppermute x24, waiting for transfers between devices: 65 us -> 44.4 us  [permute(): lax.ppermute(values, AXES, [(index[p], index[where(*p)]) for p in places])]
    all_to_all x2, starting transfers between devices: 25.3 us -> 10.5 us  [exchange(): return lax.all_to_all(pieces, axes, 0, 0, tiled=True)]
    ppermute x24, starting transfers between devices: 49.3 us -> 61.6 us  [permute(): lax.ppermute(values, AXES, [(index[p], index[where(*p)]) for p in places])]
    all_to_all x2, waiting for transfers between devices: 12.7 us -> 7.86 us  [exchange(): return lax.all_to_all(pieces, axes, 0, 0, tiled=True)]
    unnamed x12 -> x10, local copies, waits for them, and re-layouts: 8.1 us -> 8.58 us
  transfers between devices with their start and end apart: 28 -> 28, of which waited for: 24 -> 20; matrix products, arithmetic and copies ran while one was open for 0% -> 0% of each run, Pallas kernels for 3% -> 3%
where the time goes in v5:
time: 353 us
  blocking collectives  130 us (37%)
  starting transfers between devices  72.2 us (20%)
  Pallas kernels  66 us (19%)
  waiting for transfers between devices  52.3 us (15%)
  between operations  14.5 us (4%)
  local copies, waits for them, and re-layouts  10.6 us (3%)
  other arithmetic  3.59 us (1%)
    all_to_all x8, blocking collectives, exchange(): return lax.all_to_all(pieces, axes, 0, 0, tiled=True)  130 us
    ppermute x24, starting transfers between devices, permute(): lax.ppermute(values, AXES, [(index[p], index[where(*p)]) for p in places])  61.6 us
    ppermute x24, waiting for transfers between devices, permute(): lax.ppermute(values, AXES, [(index[p], index[where(*p)]) for p in places])  44.4 us
    pallas_call x2, Pallas kernels, inverse_factor(): pl.pallas_call(chol_inverse, out_shape=jax.ShapeDtypeStruct((K, K), jnp.f...  40.1 us
    pallas_call x2, Pallas kernels, product_many(): pl.pallas_call(many_step, out_shape=[part, part] + [jax.ShapeDtypeStruct(...  14.3 us
    all_to_all x2, starting transfers between devices, exchange(): return lax.all_to_all(pieces, axes, 0, 0, tiled=True)  10.5 us
    pallas_call x2, Pallas kernels, product_few(): pl.pallas_call(few_step, out_shape=[jax.ShapeDtypeStruct((2, 4, ROWS, FEW...  10.1 us
    unnamed x10, local copies, waits for them, and re-layouts  8.58 us
  transfers between devices with their start and end apart: 28, of which 20 were waited for; matrix products, arithmetic and copies ran while one was open for 0% of the time, Pallas kernels for 3%

profile of v5, /device:TPU:1, one launch (start us, length us, event | category | flops | bytes accessed | tf_op | source)
XLA Modules:
  0.0 352.5 jit_solution(4012429659073342722)
XLA Ops:
  8.4 4.6 %collective-permute-start = (bf16[112,512]{1,0:T(8,128)(2,1)S(1)}, bf16[112,512]{1,0:T(8,128)(2,1)S(1)}, u32[]{:S(2)}, u32[]{:S(2)}) collective-permute-start(bf16[112,512]{1,0:T(8,128)(2,1)S(1)} %constant_dynamic-slice_fusion.1), channel_id=1, source_target_pairs={{0,0},{1,8},{2,16},{3,24},{4,32},{5,40},{6,48},{7,56},{8,64},{9,72... | collective-permute-start | bytes 344072 | tf_op jit(solution)/shard_map/ppermute | solution.py:170
  13.0 8.8 %collective-permute-done = bf16[112,512]{1,0:T(8,128)(2,1)S(1)} collective-permute-done((bf16[112,512]{1,0:T(8,128)(2,1)S(1)}, bf16[112,512]{1,0:T(8,128)(2,1)S(1)}, u32[]{:S(2)}, u32[]{:S(2)}) %collective-permute-start) | collective-permute-done | bytes 114720 | tf_op jit(solution)/shard_map/ppermute | solution.py:170
  21.9 4.4 %collective-permute-start.1 = (bf16[112,384]{1,0:T(8,128)(2,1)S(1)}, bf16[112,384]{1,0:T(8,128)(2,1)S(1)}, u32[]{:S(2)}, u32[]{:S(2)}) collective-permute-start(bf16[112,384]{1,0:T(8,128)(2,1)S(1)} %get-tuple-element.46), channel_id=1, source_target_pairs={{0,24},{1,25},{2,26},{3,27},{4,28},{5,29},{6,30},{7,31},{8,0},{9,1... | collective-permute-start | bytes 258056 | tf_op jit(solution)/shard_map/ppermute | solution.py:170
  29.9 1.7 collective-permute-done.2
  31.6 2.5 collective-permute-done.3
  34.9 20.3 %all_to_all.50.refs_0_ = bf16[8,112,128]{2,1,0:T(8,128)(2,1)S(1)} all-to-all(bf16[8,112,128]{2,1,0:T(8,128)(2,1)S(1)} %broadcast_in_dim.18), channel_id=1, replica_groups=mesh['z'=8,'y'=4,'x'=4,'core'=2] {'z'}, dimensions={0} | all-to-all | bytes 458752 | tf_op jit(solution)/shard_map/all_to_all | solution.py:178
  55.2 2.7 collective-permute-start.4
  57.9 3.8 %collective-permute-done.5.refs_3_ = bf16[8,112,128]{2,1,0:T(8,128)(2,1)S(1)} collective-permute-done((bf16[8,112,128]{2,1,0:T(8,128)(2,1)S(1)}, bf16[8,112,128]{2,1,0:T(8,128)(2,1)S(1)}, u32[]{:S(2)}, u32[]{:S(2)}) %collective-permute-start.5) | collective-permute-done | bytes 229408 | tf_op jit(solution)/shard_map/ppermute | solution.py:170
  61.8 2.7 collective-permute-start.7
  64.6 2.6 collective-permute-done.6
  67.3 2.9 copy-done.1
  70.2 5.5 %shard_map.41 = (f32[2,4,112,128]{3,2,1,0:T(8,128)S(1)}, bf16[8,4,112,128]{3,2,1,0:T(8,128)(2,1)}) custom-call(s32[2]{0:T(128)S(1)} %pad_add_fusion.place, bf16[4,2,112,3584]{3,2,1,0:T(8,128)(2,1)S(1)} %bitcast.28, bf16[8,112,128]{2,1,0:T(8,128)(2,1)S(1)} %all_to_all.50.refs_0_, bf16[8,112,128]{2,1,0:T(8,128)(2,1)S(1)} %collective-permute-done.4.refs_1_, ...), custom_call_target="tpu_custom_call" | custom-call | flops 822083584 | bytes 8388608 | tf_op jit(solution)/shard_map/pallas_call | solution.py:243
  75.7 5.7 %collective-permute-start.8 = (f32[4,112,128]{2,1,0:T(8,128)S(1)}, f32[4,112,128]{2,1,0:T(8,128)S(1)}, u32[]{:S(2)}, u32[]{:S(2)}) collective-permute-start(f32[4,112,128]{2,1,0:T(8,128)S(1)} %slice_bitcast_fusion.3), channel_id=1, source_target_pairs={{0,1},{1,0},{2,3},{3,2},{4,5},{5,4},{6,7},{7,6},{8,9},{9,8},{10,11... | collective-permute-start | bytes 688136 | tf_op jit(solution)/shard_map/ppermute | solution.py:170
  82.5 6.4 %shard_map.42 = (f32[4,112,384]{2,1,0:T(8,128)}, f32[4,112,384]{2,1,0:T(8,128)}) custom-call(s32[1]{0:T(128)} %bitcast.place, bf16[896,3584]{1,0:T(8,128)(2,1)} %a_ref.3, bf16[3584,384]{1,0:T(8,128)(2,1)} %all-gather.3.cloned.1.call-done.b_ref), custom_call_target="tpu_custom_call" | custom-call | flops 2466250752 | bytes 12582912 | tf_op jit(solution)/shard_map/pallas_call | solution.py:314
  88.9 2.0 collective-permute-start.9
  90.9 2.0 collective-permute-done.9
  94.2 16.1 %all_to_all.51.parts_ref = f32[4,112,512]{2,1,0:T(8,128)S(1)} all-to-all(f32[4,112,512]{2,1,0:T(8,128)S(1)} %pad_maximum_fusion), channel_id=1, replica_groups=mesh['z'=8,'y'=4,'x'=4,'core'=2] {'x'}, dimensions={0} | all-to-all | bytes 1835008 | tf_op jit(solution)/shard_map/all_to_all | solution.py:178
  111.1 1.9 collective-permute-start.10
  115.0 4.7 %all-to-all-start.2 = ((f32[16,40,128]{2,1,0:T(8,128)}), f32[16,40,128]{2,1,0:T(8,128)S(1)}, u32[]{:S(2)}, u32[]{:S(2)}) async-start(f32[16,40,128]{2,1,0:T(8,128)} %bitcast.7), calls=%async_computation.2 | async-start | bytes 655360 | tf_op jit(solution)/shard_map/all_to_all | solution.py:178
  119.8 4.1 %collective-permute-start.11 = (f32[112,512]{1,0:T(8,128)S(1)}, f32[112,512]{1,0:T(8,128)S(1)}, u32[]{:S(2)}, u32[]{:S(2)}) collective-permute-start(f32[112,512]{1,0:T(8,128)S(1)} %get-tuple-element.32), channel_id=1, source_target_pairs={{0,0},{1,8},{2,16},{3,24},{4,32},{5,40},{6,48},{7,56},{8,64},{9,72... | collective-permute-start | bytes 688136 | tf_op jit(solution)/shard_map/ppermute | solution.py:170
  123.8 4.7 %all-to-all-done.2 = f32[16,40,128]{2,1,0:T(8,128)S(1)} async-done(((f32[16,40,128]{2,1,0:T(8,128)}), f32[16,40,128]{2,1,0:T(8,128)S(1)}, u32[]{:S(2)}, u32[]{:S(2)}) %all-to-all-start.2) | async-done | bytes 327712 | tf_op jit(solution)/shard_map/all_to_all | solution.py:178
  128.6 5.8 %collective-permute-done.11 = f32[112,512]{1,0:T(8,128)S(1)} collective-permute-done((f32[112,512]{1,0:T(8,128)S(1)}, f32[112,512]{1,0:T(8,128)S(1)}, u32[]{:S(2)}, u32[]{:S(2)}) %collective-permute-start.11) | collective-permute-done | bytes 229408 | tf_op jit(solution)/shard_map/ppermute | solution.py:170
  134.4 30.8 %all_to_all.52 = f32[8,40,128]{2,1,0:T(8,128)S(1)} all-to-all(f32[8,40,128]{2,1,0:T(8,128)S(1)} %broadcast_in_dim.19), channel_id=1, replica_groups=mesh['z'=8,'y'=4,'x'=4,'core'=2] {'z'}, dimensions={0} | all-to-all | bytes 327680 | tf_op jit(solution)/shard_map/all_to_all | solution.py:178
  166.0 5.8 %all-to-all-start.4 = ((f32[16,40,128]{2,1,0:T(8,128)}), f32[16,40,128]{2,1,0:T(8,128)S(1)}, u32[]{:S(2)}, u32[]{:S(2)}) async-start(f32[16,40,128]{2,1,0:T(8,128)} %broadcast_in_dim.20), calls=%async_computation.4 | async-start | bytes 655360 | tf_op jit(solution)/shard_map/all_to_all | solution.py:178
  171.9 2.8 collective-permute-start.12
  174.7 1.8 collective-permute-start.13
  176.6 3.1 all-to-all-done.4
  179.7 6.1 %collective-permute-start.15 = (f32[5,128,128]{2,1,0:T(8,128)S(1)}, f32[5,128,128]{2,1,0:T(8,128)S(1)}, u32[]{:S(2)}, u32[]{:S(2)}) collective-permute-start(f32[5,128,128]{2,1,0:T(8,128)S(1)} %bitcast.30), channel_id=1, source_target_pairs={{0,1},{1,0},{2,3},{3,2},{4,5},{5,4},{6,7},{7,6},{8,9},{9,8},{10,11... | collective-permute-start | bytes 983048 | tf_op jit(solution)/shard_map/ppermute | solution.py:170
  187.1 20.1 %shard_map.44 = f32[512,512]{1,0:T(8,128)S(1)} custom-call(s32[1]{0:T(128)} %bitcast.place, f32[5,128,128]{2,1,0:T(8,128)S(1)} %bitcast.31, f32[5,128,128]{2,1,0:T(8,128)S(1)} %collective-permute-done.15.came_ref), custom_call_target="tpu_custom_call" | custom-call | flops 268435456 | bytes 2097152 | tf_op jit(solution)/shard_map/pallas_call | solution.py:156
  207.1 1.7 fusion
  209.7 11.4 %all_to_all.53.refs_0_ = bf16[8,112,128]{2,1,0:T(8,128)(2,1)S(1)} all-to-all(bf16[8,112,128]{2,1,0:T(8,128)(2,1)S(1)} %broadcast_in_dim.21), channel_id=1, replica_groups=mesh['z'=8,'y'=4,'x'=4,'core'=2] {'z'}, dimensions={0} | all-to-all | bytes 458752 | tf_op jit(solution)/shard_map/all_to_all | solution.py:178
  221.0 2.7 collective-permute-start.16
  223.7 3.8 %collective-permute-done.17.refs_3_ = bf16[8,112,128]{2,1,0:T(8,128)(2,1)S(1)} collective-permute-done((bf16[8,112,128]{2,1,0:T(8,128)(2,1)S(1)}, bf16[8,112,128]{2,1,0:T(8,128)(2,1)S(1)}, u32[]{:S(2)}, u32[]{:S(2)}) %collective-permute-start.17) | collective-permute-done | bytes 229408 | tf_op jit(solution)/shard_map/ppermute | solution.py:170
  227.7 2.7 collective-permute-start.19
  230.4 2.7 collective-permute-done.18
  233.1 2.9 copy-done.2
  236.0 4.6 %shard_map.45 = (f32[2,4,112,128]{3,2,1,0:T(8,128)S(1)}, bf16[8,4,112,128]{3,2,1,0:T(8,128)(2,1)S(1)}) custom-call(s32[2]{0:T(128)S(1)} %pad_add_fusion.place, bf16[4,2,112,3584]{3,2,1,0:T(8,128)(2,1)S(1)} %bitcast.29, bf16[8,112,128]{2,1,0:T(8,128)(2,1)S(1)} %all_to_all.53.refs_0_, bf16[8,112,128]{2,1,0:T(8,128)(2,1)S(1)} %collective-permute-done.16.refs_1_, ...), custom_call_target="tpu_custom_call" | custom-call | flops 822083584 | bytes 8388608 | tf_op jit(solution)/shard_map/pallas_call | solution.py:243
  241.6 8.9 %collective-permute-start.20 = (f32[4,112,128]{2,1,0:T(8,128)S(1)}, f32[4,112,128]{2,1,0:T(8,128)S(1)}, u32[]{:S(2)}, u32[]{:S(2)}) collective-permute-start(f32[4,112,128]{2,1,0:T(8,128)S(1)} %slice_bitcast_fusion.2), channel_id=1, source_target_pairs={{0,1},{1,0},{2,3},{3,2},{4,5},{5,4},{6,7},{7,6},{8,9},{9,8},{10,11... | collective-permute-start | bytes 688136 | tf_op jit(solution)/shard_map/ppermute | solution.py:170
  251.6 8.0 %shard_map.46 = (f32[4,112,384]{2,1,0:T(8,128)}, f32[4,112,384]{2,1,0:T(8,128)}, bf16[3584,512]{1,0:T(8,128)(2,1)}) custom-call(s32[1]{0:T(128)} %bitcast.place, bf16[896,3584]{1,0:T(8,128)(2,1)} %a_ref.3, bf16[3584,384]{1,0:T(8,128)(2,1)} %all-gather.5.cloned.1.call-done.b_ref, bf16[3584,128]{1,0:T(8,128)(2,1)} %bitcast.34), custom_call_target="tpu_custom_call" | custom-call | flops 2466250752 | bytes 12582912 | tf_op jit(solution)/shard_map/pallas_call | solution.py:314
  260.1 2.0 collective-permute-done.21
  263.4 15.7 %all_to_all.54.parts_ref = f32[4,112,512]{2,1,0:T(8,128)S(1)} all-to-all(f32[4,112,512]{2,1,0:T(8,128)S(1)} %pad_maximum_fusion.1), channel_id=1, replica_groups=mesh['z'=8,'y'=4,'x'=4,'core'=2] {'x'}, dimensions={0} | all-to-all | bytes 1835008 | tf_op jit(solution)/shard_map/all_to_all | solution.py:178
  279.9 1.9 collective-permute-start.22
  283.1 13.4 %all_to_all.55 = f32[16,40,128]{2,1,0:T(8,128)S(1)} all-to-all(f32[16,40,128]{2,1,0:T(8,128)S(1)} %bitcast.35), channel_id=1, replica_groups=mesh['z'=8,'y'=4,'x'=4,'core'=2] {'y','x'}, dimensions={0} | all-to-all | bytes 655360 | tf_op jit(solution)/shard_map/all_to_all | solution.py:178
  296.5 11.1 %all_to_all.56 = f32[8,40,128]{2,1,0:T(8,128)S(1)} all-to-all(f32[8,40,128]{2,1,0:T(8,128)S(1)} %broadcast_in_dim.22), channel_id=1, replica_groups=mesh['z'=8,'y'=4,'x'=4,'core'=2] {'z'}, dimensions={0} | all-to-all | bytes 327680 | tf_op jit(solution)/shard_map/all_to_all | solution.py:178
  307.7 10.9 %all_to_all.57 = f32[16,40,128]{2,1,0:T(8,128)S(1)} all-to-all(f32[16,40,128]{2,1,0:T(8,128)S(1)} %broadcast_in_dim.23), channel_id=1, replica_groups=mesh['z'=8,'y'=4,'x'=4,'core'=2] {'y','x'}, dimensions={0} | all-to-all | bytes 655360 | tf_op jit(solution)/shard_map/all_to_all | solution.py:178
  318.6 3.9 %collective-permute-start.23 = (f32[5,128,128]{2,1,0:T(8,128)S(1)}, f32[5,128,128]{2,1,0:T(8,128)S(1)}, u32[]{:S(2)}, u32[]{:S(2)}) collective-permute-start(f32[5,128,128]{2,1,0:T(8,128)S(1)} %bitcast.32), channel_id=1, source_target_pairs={{0,1},{1,0},{2,3},{3,2},{4,5},{5,4},{6,7},{7,6},{8,9},{9,8},{10,11... | collective-permute-start | bytes 983048 | tf_op jit(solution)/shard_map/ppermute | solution.py:170
  323.8 20.0 %shard_map.48 = f32[512,512]{1,0:T(8,128)S(1)} custom-call(s32[1]{0:T(128)} %bitcast.place, f32[5,128,128]{2,1,0:T(8,128)S(1)} %bitcast.33, f32[5,128,128]{2,1,0:T(8,128)S(1)} %collective-permute-done.23.came_ref), custom_call_target="tpu_custom_call" | custom-call | flops 268435456 | bytes 2097152 | tf_op jit(solution)/shard_map/pallas_call | solution.py:156
  343.8 1.9 convolution_multiply_fusion.1
  (81 shorter events, 21.5 us)
Async XLA Ops:
  7.2 1.2 copy-start
  7.2 75.3 %all-gather.3.cloned.1.call-start = ((), (), s32[]{:S(2)}) async-start(), calls=%async_computation.10 | async-start | bytes 3096576 | tf_op jit(solution)/shard_map/all_gather | solution.py:216
  8.4 13.4 %collective-permute-start = (bf16[112,512]{1,0:T(8,128)(2,1)S(1)}, bf16[112,512]{1,0:T(8,128)(2,1)S(1)}, u32[]{:S(2)}, u32[]{:S(2)}) collective-permute-start(bf16[112,512]{1,0:T(8,128)(2,1)S(1)} %constant_dynamic-slice_fusion.1), channel_id=1, source_target_pairs={{0,0},{1,8},{2,16},{3,24},{4,32},{5,40},{6,48},{7,56},{8,64},{9,72... | collective-permute-start | bytes 344072 | tf_op jit(solution)/shard_map/ppermute | solution.py:170
  21.9 8.0 %collective-permute-start.1 = (bf16[112,384]{1,0:T(8,128)(2,1)S(1)}, bf16[112,384]{1,0:T(8,128)(2,1)S(1)}, u32[]{:S(2)}, u32[]{:S(2)}) collective-permute-start(bf16[112,384]{1,0:T(8,128)(2,1)S(1)} %get-tuple-element.46), channel_id=1, source_target_pairs={{0,24},{1,25},{2,26},{3,27},{4,28},{5,29},{6,30},{7,31},{8,0},{9,1... | collective-permute-start | bytes 258056 | tf_op jit(solution)/shard_map/ppermute | solution.py:170
  26.2 5.3 %collective-permute-start.2 = (bf16[112,384]{1,0:T(8,128)(2,1)S(1)}, bf16[112,384]{1,0:T(8,128)(2,1)S(1)}, u32[]{:S(2)}, u32[]{:S(2)}) collective-permute-start(bf16[112,384]{1,0:T(8,128)(2,1)S(1)} %get-tuple-element.46), channel_id=1, source_target_pairs={{0,16},{1,17},{2,18},{3,19},{4,20},{5,21},{6,22},{7,23},{8,24},{9,... | collective-permute-start | bytes 258056 | tf_op jit(solution)/shard_map/ppermute | solution.py:170
  27.6 6.5 %collective-permute-start.3 = (bf16[112,384]{1,0:T(8,128)(2,1)S(1)}, bf16[112,384]{1,0:T(8,128)(2,1)S(1)}, u32[]{:S(2)}, u32[]{:S(2)}) collective-permute-start(bf16[112,384]{1,0:T(8,128)(2,1)S(1)} %get-tuple-element.46), channel_id=1, source_target_pairs={{0,8},{1,9},{2,10},{3,11},{4,12},{5,13},{6,14},{7,15},{8,16},{9,17... | collective-permute-start | bytes 258056 | tf_op jit(solution)/shard_map/ppermute | solution.py:170
  34.1 0.7 copy-start.4
  55.2 6.5 %collective-permute-start.5 = (bf16[8,112,128]{2,1,0:T(8,128)(2,1)S(1)}, bf16[8,112,128]{2,1,0:T(8,128)(2,1)S(1)}, u32[]{:S(2)}, u32[]{:S(2)}) collective-permute-start(bf16[8,112,128]{2,1,0:T(8,128)(2,1)S(1)} %all_to_all.50.refs_0_), channel_id=1, source_target_pairs={{0,8},{1,9},{2,10},{3,11},{4,12},{5,13},{6,14},{7,15},{8,16},{9,17... | collective-permute-start | bytes 688136 | tf_op jit(solution)/shard_map/ppermute | solution.py:170
  55.2 6.6 %collective-permute-start.4 = (bf16[8,112,128]{2,1,0:T(8,128)(2,1)S(1)}, bf16[8,112,128]{2,1,0:T(8,128)(2,1)S(1)}, u32[]{:S(2)}, u32[]{:S(2)}) collective-permute-start(bf16[8,112,128]{2,1,0:T(8,128)(2,1)S(1)} %all_to_all.50.refs_0_), channel_id=1, source_target_pairs={{0,24},{1,25},{2,26},{3,27},{4,28},{5,29},{6,30},{7,31},{8,0},{9,1... | collective-permute-start | bytes 688136 | tf_op jit(solution)/shard_map/ppermute | solution.py:170
  61.7 5.5 %collective-permute-start.6 = (bf16[4,112,128]{2,1,0:T(8,128)(2,1)S(1)}, bf16[4,112,128]{2,1,0:T(8,128)(2,1)S(1)}, u32[]{:S(2)}, u32[]{:S(2)}) collective-permute-start(bf16[4,112,128]{2,1,0:T(8,128)(2,1)S(1)} %slice.66), channel_id=1, source_target_pairs={{0,8},{1,9},{2,10},{3,11},{4,12},{5,13},{6,14},{7,15},{8,16},{9,17... | collective-permute-start | bytes 344072 | tf_op jit(solution)/shard_map/ppermute | solution.py:170
  61.8 5.4 %collective-permute-start.7 = (bf16[4,112,128]{2,1,0:T(8,128)(2,1)S(1)}, bf16[4,112,128]{2,1,0:T(8,128)(2,1)S(1)}, u32[]{:S(2)}, u32[]{:S(2)}) collective-permute-start(bf16[4,112,128]{2,1,0:T(8,128)(2,1)S(1)} %slice.67), channel_id=1, source_target_pairs={{0,24},{1,25},{2,26},{3,27},{4,28},{5,29},{6,30},{7,31},{8,0},{9,1... | collective-permute-start | bytes 344072 | tf_op jit(solution)/shard_map/ppermute | solution.py:170
  67.2 2.9 copy-start.1
  75.7 6.8 %collective-permute-start.8 = (f32[4,112,128]{2,1,0:T(8,128)S(1)}, f32[4,112,128]{2,1,0:T(8,128)S(1)}, u32[]{:S(2)}, u32[]{:S(2)}) collective-permute-start(f32[4,112,128]{2,1,0:T(8,128)S(1)} %slice_bitcast_fusion.3), channel_id=1, source_target_pairs={{0,1},{1,0},{2,3},{3,2},{4,5},{5,4},{6,7},{7,6},{8,9},{9,8},{10,11... | collective-permute-start | bytes 688136 | tf_op jit(solution)/shard_map/ppermute | solution.py:170
  88.9 4.0 %collective-permute-start.9 = (f32[4,112,384]{2,1,0:T(8,128)}, f32[4,112,384]{2,1,0:T(8,128)S(1)}, u32[]{:S(2)}, u32[]{:S(2)}) collective-permute-start(f32[4,112,384]{2,1,0:T(8,128)} %get-tuple-element.30), channel_id=1, source_target_pairs={{0,1},{1,0},{2,3},{3,2},{4,5},{5,4},{6,7},{7,6},{8,9},{9,8},{10,11... | collective-permute-start | bytes 2064392 | tf_op jit(solution)/shard_map/ppermute | solution.py:170
  111.1 3.2 collective-permute-start.10
  115.0 13.5 %all-to-all-start.2 = ((f32[16,40,128]{2,1,0:T(8,128)}), f32[16,40,128]{2,1,0:T(8,128)S(1)}, u32[]{:S(2)}, u32[]{:S(2)}) async-start(f32[16,40,128]{2,1,0:T(8,128)} %bitcast.7), calls=%async_computation.2 | async-start | bytes 655360 | tf_op jit(solution)/shard_map/all_to_all | solution.py:178
  119.8 14.6 %collective-permute-start.11 = (f32[112,512]{1,0:T(8,128)S(1)}, f32[112,512]{1,0:T(8,128)S(1)}, u32[]{:S(2)}, u32[]{:S(2)}) collective-permute-start(f32[112,512]{1,0:T(8,128)S(1)} %get-tuple-element.32), channel_id=1, source_target_pairs={{0,0},{1,8},{2,16},{3,24},{4,32},{5,40},{6,48},{7,56},{8,64},{9,72... | collective-permute-start | bytes 688136 | tf_op jit(solution)/shard_map/ppermute | solution.py:170
  166.0 13.7 %all-to-all-start.4 = ((f32[16,40,128]{2,1,0:T(8,128)}), f32[16,40,128]{2,1,0:T(8,128)S(1)}, u32[]{:S(2)}, u32[]{:S(2)}) async-start(f32[16,40,128]{2,1,0:T(8,128)} %broadcast_in_dim.20), calls=%async_computation.4 | async-start | bytes 655360 | tf_op jit(solution)/shard_map/all_to_all | solution.py:178
  171.8 79.8 %all-gather.5.cloned.1.call-start = ((), (), s32[]{:S(2)}) async-start(), calls=%async_computation.11 | async-start | bytes 3096576 | tf_op jit(solution)/shard_map/all_gather | solution.py:216
  171.9 14.0 %collective-permute-start.12 = (f32[112,512]{1,0:T(8,128)S(1)}, f32[112,512]{1,0:T(8,128)S(1)}, u32[]{:S(2)}, u32[]{:S(2)}) collective-permute-start(f32[112,512]{1,0:T(8,128)S(1)} %collective-permute-done.11), channel_id=1, source_target_pairs={{0,24},{1,25},{2,26},{3,27},{4,28},{5,29},{6,30},{7,31},{8,0},{9,1... | collective-permute-start | bytes 688136 | tf_op jit(solution)/shard_map/ppermute | solution.py:170
  174.7 11.9 %collective-permute-start.14 = (f32[112,512]{1,0:T(8,128)S(1)}, f32[112,512]{1,0:T(8,128)S(1)}, u32[]{:S(2)}, u32[]{:S(2)}) collective-permute-start(f32[112,512]{1,0:T(8,128)S(1)} %collective-permute-done.11), channel_id=1, source_target_pairs={{0,8},{1,9},{2,10},{3,11},{4,12},{5,13},{6,14},{7,15},{8,16},{9,17... | collective-permute-start | bytes 688136 | tf_op jit(solution)/shard_map/ppermute | solution.py:170
  174.7 11.9 %collective-permute-start.13 = (f32[112,512]{1,0:T(8,128)S(1)}, f32[112,512]{1,0:T(8,128)S(1)}, u32[]{:S(2)}, u32[]{:S(2)}) collective-permute-start(f32[112,512]{1,0:T(8,128)S(1)} %collective-permute-done.11), channel_id=1, source_target_pairs={{0,16},{1,17},{2,18},{3,19},{4,20},{5,21},{6,22},{7,23},{8,24},{9,... | collective-permute-start | bytes 688136 | tf_op jit(solution)/shard_map/ppermute | solution.py:170
  179.7 7.3 %collective-permute-start.15 = (f32[5,128,128]{2,1,0:T(8,128)S(1)}, f32[5,128,128]{2,1,0:T(8,128)S(1)}, u32[]{:S(2)}, u32[]{:S(2)}) collective-permute-start(f32[5,128,128]{2,1,0:T(8,128)S(1)} %bitcast.30), channel_id=1, source_target_pairs={{0,1},{1,0},{2,3},{3,2},{4,5},{5,4},{6,7},{7,6},{8,9},{9,8},{10,11... | collective-permute-start | bytes 983048 | tf_op jit(solution)/shard_map/ppermute | solution.py:170
  221.0 6.5 %collective-permute-start.17 = (bf16[8,112,128]{2,1,0:T(8,128)(2,1)S(1)}, bf16[8,112,128]{2,1,0:T(8,128)(2,1)S(1)}, u32[]{:S(2)}, u32[]{:S(2)}) collective-permute-start(bf16[8,112,128]{2,1,0:T(8,128)(2,1)S(1)} %all_to_all.53.refs_0_), channel_id=1, source_target_pairs={{0,8},{1,9},{2,10},{3,11},{4,12},{5,13},{6,14},{7,15},{8,16},{9,17... | collective-permute-start | bytes 688136 | tf_op jit(solution)/shard_map/ppermute | solution.py:170
  221.0 6.6 %collective-permute-start.16 = (bf16[8,112,128]{2,1,0:T(8,128)(2,1)S(1)}, bf16[8,112,128]{2,1,0:T(8,128)(2,1)S(1)}, u32[]{:S(2)}, u32[]{:S(2)}) collective-permute-start(bf16[8,112,128]{2,1,0:T(8,128)(2,1)S(1)} %all_to_all.53.refs_0_), channel_id=1, source_target_pairs={{0,24},{1,25},{2,26},{3,27},{4,28},{5,29},{6,30},{7,31},{8,0},{9,1... | collective-permute-start | bytes 688136 | tf_op jit(solution)/shard_map/ppermute | solution.py:170
  227.5 5.5 %collective-permute-start.18 = (bf16[4,112,128]{2,1,0:T(8,128)(2,1)S(1)}, bf16[4,112,128]{2,1,0:T(8,128)(2,1)S(1)}, u32[]{:S(2)}, u32[]{:S(2)}) collective-permute-start(bf16[4,112,128]{2,1,0:T(8,128)(2,1)S(1)} %slice.69), channel_id=1, source_target_pairs={{0,8},{1,9},{2,10},{3,11},{4,12},{5,13},{6,14},{7,15},{8,16},{9,17... | collective-permute-start | bytes 344072 | tf_op jit(solution)/shard_map/ppermute | solution.py:170
  227.7 5.4 %collective-permute-start.19 = (bf16[4,112,128]{2,1,0:T(8,128)(2,1)S(1)}, bf16[4,112,128]{2,1,0:T(8,128)(2,1)S(1)}, u32[]{:S(2)}, u32[]{:S(2)}) collective-permute-start(bf16[4,112,128]{2,1,0:T(8,128)(2,1)S(1)} %slice.70), channel_id=1, source_target_pairs={{0,24},{1,25},{2,26},{3,27},{4,28},{5,29},{6,30},{7,31},{8,0},{9,1... | collective-permute-start | bytes 344072 | tf_op jit(solution)/shard_map/ppermute | solution.py:170
  233.1 2.9 copy-start.2
  240.6 0.9 copy-start.3
  241.6 10.0 %collective-permute-start.20 = (f32[4,112,128]{2,1,0:T(8,128)S(1)}, f32[4,112,128]{2,1,0:T(8,128)S(1)}, u32[]{:S(2)}, u32[]{:S(2)}) collective-permute-start(f32[4,112,128]{2,1,0:T(8,128)S(1)} %slice_bitcast_fusion.2), channel_id=1, source_target_pairs={{0,1},{1,0},{2,3},{3,2},{4,5},{5,4},{6,7},{7,6},{8,9},{9,8},{10,11... | collective-permute-start | bytes 688136 | tf_op jit(solution)/shard_map/ppermute | solution.py:170
  259.6 2.4 collective-permute-start.21
  279.9 3.2 collective-permute-start.22
  318.6 5.2 %collective-permute-start.23 = (f32[5,128,128]{2,1,0:T(8,128)S(1)}, f32[5,128,128]{2,1,0:T(8,128)S(1)}, u32[]{:S(2)}, u32[]{:S(2)}) collective-permute-start(f32[5,128,128]{2,1,0:T(8,128)S(1)} %bitcast.32), channel_id=1, source_target_pairs={{0,1},{1,0},{2,3},{3,2},{4,5},{5,4},{6,7},{7,6},{8,9},{9,8},{10,11... | collective-permute-start | bytes 983048 | tf_op jit(solution)/shard_map/ppermute | solution.py:170
Sparse Core Ops, SparseCore 0:
  35.0 46.8 all-gather.2
  209.7 39.4 all-gather.4

commit v6 on v5

--- a/solution.py
+++ b/solution.py
@@ -160,7 +160,7 @@
         out_specs=VMEM,
         scratch_shapes=[pltpu.VMEM((K, K), jnp.float32)],
         compiler_params=pltpu.CompilerParams(vmem_limit_bytes=12 * 1024 * 1024),
-        cost_estimate=pl.CostEstimate(flops=2 * K ** 3, bytes_accessed=8 * K * K, transcendentals=0),
+        cost_estimate=pl.CostEstimate(flops=150 * K ** 3, bytes_accessed=8 * K * K, transcendentals=0),
     )(place, own, came)
 
 
@@ -197,11 +197,15 @@
     return [own, after, far, before]
 
 
-def gather_y_small(own):
+def small_pieces(own):
     far = permute(own, lambda z, y, x, c: (z, (y + 2) % 4, x, c))
-    rows = own.shape[0]
-    out = jnp.zeros((4 * rows, own.shape[1]), own.dtype)
-    for step, piece in enumerate([own, permute(own, down), far, permute(own, up)]):
+    return [own, permute(own, down), far, permute(own, up)]
+
+
+def in_order(pieces):
+    rows, width = pieces[0].shape
+    out = jnp.zeros((4 * rows, width), pieces[0].dtype)
+    for step, piece in enumerate(pieces):
         out = lax.dynamic_update_slice_in_dim(out, piece, lax.rem(lax.axis_index("y") + step, 4) * rows, 0)
     return out
 
@@ -343,9 +347,9 @@
 def gram_inverse(packed, moved=None):
     share = packed[1] + permute(packed[0], other_core)
     share = jnp.sum(exchange(share.reshape(16, 5 * B // 16, B), ("y", "x")), axis=0)
-    share, moved = lax.optimization_barrier((share, moved))
     share = jnp.sum(exchange(copies(share, "z"), "z"), axis=0)
     share = exchange(copies(share, ("y", "x")), ("y", "x")).reshape(5, B, B)
+    share, moved = lax.optimization_barrier((share, moved))
     return inverse_factor(core_place(), share, permute(share, other_core)), moved
 
 
@@ -353,9 +357,10 @@
     scale = math.sqrt(M)
     rows = lax.dynamic_slice_in_dim(basis, lax.axis_index(("x", "core")) * ROWS, ROWS, 0)
     own = permute(rows, chunk_place)
-    (first, packed), _ = summed_product(factor, own[:, :FEW], gather_y_small(own[:, FEW:]), False)
+    (first, packed), _ = summed_product(factor, own[:, :FEW], in_order(small_pieces(own[:, FEW:])), False)
     inverse, moved = gram_inverse(packed, permute(first, chunk_place))
-    middle = (dot(gather_y_small(moved), inverse, 1, 1) * scale).astype(jnp.bfloat16)
+    inverse, pieces = lax.optimization_barrier((inverse, small_pieces(moved)))
+    middle = (dot(in_order(pieces), inverse, 1, 1) * scale).astype(jnp.bfloat16)
     own = lax.dynamic_slice_in_dim(middle, lax.axis_index("y") * ROWS, ROWS, 0)
     (second, packed), (column_basis,) = summed_product(factor, own[:, :FEW], middle[:, FEW:], True)
     inverse, _ = gram_inverse(packed)

time: 353 us -> 352 us (level)
  blocking collectives: 130 us -> 138 us
  waiting for transfers between devices: 52.3 us -> 47.1 us
    all_to_all x2 -> x1, waiting for transfers between devices: 7.86 us -> 0.01 us  [exchange(): return lax.all_to_all(pieces, axes, 0, 0, tiled=True)]
    all_to_all x8 -> x9, blocking collectives: 130 us -> 138 us  [exchange(): return lax.all_to_all(pieces, axes, 0, 0, tiled=True)]
    all_to_all x2 -> x1, starting transfers between devices: 10.5 us -> 3.54 us  [exchange(): return lax.all_to_all(pieces, axes, 0, 0, tiled=True)]
    ppermute x24, starting transfers between devices: 61.6 us -> 65.5 us  [permute(): lax.ppermute(values, AXES, [(index[p], index[where(*p)]) for p in places])]
  transfers between devices with their start and end apart: 28 -> 27, of which waited for: 20 -> 17; matrix products, arithmetic and copies ran while one was open for 0% -> 0% of each run, Pallas kernels for 3% -> 9%
where the time goes in v6:
time: 352 us; the launch traced here: 351 us
  blocking collectives  138 us (39%)
  starting transfers between devices  69.1 us (20%)
  Pallas kernels  66 us (19%)
  waiting for transfers between devices  47.1 us (13%)
  between operations  14.5 us (4%)
  local copies, waits for them, and re-layouts  10.6 us (3%)
  matrix products  3.52 us (1%)
    all_to_all x9, blocking collectives, exchange(): return lax.all_to_all(pieces, axes, 0, 0, tiled=True)  138 us
    ppermute x24, starting transfers between devices, permute(): lax.ppermute(values, AXES, [(index[p], index[where(*p)]) for p in places])  65.5 us
    ppermute x24, waiting for transfers between devices, permute(): lax.ppermute(values, AXES, [(index[p], index[where(*p)]) for p in places])  46.9 us
    pallas_call x2, Pallas kernels, inverse_factor(): pl.pallas_call(chol_inverse, out_shape=jax.ShapeDtypeStruct((K, K), jnp.f...  40.1 us
    pallas_call x2, Pallas kernels, product_many(): pl.pallas_call(many_step, out_shape=[part, part] + [jax.ShapeDtypeStruct(...  14.3 us
    pallas_call x2, Pallas kernels, product_few(): pl.pallas_call(few_step, out_shape=[jax.ShapeDtypeStruct((2, 4, ROWS, FEW...  10.1 us
    unnamed x10, local copies, waits for them, and re-layouts  8.56 us
  transfers between devices with their start and end apart: 27, of which 17 were waited for; matrix products, arithmetic and copies ran while one was open for 0% of the time, Pallas kernels for 9%

profile of v6, /device:TPU:1, one launch (start us, length us, event | category | flops | bytes accessed | tf_op | source)
XLA Modules:
  0.0 351.3 jit_solution(7129464769411776248)
XLA Ops:
  8.4 4.6 %collective-permute-start = (bf16[112,512]{1,0:T(8,128)(2,1)S(1)}, bf16[112,512]{1,0:T(8,128)(2,1)S(1)}, u32[]{:S(2)}, u32[]{:S(2)}) collective-permute-start(bf16[112,512]{1,0:T(8,128)(2,1)S(1)} %constant_dynamic-slice_fusion.1), channel_id=1, source_target_pairs={{0,0},{1,8},{2,16},{3,24},{4,32},{5,40},{6,48},{7,56},{8,64},{9,72... | collective-permute-start | bytes 344072 | tf_op jit(solution)/shard_map/ppermute | solution.py:170
  13.0 8.8 %collective-permute-done = bf16[112,512]{1,0:T(8,128)(2,1)S(1)} collective-permute-done((bf16[112,512]{1,0:T(8,128)(2,1)S(1)}, bf16[112,512]{1,0:T(8,128)(2,1)S(1)}, u32[]{:S(2)}, u32[]{:S(2)}) %collective-permute-start) | collective-permute-done | bytes 114720 | tf_op jit(solution)/shard_map/ppermute | solution.py:170
  21.9 4.4 %collective-permute-start.1 = (bf16[112,384]{1,0:T(8,128)(2,1)S(1)}, bf16[112,384]{1,0:T(8,128)(2,1)S(1)}, u32[]{:S(2)}, u32[]{:S(2)}) collective-permute-start(bf16[112,384]{1,0:T(8,128)(2,1)S(1)} %get-tuple-element.56), channel_id=1, source_target_pairs={{0,24},{1,25},{2,26},{3,27},{4,28},{5,29},{6,30},{7,31},{8,0},{9,1... | collective-permute-start | bytes 258056 | tf_op jit(solution)/shard_map/ppermute | solution.py:170
  26.2 1.4 collective-permute-start.2
  28.3 1.5 collective-permute-done.1
  29.9 1.7 collective-permute-done.2
  31.6 2.5 collective-permute-done.3
  34.9 20.3 %all_to_all.50.refs_0_ = bf16[8,112,128]{2,1,0:T(8,128)(2,1)S(1)} all-to-all(bf16[8,112,128]{2,1,0:T(8,128)(2,1)S(1)} %broadcast_in_dim.18), channel_id=1, replica_groups=mesh['z'=8,'y'=4,'x'=4,'core'=2] {'z'}, dimensions={0} | all-to-all | bytes 458752 | tf_op jit(solution)/shard_map/all_to_all | solution.py:178
  55.2 2.7 collective-permute-start.4
  57.9 3.8 %collective-permute-done.5.refs_3_ = bf16[8,112,128]{2,1,0:T(8,128)(2,1)S(1)} collective-permute-done((bf16[8,112,128]{2,1,0:T(8,128)(2,1)S(1)}, bf16[8,112,128]{2,1,0:T(8,128)(2,1)S(1)}, u32[]{:S(2)}, u32[]{:S(2)}) %collective-permute-start.5) | collective-permute-done | bytes 229408 | tf_op jit(solution)/shard_map/ppermute | solution.py:170
  61.8 2.7 collective-permute-start.7
  64.6 2.6 collective-permute-done.6
  67.2 2.9 copy-done.1
  70.1 5.5 %shard_map.41 = (f32[2,4,112,128]{3,2,1,0:T(8,128)S(1)}, bf16[8,4,112,128]{3,2,1,0:T(8,128)(2,1)}) custom-call(s32[2]{0:T(128)S(1)} %pad_add_fusion.place, bf16[4,2,112,3584]{3,2,1,0:T(8,128)(2,1)S(1)} %bitcast.28, bf16[8,112,128]{2,1,0:T(8,128)(2,1)S(1)} %all_to_all.50.refs_0_, bf16[8,112,128]{2,1,0:T(8,128)(2,1)S(1)} %collective-permute-done.4.refs_1_, ...), custom_call_target="tpu_custom_call" | custom-call | flops 822083584 | bytes 8388608 | tf_op jit(solution)/shard_map/pallas_call | solution.py:247
  75.7 5.7 %collective-permute-start.8 = (f32[4,112,128]{2,1,0:T(8,128)S(1)}, f32[4,112,128]{2,1,0:T(8,128)S(1)}, u32[]{:S(2)}, u32[]{:S(2)}) collective-permute-start(f32[4,112,128]{2,1,0:T(8,128)S(1)} %slice_bitcast_fusion.3), channel_id=1, source_target_pairs={{0,1},{1,0},{2,3},{3,2},{4,5},{5,4},{6,7},{7,6},{8,9},{9,8},{10,11... | collective-permute-start | bytes 688136 | tf_op jit(solution)/shard_map/ppermute | solution.py:170
  82.5 6.4 %shard_map.42 = (f32[4,112,384]{2,1,0:T(8,128)}, f32[4,112,384]{2,1,0:T(8,128)}) custom-call(s32[1]{0:T(128)} %bitcast.place, bf16[896,3584]{1,0:T(8,128)(2,1)} %a_ref.3, bf16[3584,384]{1,0:T(8,128)(2,1)} %all-gather.3.cloned.1.call-done.b_ref), custom_call_target="tpu_custom_call" | custom-call | flops 2466250752 | bytes 12582912 | tf_op jit(solution)/shard_map/pallas_call | solution.py:318
  88.9 2.0 collective-permute-start.9
  90.9 2.0 collective-permute-done.9
  94.2 16.1 %all_to_all.51.parts_ref = f32[4,112,512]{2,1,0:T(8,128)S(1)} all-to-all(f32[4,112,512]{2,1,0:T(8,128)S(1)} %pad_maximum_fusion), channel_id=1, replica_groups=mesh['z'=8,'y'=4,'x'=4,'core'=2] {'x'}, dimensions={0} | all-to-all | bytes 1835008 | tf_op jit(solution)/shard_map/all_to_all | solution.py:178
  111.1 1.9 collective-permute-start.10
  114.3 13.3 %all_to_all.52 = f32[16,40,128]{2,1,0:T(8,128)S(1)} all-to-all(f32[16,40,128]{2,1,0:T(8,128)S(1)} %bitcast.35), channel_id=1, replica_groups=mesh['z'=8,'y'=4,'x'=4,'core'=2] {'y','x'}, dimensions={0} | all-to-all | bytes 655360 | tf_op jit(solution)/shard_map/all_to_all | solution.py:178
  127.7 12.0 %all_to_all.53 = f32[8,40,128]{2,1,0:T(8,128)S(1)} all-to-all(f32[8,40,128]{2,1,0:T(8,128)S(1)} %broadcast_in_dim.19), channel_id=1, replica_groups=mesh['z'=8,'y'=4,'x'=4,'core'=2] {'z'}, dimensions={0} | all-to-all | bytes 327680 | tf_op jit(solution)/shard_map/all_to_all | solution.py:178
  140.4 3.5 %all-to-all-start.4 = ((f32[16,40,128]{2,1,0:T(8,128)}), f32[16,40,128]{2,1,0:T(8,128)S(1)}, u32[]{:S(2)}, u32[]{:S(2)}) async-start(f32[16,40,128]{2,1,0:T(8,128)} %broadcast_in_dim.20), calls=%async_computation.4 | async-start | bytes 655360 | tf_op jit(solution)/shard_map/all_to_all | solution.py:178
  144.0 6.3 %collective-permute-start.11 = (f32[112,512]{1,0:T(8,128)S(1)}, f32[112,512]{1,0:T(8,128)S(1)}, u32[]{:S(2)}, u32[]{:S(2)}) collective-permute-start(f32[112,512]{1,0:T(8,128)S(1)} %get-tuple-element.37), channel_id=1, source_target_pairs={{0,0},{1,8},{2,16},{3,24},{4,32},{5,40},{6,48},{7,56},{8,64},{9,72... | collective-permute-start | bytes 688136 | tf_op jit(solution)/shard_map/ppermute | solution.py:170
  150.3 9.8 %collective-permute-done.11 = f32[112,512]{1,0:T(8,128)S(1)} collective-permute-done((f32[112,512]{1,0:T(8,128)S(1)}, f32[112,512]{1,0:T(8,128)S(1)}, u32[]{:S(2)}, u32[]{:S(2)}) %collective-permute-start.11) | collective-permute-done | bytes 229408 | tf_op jit(solution)/shard_map/ppermute | solution.py:170
  160.1 12.7 %collective-permute-start.15 = (f32[112,512]{1,0:T(8,128)S(1)}, f32[112,512]{1,0:T(8,128)S(1)}, u32[]{:S(2)}, u32[]{:S(2)}) collective-permute-start(f32[112,512]{1,0:T(8,128)S(1)} %collective-permute-done.11), channel_id=1, source_target_pairs={{0,8},{1,9},{2,10},{3,11},{4,12},{5,13},{6,14},{7,15},{8,16},{9,17... | collective-permute-start | bytes 688136 | tf_op jit(solution)/shard_map/ppermute | solution.py:170
  172.7 2.4 collective-permute-start.13
  175.2 20.1 %shard_map.44 = f32[512,512]{1,0:T(8,128)S(1)} custom-call(s32[1]{0:T(128)} %bitcast.place, f32[5,128,128]{2,1,0:T(8,128)S(1)} %bitcast.32, f32[5,128,128]{2,1,0:T(8,128)S(1)} %collective-permute-done.12.came_ref), custom_call_target="tpu_custom_call" | custom-call | flops 20132659200 | bytes 2097152 | tf_op jit(solution)/shard_map/pallas_call | solution.py:156
  195.5 1.7 fusion
  198.0 21.3 %all_to_all.54.refs_0_ = bf16[8,112,128]{2,1,0:T(8,128)(2,1)S(1)} all-to-all(bf16[8,112,128]{2,1,0:T(8,128)(2,1)S(1)} %broadcast_in_dim.21), channel_id=1, replica_groups=mesh['z'=8,'y'=4,'x'=4,'core'=2] {'z'}, dimensions={0} | all-to-all | bytes 458752 | tf_op jit(solution)/shard_map/all_to_all | solution.py:178
  220.3 1.7 collective-permute-start.16
  222.0 3.8 %collective-permute-done.17.refs_3_ = bf16[8,112,128]{2,1,0:T(8,128)(2,1)S(1)} collective-permute-done((bf16[8,112,128]{2,1,0:T(8,128)(2,1)S(1)}, bf16[8,112,128]{2,1,0:T(8,128)(2,1)S(1)}, u32[]{:S(2)}, u32[]{:S(2)}) %collective-permute-start.17) | collective-permute-done | bytes 229408 | tf_op jit(solution)/shard_map/ppermute | solution.py:170
  225.9 2.7 collective-permute-start.19
  228.6 2.5 collective-permute-done.18
  231.1 2.9 copy-done.2
  234.0 4.6 %shard_map.45 = (f32[2,4,112,128]{3,2,1,0:T(8,128)S(1)}, bf16[8,4,112,128]{3,2,1,0:T(8,128)(2,1)S(1)}) custom-call(s32[2]{0:T(128)S(1)} %pad_add_fusion.place, bf16[4,2,112,3584]{3,2,1,0:T(8,128)(2,1)S(1)} %bitcast.29, bf16[8,112,128]{2,1,0:T(8,128)(2,1)S(1)} %all_to_all.54.refs_0_, bf16[8,112,128]{2,1,0:T(8,128)(2,1)S(1)} %collective-permute-done.16.refs_1_, ...), custom_call_target="tpu_custom_call" | custom-call | flops 822083584 | bytes 8388608 | tf_op jit(solution)/shard_map/pallas_call | solution.py:247
  239.6 4.4 %collective-permute-start.20 = (f32[4,112,128]{2,1,0:T(8,128)S(1)}, f32[4,112,128]{2,1,0:T(8,128)S(1)}, u32[]{:S(2)}, u32[]{:S(2)}) collective-permute-start(f32[4,112,128]{2,1,0:T(8,128)S(1)} %slice_bitcast_fusion.2), channel_id=1, source_target_pairs={{0,1},{1,0},{2,3},{3,2},{4,5},{5,4},{6,7},{7,6},{8,9},{9,8},{10,11... | collective-permute-start | bytes 688136 | tf_op jit(solution)/shard_map/ppermute | solution.py:170
  245.2 8.0 %shard_map.46 = (f32[4,112,384]{2,1,0:T(8,128)}, f32[4,112,384]{2,1,0:T(8,128)}, bf16[3584,512]{1,0:T(8,128)(2,1)}) custom-call(s32[1]{0:T(128)} %bitcast.place, bf16[896,3584]{1,0:T(8,128)(2,1)} %a_ref.3, bf16[3584,384]{1,0:T(8,128)(2,1)} %all-gather.5.cloned.1.call-done.b_ref, bf16[3584,128]{1,0:T(8,128)(2,1)} %bitcast.30), custom_call_target="tpu_custom_call" | custom-call | flops 2466250752 | bytes 12582912 | tf_op jit(solution)/shard_map/pallas_call | solution.py:318
  253.2 2.3 collective-permute-start.21
  255.5 2.0 collective-permute-done.21
  258.7 19.4 %all_to_all.55.parts_ref = f32[4,112,512]{2,1,0:T(8,128)S(1)} all-to-all(f32[4,112,512]{2,1,0:T(8,128)S(1)} %pad_maximum_fusion.1), channel_id=1, replica_groups=mesh['z'=8,'y'=4,'x'=4,'core'=2] {'x'}, dimensions={0} | all-to-all | bytes 1835008 | tf_op jit(solution)/shard_map/all_to_all | solution.py:178
  279.0 1.9 collective-permute-start.22
  282.1 13.6 %all_to_all.56 = f32[16,40,128]{2,1,0:T(8,128)S(1)} all-to-all(f32[16,40,128]{2,1,0:T(8,128)S(1)} %bitcast.36), channel_id=1, replica_groups=mesh['z'=8,'y'=4,'x'=4,'core'=2] {'y','x'}, dimensions={0} | all-to-all | bytes 655360 | tf_op jit(solution)/shard_map/all_to_all | solution.py:178
  295.8 10.8 %all_to_all.57 = f32[8,40,128]{2,1,0:T(8,128)S(1)} all-to-all(f32[8,40,128]{2,1,0:T(8,128)S(1)} %broadcast_in_dim.22), channel_id=1, replica_groups=mesh['z'=8,'y'=4,'x'=4,'core'=2] {'z'}, dimensions={0} | all-to-all | bytes 327680 | tf_op jit(solution)/shard_map/all_to_all | solution.py:178
  306.7 10.8 %all_to_all.58 = f32[16,40,128]{2,1,0:T(8,128)S(1)} all-to-all(f32[16,40,128]{2,1,0:T(8,128)S(1)} %broadcast_in_dim.23), channel_id=1, replica_groups=mesh['z'=8,'y'=4,'x'=4,'core'=2] {'y','x'}, dimensions={0} | all-to-all | bytes 655360 | tf_op jit(solution)/shard_map/all_to_all | solution.py:178
  317.4 3.9 %collective-permute-start.23 = (f32[5,128,128]{2,1,0:T(8,128)S(1)}, f32[5,128,128]{2,1,0:T(8,128)S(1)}, u32[]{:S(2)}, u32[]{:S(2)}) collective-permute-start(f32[5,128,128]{2,1,0:T(8,128)S(1)} %bitcast.33), channel_id=1, source_target_pairs={{0,1},{1,0},{2,3},{3,2},{4,5},{5,4},{6,7},{7,6},{8,9},{9,8},{10,11... | collective-permute-start | bytes 983048 | tf_op jit(solution)/shard_map/ppermute | solution.py:170
  322.6 20.0 %shard_map.48 = f32[512,512]{1,0:T(8,128)S(1)} custom-call(s32[1]{0:T(128)} %bitcast.place, f32[5,128,128]{2,1,0:T(8,128)S(1)} %bitcast.34, f32[5,128,128]{2,1,0:T(8,128)S(1)} %collective-permute-done.23.came_ref), custom_call_target="tpu_custom_call" | custom-call | flops 20132659200 | bytes 2097152 | tf_op jit(solution)/shard_map/pallas_call | solution.py:156
  342.6 1.9 convolution_multiply_fusion.1
  (80 shorter events, 17.4 us)
Async XLA Ops:
  7.2 1.2 copy-start
  7.2 75.3 %all-gather.3.cloned.1.call-start = ((), (), s32[]{:S(2)}) async-start(), calls=%async_computation.10 | async-start | bytes 3096576 | tf_op jit(solution)/shard_map/all_gather | solution.py:220
  8.4 13.4 %collective-permute-start = (bf16[112,512]{1,0:T(8,128)(2,1)S(1)}, bf16[112,512]{1,0:T(8,128)(2,1)S(1)}, u32[]{:S(2)}, u32[]{:S(2)}) collective-permute-start(bf16[112,512]{1,0:T(8,128)(2,1)S(1)} %constant_dynamic-slice_fusion.1), channel_id=1, source_target_pairs={{0,0},{1,8},{2,16},{3,24},{4,32},{5,40},{6,48},{7,56},{8,64},{9,72... | collective-permute-start | bytes 344072 | tf_op jit(solution)/shard_map/ppermute | solution.py:170
  21.9 8.0 %collective-permute-start.1 = (bf16[112,384]{1,0:T(8,128)(2,1)S(1)}, bf16[112,384]{1,0:T(8,128)(2,1)S(1)}, u32[]{:S(2)}, u32[]{:S(2)}) collective-permute-start(bf16[112,384]{1,0:T(8,128)(2,1)S(1)} %get-tuple-element.56), channel_id=1, source_target_pairs={{0,24},{1,25},{2,26},{3,27},{4,28},{5,29},{6,30},{7,31},{8,0},{9,1... | collective-permute-start | bytes 258056 | tf_op jit(solution)/shard_map/ppermute | solution.py:170
  26.2 5.3 %collective-permute-start.2 = (bf16[112,384]{1,0:T(8,128)(2,1)S(1)}, bf16[112,384]{1,0:T(8,128)(2,1)S(1)}, u32[]{:S(2)}, u32[]{:S(2)}) collective-permute-start(bf16[112,384]{1,0:T(8,128)(2,1)S(1)} %get-tuple-element.56), channel_id=1, source_target_pairs={{0,16},{1,17},{2,18},{3,19},{4,20},{5,21},{6,22},{7,23},{8,24},{9,... | collective-permute-start | bytes 258056 | tf_op jit(solution)/shard_map/ppermute | solution.py:170
  27.6 6.5 %collective-permute-start.3 = (bf16[112,384]{1,0:T(8,128)(2,1)S(1)}, bf16[112,384]{1,0:T(8,128)(2,1)S(1)}, u32[]{:S(2)}, u32[]{:S(2)}) collective-permute-start(bf16[112,384]{1,0:T(8,128)(2,1)S(1)} %get-tuple-element.56), channel_id=1, source_target_pairs={{0,8},{1,9},{2,10},{3,11},{4,12},{5,13},{6,14},{7,15},{8,16},{9,17... | collective-permute-start | bytes 258056 | tf_op jit(solution)/shard_map/ppermute | solution.py:170
  34.1 0.7 copy-start.4
  55.2 6.5 %collective-permute-start.5 = (bf16[8,112,128]{2,1,0:T(8,128)(2,1)S(1)}, bf16[8,112,128]{2,1,0:T(8,128)(2,1)S(1)}, u32[]{:S(2)}, u32[]{:S(2)}) collective-permute-start(bf16[8,112,128]{2,1,0:T(8,128)(2,1)S(1)} %all_to_all.50.refs_0_), channel_id=1, source_target_pairs={{0,8},{1,9},{2,10},{3,11},{4,12},{5,13},{6,14},{7,15},{8,16},{9,17... | collective-permute-start | bytes 688136 | tf_op jit(solution)/shard_map/ppermute | solution.py:170
  55.2 6.6 %collective-permute-start.4 = (bf16[8,112,128]{2,1,0:T(8,128)(2,1)S(1)}, bf16[8,112,128]{2,1,0:T(8,128)(2,1)S(1)}, u32[]{:S(2)}, u32[]{:S(2)}) collective-permute-start(bf16[8,112,128]{2,1,0:T(8,128)(2,1)S(1)} %all_to_all.50.refs_0_), channel_id=1, source_target_pairs={{0,24},{1,25},{2,26},{3,27},{4,28},{5,29},{6,30},{7,31},{8,0},{9,1... | collective-permute-start | bytes 688136 | tf_op jit(solution)/shard_map/ppermute | solution.py:170
  61.7 5.5 %collective-permute-start.6 = (bf16[4,112,128]{2,1,0:T(8,128)(2,1)S(1)}, bf16[4,112,128]{2,1,0:T(8,128)(2,1)S(1)}, u32[]{:S(2)}, u32[]{:S(2)}) collective-permute-start(bf16[4,112,128]{2,1,0:T(8,128)(2,1)S(1)} %slice.66), channel_id=1, source_target_pairs={{0,8},{1,9},{2,10},{3,11},{4,12},{5,13},{6,14},{7,15},{8,16},{9,17... | collective-permute-start | bytes 344072 | tf_op jit(solution)/shard_map/ppermute | solution.py:170
  61.8 5.4 %collective-permute-start.7 = (bf16[4,112,128]{2,1,0:T(8,128)(2,1)S(1)}, bf16[4,112,128]{2,1,0:T(8,128)(2,1)S(1)}, u32[]{:S(2)}, u32[]{:S(2)}) collective-permute-start(bf16[4,112,128]{2,1,0:T(8,128)(2,1)S(1)} %slice.67), channel_id=1, source_target_pairs={{0,24},{1,25},{2,26},{3,27},{4,28},{5,29},{6,30},{7,31},{8,0},{9,1... | collective-permute-start | bytes 344072 | tf_op jit(solution)/shard_map/ppermute | solution.py:170
  67.2 2.9 copy-start.1
  75.7 6.8 %collective-permute-start.8 = (f32[4,112,128]{2,1,0:T(8,128)S(1)}, f32[4,112,128]{2,1,0:T(8,128)S(1)}, u32[]{:S(2)}, u32[]{:S(2)}) collective-permute-start(f32[4,112,128]{2,1,0:T(8,128)S(1)} %slice_bitcast_fusion.3), channel_id=1, source_target_pairs={{0,1},{1,0},{2,3},{3,2},{4,5},{5,4},{6,7},{7,6},{8,9},{9,8},{10,11... | collective-permute-start | bytes 688136 | tf_op jit(solution)/shard_map/ppermute | solution.py:170
  88.9 4.0 %collective-permute-start.9 = (f32[4,112,384]{2,1,0:T(8,128)}, f32[4,112,384]{2,1,0:T(8,128)S(1)}, u32[]{:S(2)}, u32[]{:S(2)}) collective-permute-start(f32[4,112,384]{2,1,0:T(8,128)} %get-tuple-element.35), channel_id=1, source_target_pairs={{0,1},{1,0},{2,3},{3,2},{4,5},{5,4},{6,7},{7,6},{8,9},{9,8},{10,11... | collective-permute-start | bytes 2064392 | tf_op jit(solution)/shard_map/ppermute | solution.py:170
  111.1 3.2 collective-permute-start.10
  140.4 19.6 %all-to-all-start.4 = ((f32[16,40,128]{2,1,0:T(8,128)}), f32[16,40,128]{2,1,0:T(8,128)S(1)}, u32[]{:S(2)}, u32[]{:S(2)}) async-start(f32[16,40,128]{2,1,0:T(8,128)} %broadcast_in_dim.20), calls=%async_computation.4 | async-start | bytes 655360 | tf_op jit(solution)/shard_map/all_to_all | solution.py:178
  144.0 101.3 %all-gather.5.cloned.1.call-start = ((), (), s32[]{:S(2)}) async-start(), calls=%async_computation.11 | async-start | bytes 3096576 | tf_op jit(solution)/shard_map/all_gather | solution.py:220
  144.0 16.0 %collective-permute-start.11 = (f32[112,512]{1,0:T(8,128)S(1)}, f32[112,512]{1,0:T(8,128)S(1)}, u32[]{:S(2)}, u32[]{:S(2)}) collective-permute-start(f32[112,512]{1,0:T(8,128)S(1)} %get-tuple-element.37), channel_id=1, source_target_pairs={{0,0},{1,8},{2,16},{3,24},{4,32},{5,40},{6,48},{7,56},{8,64},{9,72... | collective-permute-start | bytes 688136 | tf_op jit(solution)/shard_map/ppermute | solution.py:170
  160.1 15.1 %collective-permute-start.12 = (f32[5,128,128]{2,1,0:T(8,128)S(1)}, f32[5,128,128]{2,1,0:T(8,128)S(1)}, u32[]{:S(2)}, u32[]{:S(2)}) collective-permute-start(f32[5,128,128]{2,1,0:T(8,128)S(1)} %bitcast.31), channel_id=1, source_target_pairs={{0,1},{1,0},{2,3},{3,2},{4,5},{5,4},{6,7},{7,6},{8,9},{9,8},{10,11... | collective-permute-start | bytes 983048 | tf_op jit(solution)/shard_map/ppermute | solution.py:170
  160.1 35.2 %collective-permute-start.15 = (f32[112,512]{1,0:T(8,128)S(1)}, f32[112,512]{1,0:T(8,128)S(1)}, u32[]{:S(2)}, u32[]{:S(2)}) collective-permute-start(f32[112,512]{1,0:T(8,128)S(1)} %collective-permute-done.11), channel_id=1, source_target_pairs={{0,8},{1,9},{2,10},{3,11},{4,12},{5,13},{6,14},{7,15},{8,16},{9,17... | collective-permute-start | bytes 688136 | tf_op jit(solution)/shard_map/ppermute | solution.py:170
  172.7 22.5 %collective-permute-start.14 = (f32[112,512]{1,0:T(8,128)S(1)}, f32[112,512]{1,0:T(8,128)S(1)}, u32[]{:S(2)}, u32[]{:S(2)}) collective-permute-start(f32[112,512]{1,0:T(8,128)S(1)} %collective-permute-done.11), channel_id=1, source_target_pairs={{0,16},{1,17},{2,18},{3,19},{4,20},{5,21},{6,22},{7,23},{8,24},{9,... | collective-permute-start | bytes 688136 | tf_op jit(solution)/shard_map/ppermute | solution.py:170
  172.7 22.5 %collective-permute-start.13 = (f32[112,512]{1,0:T(8,128)S(1)}, f32[112,512]{1,0:T(8,128)S(1)}, u32[]{:S(2)}, u32[]{:S(2)}) collective-permute-start(f32[112,512]{1,0:T(8,128)S(1)} %collective-permute-done.11), channel_id=1, source_target_pairs={{0,24},{1,25},{2,26},{3,27},{4,28},{5,29},{6,30},{7,31},{8,0},{9,1... | collective-permute-start | bytes 688136 | tf_op jit(solution)/shard_map/ppermute | solution.py:170
  219.3 6.5 %collective-permute-start.17 = (bf16[8,112,128]{2,1,0:T(8,128)(2,1)S(1)}, bf16[8,112,128]{2,1,0:T(8,128)(2,1)S(1)}, u32[]{:S(2)}, u32[]{:S(2)}) collective-permute-start(bf16[8,112,128]{2,1,0:T(8,128)(2,1)S(1)} %all_to_all.54.refs_0_), channel_id=1, source_target_pairs={{0,8},{1,9},{2,10},{3,11},{4,12},{5,13},{6,14},{7,15},{8,16},{9,17... | collective-permute-start | bytes 688136 | tf_op jit(solution)/shard_map/ppermute | solution.py:170
  220.3 5.6 %collective-permute-start.16 = (bf16[8,112,128]{2,1,0:T(8,128)(2,1)S(1)}, bf16[8,112,128]{2,1,0:T(8,128)(2,1)S(1)}, u32[]{:S(2)}, u32[]{:S(2)}) collective-permute-start(bf16[8,112,128]{2,1,0:T(8,128)(2,1)S(1)} %all_to_all.54.refs_0_), channel_id=1, source_target_pairs={{0,24},{1,25},{2,26},{3,27},{4,28},{5,29},{6,30},{7,31},{8,0},{9,1... | collective-permute-start | bytes 688136 | tf_op jit(solution)/shard_map/ppermute | solution.py:170
  225.8 5.3 %collective-permute-start.18 = (bf16[4,112,128]{2,1,0:T(8,128)(2,1)S(1)}, bf16[4,112,128]{2,1,0:T(8,128)(2,1)S(1)}, u32[]{:S(2)}, u32[]{:S(2)}) collective-permute-start(bf16[4,112,128]{2,1,0:T(8,128)(2,1)S(1)} %slice.69), channel_id=1, source_target_pairs={{0,8},{1,9},{2,10},{3,11},{4,12},{5,13},{6,14},{7,15},{8,16},{9,17... | collective-permute-start | bytes 344072 | tf_op jit(solution)/shard_map/ppermute | solution.py:170
  225.9 5.2 %collective-permute-start.19 = (bf16[4,112,128]{2,1,0:T(8,128)(2,1)S(1)}, bf16[4,112,128]{2,1,0:T(8,128)(2,1)S(1)}, u32[]{:S(2)}, u32[]{:S(2)}) collective-permute-start(bf16[4,112,128]{2,1,0:T(8,128)(2,1)S(1)} %slice.70), channel_id=1, source_target_pairs={{0,24},{1,25},{2,26},{3,27},{4,28},{5,29},{6,30},{7,31},{8,0},{9,1... | collective-permute-start | bytes 344072 | tf_op jit(solution)/shard_map/ppermute | solution.py:170
  231.1 2.9 copy-start.2
  238.6 0.9 copy-start.3
  239.6 5.5 %collective-permute-start.20 = (f32[4,112,128]{2,1,0:T(8,128)S(1)}, f32[4,112,128]{2,1,0:T(8,128)S(1)}, u32[]{:S(2)}, u32[]{:S(2)}) collective-permute-start(f32[4,112,128]{2,1,0:T(8,128)S(1)} %slice_bitcast_fusion.2), channel_id=1, source_target_pairs={{0,1},{1,0},{2,3},{3,2},{4,5},{5,4},{6,7},{7,6},{8,9},{9,8},{10,11... | collective-permute-start | bytes 688136 | tf_op jit(solution)/shard_map/ppermute | solution.py:170
  253.2 4.2 %collective-permute-start.21 = (f32[4,112,384]{2,1,0:T(8,128)}, f32[4,112,384]{2,1,0:T(8,128)S(1)}, u32[]{:S(2)}, u32[]{:S(2)}) collective-permute-start(f32[4,112,384]{2,1,0:T(8,128)} %get-tuple-element.52), channel_id=1, source_target_pairs={{0,1},{1,0},{2,3},{3,2},{4,5},{5,4},{6,7},{7,6},{8,9},{9,8},{10,11... | collective-permute-start | bytes 2064392 | tf_op jit(solution)/shard_map/ppermute | solution.py:170
  279.0 3.2 collective-permute-start.22
  317.4 5.2 %collective-permute-start.23 = (f32[5,128,128]{2,1,0:T(8,128)S(1)}, f32[5,128,128]{2,1,0:T(8,128)S(1)}, u32[]{:S(2)}, u32[]{:S(2)}) collective-permute-start(f32[5,128,128]{2,1,0:T(8,128)S(1)} %bitcast.33), channel_id=1, source_target_pairs={{0,1},{1,0},{2,3},{3,2},{4,5},{5,4},{6,7},{7,6},{8,9},{9,8},{10,11... | collective-permute-start | bytes 983048 | tf_op jit(solution)/shard_map/ppermute | solution.py:170
Sparse Core Ops, SparseCore 0:
  35.0 46.8 all-gather.2
  198.1 47.1 all-gather.4
